TPU v7x, 32 devices: a whole 2x2x4 slice. The times are simulated.
32 devices in a mesh: replica: 16 (over z, x, core), shard: 2 (over y).
Axes of the slice: x: 2, y: 2, z: 4, core: 2. Of those that a mesh axis runs over, the one named last changes fastest.
Arguments:
- normed: bfloat16 [8192, 8192], P(('replica', 'shard')), may hold values from -96 to 96
- out_grads: bfloat16 [8192, 1024], P(('replica', 'shard')), may hold values from -4 to 4
- weight: float32 [8192, 1024], P(('replica', 'shard')), may hold values from -6 to 6
- moment: float32 [8192, 1024], P(('replica', 'shard')), may hold values from -6 to 6
- variance: float32 [8192, 1024], P(('replica', 'shard')), may hold values from 0.5 to 8
Outputs:
- new_weight: float32 [8192, 1024], P(('replica', 'shard'))
- new_moment: float32 [8192, 1024], P(('replica', 'shard'))
- new_variance: float32 [8192, 1024], P(('replica', 'shard'))
All inputs are finite; a program needn't handle non-finite values.
Results may differ from a plain program's by a relative error of at most 0.002.
Values may be sent and summed in bfloat16 or wider, within the bound.
No kernel may reach another device: no remote copies, remote signals or barrier semaphores. Data moves between devices by JAX's collectives and lax.ppermute only.
A program may use at most 128 MiB of HBM per device.

v0:
```python
import jax
import jax.numpy as jnp
from jax import lax
from jax.sharding import PartitionSpec as P

TOK_DEV = 256
STEP = 10


def to_wire(values):
    return lax.optimization_barrier(values.astype(jnp.bfloat16)).astype(jnp.float32)


def shards(normed, out_grads, weight, moment, variance):
    tokens = normed.shape[0]
    width = normed.shape[1]
    columns = out_grads.shape[1]
    n_replica = lax.axis_size("replica")
    n_shard = lax.axis_size("shard")
    own_rows = width // (n_replica * n_shard)
    group_rows = width // n_shard
    grid = normed.reshape(tokens, n_replica, n_shard, own_rows)
    mine = lax.all_to_all(grid, "shard", split_axis=2, concat_axis=0, tiled=True)
    mine = mine.reshape(n_shard * tokens, group_rows)
    piece = lax.all_gather(out_grads, "shard", axis=0, tiled=True)
    count = piece.shape[0] // TOK_DEV
    picked = mine.reshape(count, TOK_DEV, group_rows)
    parts = jnp.einsum(
        "ktd,ktc->kdc",
        picked,
        piece.reshape(count, TOK_DEV, columns),
        preferred_element_type=jnp.float32,
    )
    summed = jnp.sum(to_wire(parts), axis=0)
    grad = lax.psum_scatter(summed, "replica", scatter_dimension=0, tiled=True)
    squares = lax.psum(jnp.sum(grad * grad), ("replica", "shard"))
    limit = jnp.sqrt(jnp.float32(width * columns))
    clip = jnp.minimum(jnp.float32(1.0), limit / (jnp.sqrt(squares) + 1e-06))
    scaled = clip * grad
    new_moment = 0.9 * moment + 0.1 * scaled
    new_variance = 0.95 * variance + 0.05 * scaled * scaled
    first = new_moment / (1.0 - 0.9**STEP)
    second = new_variance / (1.0 - 0.95**STEP)
    new_weight = weight - 0.01 * (first / (jnp.sqrt(second) + 1e-08) + 0.1 * weight)
    return (new_weight, new_moment, new_variance)


def solution(mesh):
    in_specs = (
        P(("replica", "shard"), None),
        P(("replica", "shard"), None),
        P(("replica", "shard"), None),
        P(("replica", "shard"), None),
        P(("replica", "shard"), None),
    )
    out_specs = (
        P(("replica", "shard"), None),
        P(("replica", "shard"), None),
        P(("replica", "shard"), None),
    )
    return jax.shard_map(shards, mesh=mesh, in_specs=in_specs, out_specs=out_specs, check_vma=False)
```

profile of v0, /device:TPU:0, one launch (start us, length us, event | category | flops | bytes accessed | tf_op | source)
XLA Modules:
  0.0 352.6 jit_solution(16514070420911589325)
XLA Ops:
  7.2 7.8 %reshape.13 = bf16[256,16,2,256]{3,2,1,0:T(2,128)(2,1)} reshape(bf16[256,8192]{1,0:T(8,128)(2,1)} %param.5) | data formatting | bytes 8388608 | tf_op jit(solution)/shard_map/reshape | solution.py:22
  15.0 11.1 %copy.8 = bf16[256,16,2,256]{0,3,1,2:T(8,128)(2,1)} copy(bf16[256,16,2,256]{3,2,1,0:T(2,128)(2,1)} %reshape.13) | data formatting | bytes 8388608 | tf_op jit(solution)/shard_map/reshape | solution.py:22
  26.0 5.6 %all-to-all-start = ((bf16[256,16,2,256]{0,3,1,2:T(8,128)(2,1)}), bf16[256,16,2,256]{0,3,1,2:T(8,128)(2,1)}, u32[]{:S(2)}, u32[]{:S(2)}) async-start(bf16[256,16,2,256]{0,3,1,2:T(8,128)(2,1)} %copy.8), calls=%async_computation | async-start | bytes 8388608 | tf_op jit(solution)/shard_map/all_to_all | solution.py:23
  31.7 0.0 all-gather.2.cloned.1.call-start
  31.7 0.7 all-gather.2.cloned.1.call-update
  32.4 0.0 reduce-scatter.2.cloned.1.call-start
  32.4 37.5 %all-gather.2.cloned.1.call-done = bf16[512,1024]{1,0:T(8,128)(2,1)} async-done(((bf16[256,1024]{1,0:T(8,128)(2,1)}), bf16[512,1024]{1,0:T(8,128)(2,1)}) %all-gather.2.cloned.1.call-update) | async-done | bytes 1048592 | tf_op jit(solution)/shard_map/all_gather | solution.py:25
  69.9 21.8 %all-to-all-done = bf16[256,16,2,256]{0,3,1,2:T(8,128)(2,1)} async-done(((bf16[256,16,2,256]{0,3,1,2:T(8,128)(2,1)}), bf16[256,16,2,256]{0,3,1,2:T(8,128)(2,1)}, u32[]{:S(2)}, u32[]{:S(2)}) %all-to-all-start) | async-done | bytes 4194336 | tf_op jit(solution)/shard_map/all_to_all | solution.py:23
  91.7 12.7 %convolution_convert_fusion = bf16[2,4096,1024]{2,1,0:T(8,128)(2,1)} fusion(bf16[2,256,4096]{1,2,0:T(8,128)(2,1)} %bitcast.2, bf16[2,256,1024]{2,1,0:T(8,128)(2,1)} %bitcast.8), kind=kOutput, calls=%fused_computation.1 | convolution fusion | flops 4303355904 | bytes 22020096 | tf_op jit(solution)/shard_map/ktd,ktc->kdc/dot_general | solution.py:28
  104.5 16.4 %convert_reduce_fusion = f32[4096,1024]{1,0:T(8,128)} fusion(bf16[2,4096,1024]{2,1,0:T(8,128)(2,1)} %convolution_convert_fusion), kind=kLoop, calls=%fused_computation | loop fusion | flops 12582912 | bytes 33554432 | tf_op jit(solution)/shard_map/reduce_sum | solution.py:34
  120.8 0.0 copy-start
  120.8 0.0 copy-start.1
  120.8 0.0 copy-start.2
  120.8 0.0 reduce-scatter.2.cloned.1.call-update
  120.9 179.2 %reduce-scatter.2.cloned.1.call-done = f32[256,1024]{1,0:T(8,128)} async-done(((f32[4096,1024]{1,0:T(8,128)}), f32[256,1024]{1,0:T(8,128)}) %reduce-scatter.2.cloned.1.call-update) | async-done | bytes 1048592 | tf_op jit(solution)/shard_map/reduce_scatter | solution.py:35
  300.1 2.1 multiply_reduce_fusion
  302.2 39.3 %psum.7 = f32[]{:T(128)} all-reduce(f32[]{:T(128)} %multiply_reduce_fusion), channel_id=1, replica_groups=mesh['replica'=16,'shard'=2] {'replica','shard'}, use_global_device_ids=true, to_apply=%region_3.0 | all-reduce | flops 1 | bytes 8 | tf_op jit(solution)/shard_map/psum | solution.py:36
  342.3 0.0 copy-done
  342.3 0.0 copy-done.1
  342.3 0.0 copy-done.2
  342.3 3.5 multiply_subtract_fusion
Async XLA Ops:
  26.0 65.7 %all-to-all-start = ((bf16[256,16,2,256]{0,3,1,2:T(8,128)(2,1)}), bf16[256,16,2,256]{0,3,1,2:T(8,128)(2,1)}, u32[]{:S(2)}, u32[]{:S(2)}) async-start(bf16[256,16,2,256]{0,3,1,2:T(8,128)(2,1)} %copy.8), calls=%async_computation | async-start | bytes 8388608 | tf_op jit(solution)/shard_map/all_to_all | solution.py:23
  31.7 38.2 %all-gather.2.cloned.1.call-start = ((), (), s32[]{:S(2)}) async-start(), calls=%async_computation.2 | async-start | bytes 1572864 | tf_op jit(solution)/shard_map/all_gather | solution.py:25
  32.4 267.7 %reduce-scatter.2.cloned.1.call-start = ((), (), s32[]{:S(2)}) async-start(), calls=%async_computation.3 | async-start | bytes 17825792 | tf_op jit(solution)/shard_map/reduce_scatter | solution.py:35
  120.8 221.4 %copy-start = (f32[256,1024]{1,0:T(8,128)S(1)}, f32[256,1024]{1,0:T(8,128)}, u32[]{:S(2)}) copy-start(f32[256,1024]{1,0:T(8,128)} %param.7) | copy-start | bytes 3145732
  120.8 221.4 %copy-start.1 = (f32[256,1024]{1,0:T(8,128)S(1)}, f32[256,1024]{1,0:T(8,128)}, u32[]{:S(2)}) copy-start(f32[256,1024]{1,0:T(8,128)} %param.8) | copy-start | bytes 3145732
  120.8 221.4 %copy-start.2 = (f32[256,1024]{1,0:T(8,128)S(1)}, f32[256,1024]{1,0:T(8,128)}, u32[]{:S(2)}) copy-start(f32[256,1024]{1,0:T(8,128)} %param.9) | copy-start | bytes 3145732
Sparse Core Ops, SparseCore 0:
  34.0 35.8 all-gather.1
  121.0 179.0 reduce-scatter.1
where the time goes:
time: 353 us
  waiting for transfers between devices  239 us (68%)
  blocking collectives  39.3 us (11%)
  other arithmetic  21.9 us (6%)
  local copies, waits for them, and re-layouts  18.9 us (5%)
  between operations  14.8 us (4%)
  matrix products  12.7 us (4%)
  starting transfers between devices  5.69 us (2%)
    reduce_scatter x1, waiting for transfers between devices, shards(): grad = lax.psum_scatter(summed, 'replica', scatter_dimension=0, tiled=True)  179 us
    psum x1, blocking collectives, shards(): squares = lax.psum(jnp.sum(grad * grad), ('replica', 'shard'))  39.3 us
    all_gather x1, waiting for transfers between devices, shards(): piece = lax.all_gather(out_grads, 'shard', axis=0, tiled=True)  37.5 us
    all_to_all x1, waiting for transfers between devices, shards(): lax.all_to_all(grid, 'shard', split_axis=2, concat_axis=0, tiled=True)  21.8 us
    reshape x2, local copies, waits for them, and re-layouts, shards(): grid = normed.reshape(tokens, n_replica, n_shard, own_rows)  18.9 us
    reduce_sum x1, other arithmetic, shards(): summed = jnp.sum(to_wire(parts), axis=0)  16.4 us
    dot_general x1, matrix products, shards(): jnp.einsum('ktd,ktc->kdc', picked, piece.reshape(count, TOK_DEV, columns)...  12.7 us
  transfers between devices with their start and end apart: 3, of which 3 were waited for; matrix products, arithmetic and copies ran while one was open for 0% of the time, Pallas kernels for 0%

commit v1 on v0

v1 whole, which is shorter than its diff:
```python
import functools
import jax
import jax.numpy as jnp
from jax import lax
from jax.experimental import pallas as pl
from jax.experimental.pallas import tpu as pltpu
from jax.sharding import PartitionSpec as P

STEP = 10
AXES = ("replica", "shard")
F32 = jnp.float32
BF16 = jnp.bfloat16
VMEM_LIMIT = 32 * 2**20


def flip(values, n_replica, n_shard, replica_bits, shard_bits):
    pairs = []
    for rep in range(n_replica):
        for sh in range(n_shard):
            there = (rep ^ replica_bits) * n_shard + (sh ^ shard_bits)
            pairs.append((rep * n_shard + sh, there))
    return lax.ppermute(values, AXES, pairs)


def pack_kernel(chunks, n_shard, own, where, normed, *refs):
    outs, (buf, turned, sems) = refs[: 2 + 4 * chunks], refs[2 + 4 * chunks :]
    mine, core, cross = outs[0], outs[1], outs[2:]
    rest, x, c, y = where[0], where[1], where[2], where[3]
    width = n_shard * own
    order = []
    for step in range(chunks):
        for dx, dc in ((1, 0), (1, 1)):
            order.append((step, dx, dc))
    for step in range(chunks):
        for dx, dc in ((0, 1), (0, 0)):
            order.append((step, dx, dc))
    copies = []
    for at, (step, dx, dc) in enumerate(order):
        k = chunks - 1 - step
        block = ((rest ^ k) * 2 + (x ^ dx)) * 2 + (c ^ dc)
        start = pl.multiple_of(block * width, width)
        copy = pltpu.make_async_copy(normed.at[:, pl.ds(start, width)], buf.at[at], sems.at[at])
        copy.start()
        copies.append(copy)
    for at, (step, dx, dc) in enumerate(order):
        copies[at].wait()
        turned[...] = buf[at].T
        for j in range(n_shard):
            rows = turned[pl.ds(pl.multiple_of((y ^ j) * own, own), own), :]
            if dx:
                base = 4 * step + 2 * dc
                if j == 0:
                    cross[base + 1][...] = rows
                else:
                    cross[base][pl.ds((j - 1) * own, own), :] = rows
            else:
                into = core if dc else mine
                into[pl.ds(step * width + j * own, own), :] = rows


def product_kernel(rounds, a0, a1, a2, a3, b0, b1, b2, b3, out):
    lhs = (a0, a1, a2, a3)
    rhs = (b0, b1, b2, b3)
    tile = 256
    for col in range(0, out.shape[1], tile):
        total = None
        for a, b in zip(lhs, rhs):
            part = jnp.dot(a[...], b[:, pl.ds(col, tile)], preferred_element_type=F32)
            part = part.astype(BF16).astype(F32)
            total = part if total is None else total + part
        out[:, pl.ds(col, tile)] = total.astype(out.dtype)


def product(lhs, rhs, dtype):
    rows, columns = lhs[0].shape[0], rhs[0].shape[1]
    depth = rhs[0].shape[0]
    return pl.pallas_call(
        functools.partial(product_kernel, 4),
        out_shape=jax.ShapeDtypeStruct((rows, columns), dtype),
        in_specs=[pl.BlockSpec(memory_space=pltpu.VMEM)] * 8,
        out_specs=pl.BlockSpec(memory_space=pltpu.VMEM),
        compiler_params=pltpu.CompilerParams(vmem_limit_bytes=VMEM_LIMIT),
        cost_estimate=pl.CostEstimate(
            flops=8 * rows * columns * depth,
            bytes_accessed=4 * (rows + columns) * depth * 2 + rows * columns * 4,
            transcendentals=0,
        ),
    )(*lhs, *rhs)


def shards(normed, out_grads, weight, moment, variance):
    depth, width = normed.shape
    columns = out_grads.shape[1]
    n_replica = lax.axis_size("replica")
    n_shard = lax.axis_size("shard")
    chunks = n_replica // 4
    own = width // (n_replica * n_shard)
    group = n_shard * own
    rep = lax.axis_index("replica")
    where = jnp.stack([rep // 4, (rep // 2) % 2, rep % 2, lax.axis_index("shard")]).astype(jnp.int32)
    move = lambda values, rb, sb: flip(values, n_replica, n_shard, rb, sb)

    b_own = out_grads
    b_x = move(b_own, 2, 0)
    b_core = move(b_own, 1, 0)

    shapes = [jax.ShapeDtypeStruct((chunks * group, depth), BF16)] * 2
    for _ in range(chunks):
        for _ in range(2):
            shapes.append(jax.ShapeDtypeStruct((group - own, depth), BF16))
            shapes.append(jax.ShapeDtypeStruct((own, depth), BF16))
    packed = pl.pallas_call(
        functools.partial(pack_kernel, chunks, n_shard, own),
        out_shape=shapes,
        in_specs=[pl.BlockSpec(memory_space=pltpu.SMEM), pl.BlockSpec(memory_space=pl.ANY)],
        out_specs=[pl.BlockSpec(memory_space=pltpu.VMEM)] * len(shapes),
        scratch_shapes=[
            pltpu.VMEM((4 * chunks, depth, group), BF16),
            pltpu.VMEM((group, depth), BF16),
            pltpu.SemaphoreType.DMA((4 * chunks,)),
        ],
        compiler_params=pltpu.CompilerParams(vmem_limit_bytes=VMEM_LIMIT),
        cost_estimate=pl.CostEstimate(flops=0, bytes_accessed=4 * width * depth, transcendentals=0),
    )(where, normed)
    a_own, cross = packed[0], packed[2:]

    b_xc = None
    a_core = move(packed[1], 1, 0)
    far, near = [None] * chunks, [None] * chunks
    order = [("far", 0)]
    for step in range(1, chunks):
        order += [("far", step), ("near", step - 1)]
    order.append(("near", chunks - 1))
    for kind, step in order:
        base = 4 * step + (0 if kind == "far" else 1)
        got = (move(cross[base], 2, 0), move(cross[base + 2], 3, 0))
        (far if kind == "far" else near)[step] = got
    b_xc = move(b_x, 1, 0)
    rhs = (b_own, b_core, b_x, b_xc)

    def rows_of(values, step, first, count):
        start = step * group + first
        return lax.slice_in_dim(values, start, start + count, axis=0)

    sums = [None] * chunks
    arriving = [[] for _ in range(chunks)]
    for step in range(chunks):
        k = chunks - 1 - step
        lhs = [rows_of(a_own, step, own, group - own), rows_of(a_core, step, own, group - own), *far[step]]
        outward = product(lhs, rhs, BF16)
        lhs = [rows_of(a_own, step, 0, own), rows_of(a_core, step, 0, own), *near[step]]
        total = product(lhs, rhs, F32)
        for j in range(1, n_shard):
            piece = lax.slice_in_dim(outward, (j - 1) * own, j * own, axis=0)
            total = total + move(piece, 0, j).astype(F32)
        for piece in arriving[k]:
            total = total + piece.astype(F32)
        if k > 0:
            low = k & -k
            arriving[k ^ low].append(move(total.astype(BF16), 4 * low, 0))
        sums[k] = total
    grad = sums[0]

    squares = jnp.sum(grad * grad).reshape(1, 1)
    squares = jnp.broadcast_to(squares, (1, 128))
    squares = squares + move(squares, 1, 0)
    bits = [("s", 1 << i) for i in range(n_shard.bit_length() - 1)]
    bits += [("r", 1 << i) for i in range(1, n_replica.bit_length() - 1)]
    while bits:
        stage, bits = bits[:2], bits[2:]
        combos = [[stage[0]]] if len(stage) == 1 else [[stage[0]], [stage[1]], stage]
        parts = []
        for combo in combos:
            rb = sum(b for kind, b in combo if kind == "r")
            sb = sum(b for kind, b in combo if kind == "s")
            parts.append(move(squares, rb, sb))
        for part in parts:
            squares = squares + part
    squares = squares[0, 0]

    limit = jnp.sqrt(jnp.float32(width * columns))
    clip = jnp.minimum(jnp.float32(1.0), limit / (jnp.sqrt(squares) + 1e-06))
    scaled = clip * grad
    new_moment = 0.9 * moment + 0.1 * scaled
    new_variance = 0.95 * variance + 0.05 * scaled * scaled
    first = new_moment / (1.0 - 0.9**STEP)
    second = new_variance / (1.0 - 0.95**STEP)
    new_weight = weight - 0.01 * (first / (jnp.sqrt(second) + 1e-08) + 0.1 * weight)
    return (new_weight, new_moment, new_variance)


def solution(mesh):
    spec = P(("replica", "shard"), None)
    return jax.shard_map(shards, mesh=mesh, in_specs=(spec,) * 5, out_specs=(spec,) * 3, check_vma=False)
```

time: 353 us -> 125 us (0.35)
  waiting for transfers between devices: 239 us -> 63.7 us
  blocking collectives: 39.3 us -> 0 us
  starting transfers between devices: 5.69 us -> 43.2 us
  other arithmetic: 21.9 us -> 5.13 us
  local copies, waits for them, and re-layouts: 18.9 us -> 3.03 us
  between operations: 14.8 us -> 1.05 us
  matrix products: 12.7 us -> 0 us
  Pallas kernels: 0 us -> 9.13 us
    reduce_scatter x1 -> x0, waiting for transfers between devices: 179 us -> none  [shards(): grad = lax.psum_scatter(summed, 'replica', scatter_dimension=0, tiled=True)]
    ppermute x0 -> x34, waiting for transfers between devices: none -> 63.7 us  [flip(): return lax.ppermute(values, AXES, pairs)]
    ppermute x0 -> x34, starting transfers between devices: none -> 43.2 us  [flip(): return lax.ppermute(values, AXES, pairs)]
    psum x1 -> x0, blocking collectives: 39.3 us -> none  [shards(): squares = lax.psum(jnp.sum(grad * grad), ('replica', 'shard'))]
    all_gather x1 -> x0, waiting for transfers between devices: 37.5 us -> none  [shards(): piece = lax.all_gather(out_grads, 'shard', axis=0, tiled=True)]
    all_to_all x1 -> x0, waiting for transfers between devices: 21.8 us -> none  [shards(): lax.all_to_all(grid, 'shard', split_axis=2, concat_axis=0, tiled=True)]
    reshape x2 -> x0, local copies, waits for them, and re-layouts: 18.9 us -> none  [shards(): grid = normed.reshape(tokens, n_replica, n_shard, own_rows)]
    reduce_sum x2 -> x1, other arithmetic: 18.5 us -> 0.94 us  [shards(): squares = jnp.sum(grad * grad).reshape(1, 1)]
  transfers between devices with their start and end apart: 3 -> 34, of which waited for: 3 -> 22; matrix products, arithmetic and copies ran while one was open for 0% -> 1% of each run, Pallas kernels for 0% -> 4%
where the time goes in v1:
time: 125 us
  waiting for transfers between devices  63.7 us (51%)
  starting transfers between devices  43.2 us (35%)
  Pallas kernels  9.13 us (7%)
  other arithmetic  5.13 us (4%)
  local copies, waits for them, and re-layouts  3.03 us (2%)
    ppermute x34, waiting for transfers between devices, flip(): return lax.ppermute(values, AXES, pairs)  63.7 us
    ppermute x34, starting transfers between devices, flip(): return lax.ppermute(values, AXES, pairs)  43.2 us
    pallas_call x8, Pallas kernels, product(): pl.pallas_call(functools.partial(product_kernel, 4), out_shape=jax.ShapeD...  5.85 us
    pallas_call x1, Pallas kernels, shards(): pl.pallas_call(functools.partial(pack_kernel, chunks, n_shard, own), out_...  3.29 us
  transfers between devices with their start and end apart: 34, of which 22 were waited for; matrix products, arithmetic and copies ran while one was open for 1% of the time, Pallas kernels for 4%

profile of v1, /device:TPU:0, one launch (start us, length us, event | category | flops | bytes accessed | tf_op | source)
XLA Modules:
  0.0 125.2 jit_solution(3555071808060694942)
XLA Ops:
  0.8 2.2 %copy-done.1 = bf16[256,8192]{1,0:T(8,128)(2,1)S(1)} copy-done((bf16[256,8192]{1,0:T(8,128)(2,1)S(1)}, bf16[256,8192]{1,0:T(8,128)(2,1)}, u32[]{:S(2)}) %copy-start.1) | copy-done | bytes 4194328
  3.0 3.3 %shard_map.76 = (bf16[2048,256]{1,0:T(8,128)(2,1)S(1)}, bf16[2048,256]{1,0:T(8,128)(2,1)S(1)}, bf16[256,256]{1,0:T(8,128)(2,1)S(1)}, bf16[256,256]{1,0:T(8,128)(...) custom-call(s32[4]{0:T(128)S(1)} %pad_add_fusion.where, ...), custom_call_target="tpu_custom_call" | custom-call | bytes 8388608 | tf_op jit(solution)/shard_map/pallas_call | solution.py:112
  6.8 2.6 %collective-permute-start.4 = (bf16[256,1024]{1,0:T(8,128)(2,1)S(1)}, bf16[256,1024]{1,0:T(8,128)(2,1)S(1)}, u32[]{:S(2)}, u32[]{:S(2)}) collective-permute-start(bf16[256,1024]{1,0:T(8,128)(2,1)S(1)} %copy-done), channel_id=1, source_target_pairs={{0,4},{1,5},{2,6},{3,7},{4,0},{5,1},{6,2},{7,3},{8,12},{9,13},{10,... | collective-permute-start | bytes 1572872 | tf_op jit(solution)/shard_map/ppermute | solution.py:22
  9.5 12.4 %collective-permute-done.4.b2 = bf16[256,1024]{1,0:T(8,128)(2,1)S(1)} collective-permute-done((bf16[256,1024]{1,0:T(8,128)(2,1)S(1)}, bf16[256,1024]{1,0:T(8,128)(2,1)S(1)}, u32[]{:S(2)}, u32[]{:S(2)}) %collective-permute-start.4) | collective-permute-done | bytes 524320 | tf_op jit(solution)/shard_map/ppermute | solution.py:22
  21.9 1.8 %collective-permute-start.16 = (bf16[256,256]{1,0:T(8,128)(2,1)S(1)}, bf16[256,256]{1,0:T(8,128)(2,1)S(1)}, u32[]{:S(2)}, u32[]{:S(2)}) collective-permute-start(bf16[256,256]{1,0:T(8,128)(2,1)S(1)} %get-tuple-element.33), channel_id=1, source_target_pairs={{0,4},{1,5},{2,6},{3,7},{4,0},{5,1},{6,2},{7,3},{8,12},{9,13},{10,... | collective-permute-start | bytes 393224 | tf_op jit(solution)/shard_map/ppermute | solution.py:22
  23.9 4.2 %collective-permute-done.16.a2 = bf16[256,256]{1,0:T(8,128)(2,1)S(1)} collective-permute-done((bf16[256,256]{1,0:T(8,128)(2,1)S(1)}, bf16[256,256]{1,0:T(8,128)(2,1)S(1)}, u32[]{:S(2)}, u32[]{:S(2)}) %collective-permute-start.16) | collective-permute-done | bytes 131104 | tf_op jit(solution)/shard_map/ppermute | solution.py:22
  28.2 2.1 %collective-permute-done.17.a3 = bf16[256,256]{1,0:T(8,128)(2,1)S(1)} collective-permute-done((bf16[256,256]{1,0:T(8,128)(2,1)S(1)}, bf16[256,256]{1,0:T(8,128)(2,1)S(1)}, u32[]{:S(2)}, u32[]{:S(2)}) %collective-permute-start.17) | collective-permute-done | bytes 131104 | tf_op jit(solution)/shard_map/ppermute | solution.py:22
  31.0 1.8 %collective-permute-start.18 = (bf16[256,1024]{1,0:T(8,128)(2,1)S(1)}, bf16[256,1024]{1,0:T(8,128)(2,1)S(1)}, u32[]{:S(2)}, u32[]{:S(2)}) collective-permute-start(bf16[256,1024]{1,0:T(8,128)(2,1)S(1)} %shard_map.82), channel_id=1, source_target_pairs={{0,1},{1,0},{2,3},{3,2},{4,5},{5,4},{6,7},{7,6},{8,9},{9,8},{10,11... | collective-permute-start | bytes 1572872 | tf_op jit(solution)/shard_map/ppermute | solution.py:22
  36.3 2.7 %collective-permute-done.23.a2 = bf16[256,256]{1,0:T(8,128)(2,1)S(1)} collective-permute-done((bf16[256,256]{1,0:T(8,128)(2,1)S(1)}, bf16[256,256]{1,0:T(8,128)(2,1)S(1)}, u32[]{:S(2)}, u32[]{:S(2)}) %collective-permute-start.23) | collective-permute-done | bytes 131104 | tf_op jit(solution)/shard_map/ppermute | solution.py:22
  41.0 2.2 %collective-permute-start.15 = (bf16[256,256]{1,0:T(8,128)(2,1)S(1)}, bf16[256,256]{1,0:T(8,128)(2,1)S(1)}, u32[]{:S(2)}, u32[]{:S(2)}) collective-permute-start(bf16[256,256]{1,0:T(8,128)(2,1)S(1)} %get-tuple-element.32), channel_id=1, source_target_pairs={{0,6},{1,7},{2,4},{3,5},{4,2},{5,3},{6,0},{7,1},{8,14},{9,15},{10,... | collective-permute-start | bytes 393224 | tf_op jit(solution)/shard_map/ppermute | solution.py:22
  46.6 1.9 %collective-permute-start.7 = (bf16[256,256]{1,0:T(8,128)(2,1)S(1)}, bf16[256,256]{1,0:T(8,128)(2,1)S(1)}, u32[]{:S(2)}, u32[]{:S(2)}) collective-permute-start(bf16[256,256]{1,0:T(8,128)(2,1)S(1)} %get-tuple-element.26), channel_id=1, source_target_pairs={{0,6},{1,7},{2,4},{3,5},{4,2},{5,3},{6,0},{7,1},{8,14},{9,15},{10,... | collective-permute-start | bytes 393224 | tf_op jit(solution)/shard_map/ppermute | solution.py:22
  52.3 1.9 %collective-permute-start.22 = (bf16[256,256]{1,0:T(8,128)(2,1)S(1)}, bf16[256,256]{1,0:T(8,128)(2,1)S(1)}, u32[]{:S(2)}, u32[]{:S(2)}) collective-permute-start(bf16[256,256]{1,0:T(8,128)(2,1)S(1)} %get-tuple-element.36), channel_id=1, source_target_pairs={{0,6},{1,7},{2,4},{3,5},{4,2},{5,3},{6,0},{7,1},{8,14},{9,15},{10,... | collective-permute-start | bytes 393224 | tf_op jit(solution)/shard_map/ppermute | solution.py:22
  59.5 2.0 %collective-permute-done.21.a2 = bf16[256,256]{1,0:T(8,128)(2,1)S(1)} collective-permute-done((bf16[256,256]{1,0:T(8,128)(2,1)S(1)}, bf16[256,256]{1,0:T(8,128)(2,1)S(1)}, u32[]{:S(2)}, u32[]{:S(2)}) %collective-permute-start.21) | collective-permute-done | bytes 131104 | tf_op jit(solution)/shard_map/ppermute | solution.py:22
  63.2 2.0 %collective-permute-start.10 = (bf16[256,256]{1,0:T(8,128)(2,1)S(1)}, bf16[256,256]{1,0:T(8,128)(2,1)S(1)}, u32[]{:S(2)}, u32[]{:S(2)}) collective-permute-start(bf16[256,256]{1,0:T(8,128)(2,1)S(1)} %get-tuple-element.28), channel_id=1, source_target_pairs={{0,6},{1,7},{2,4},{3,5},{4,2},{5,3},{6,0},{7,1},{8,14},{9,15},{10,... | collective-permute-start | bytes 393224 | tf_op jit(solution)/shard_map/ppermute | solution.py:22
  70.0 1.7 %collective-permute-start.26 = (bf16[256,1024]{1,0:T(8,128)(2,1)S(1)}, bf16[256,1024]{1,0:T(8,128)(2,1)S(1)}, u32[]{:S(2)}, u32[]{:S(2)}) collective-permute-start(bf16[256,1024]{1,0:T(8,128)(2,1)S(1)} %add_convert_fusion), channel_id=1, source_target_pairs={{0,8},{1,9},{2,10},{3,11},{4,12},{5,13},{6,14},{7,15},{8,0},{9,1},... | collective-permute-start | bytes 1572872 | tf_op jit(solution)/shard_map/ppermute | solution.py:22
  71.7 9.4 %collective-permute-done.13 = bf16[256,1024]{1,0:T(8,128)(2,1)S(1)} collective-permute-done((bf16[256,1024]{1,0:T(8,128)(2,1)S(1)}, bf16[256,1024]{1,0:T(8,128)(2,1)S(1)}, u32[]{:S(2)}, u32[]{:S(2)}) %collective-permute-start.13) | collective-permute-done | bytes 524320 | tf_op jit(solution)/shard_map/ppermute | solution.py:22
  81.4 2.7 %collective-permute-start.20 = (bf16[256,1024]{1,0:T(8,128)(2,1)S(1)}, bf16[256,1024]{1,0:T(8,128)(2,1)S(1)}, u32[]{:S(2)}, u32[]{:S(2)}) collective-permute-start(bf16[256,1024]{1,0:T(8,128)(2,1)S(1)} %add_convert_fusion.1), channel_id=1, source_target_pairs={{0,16},{1,17},{2,18},{3,19},{4,20},{5,21},{6,22},{7,23},{8,24},{9,... | collective-permute-start | bytes 1572872 | tf_op jit(solution)/shard_map/ppermute | solution.py:22
  84.3 5.8 %collective-permute-done.1.a2 = bf16[256,256]{1,0:T(8,128)(2,1)S(1)} collective-permute-done((bf16[256,256]{1,0:T(8,128)(2,1)S(1)}, bf16[256,256]{1,0:T(8,128)(2,1)S(1)}, u32[]{:S(2)}, u32[]{:S(2)}) %collective-permute-start.1) | collective-permute-done | bytes 131104 | tf_op jit(solution)/shard_map/ppermute | solution.py:22
  90.9 12.1 %collective-permute-done.20 = bf16[256,1024]{1,0:T(8,128)(2,1)S(1)} collective-permute-done((bf16[256,1024]{1,0:T(8,128)(2,1)S(1)}, bf16[256,1024]{1,0:T(8,128)(2,1)S(1)}, u32[]{:S(2)}, u32[]{:S(2)}) %collective-permute-start.20) | collective-permute-done | bytes 524320 | tf_op jit(solution)/shard_map/ppermute | solution.py:22
  106.4 3.1 %collective-permute-start.29 = (f32[1,128]{1,0:T(1,128)S(1)}, f32[1,128]{1,0:T(1,128)S(1)}, u32[]{:S(2)}, u32[]{:S(2)}) collective-permute-start(f32[1,128]{1,0:T(1,128)S(1)} %broadcast_add_fusion), channel_id=1, source_target_pairs={{0,4},{1,5},{2,6},{3,7},{4,0},{5,1},{6,2},{7,3},{8,12},{9,13},{10,... | collective-permute-start | bytes 1544 | tf_op jit(solution)/shard_map/ppermute | solution.py:22
  111.1 2.9 %collective-permute-done.30 = f32[1,128]{1,0:T(1,128)S(1)} collective-permute-done((f32[1,128]{1,0:T(1,128)S(1)}, f32[1,128]{1,0:T(1,128)S(1)}, u32[]{:S(2)}, u32[]{:S(2)}) %collective-permute-start.30) | collective-permute-done | bytes 544 | tf_op jit(solution)/shard_map/ppermute | solution.py:22
  114.6 3.7 %collective-permute-start.33 = (f32[1,128]{1,0:T(1,128)S(1)}, f32[1,128]{1,0:T(1,128)S(1)}, u32[]{:S(2)}, u32[]{:S(2)}) collective-permute-start(f32[1,128]{1,0:T(1,128)S(1)} %add_add_fusion.1), channel_id=1, source_target_pairs={{0,24},{1,25},{2,26},{3,27},{4,28},{5,29},{6,30},{7,31},{8,16},{9,... | collective-permute-start | bytes 1544 | tf_op jit(solution)/shard_map/ppermute | solution.py:22
  120.0 2.7 %collective-permute-done.32 = f32[1,128]{1,0:T(1,128)S(1)} collective-permute-done((f32[1,128]{1,0:T(1,128)S(1)}, f32[1,128]{1,0:T(1,128)S(1)}, u32[]{:S(2)}, u32[]{:S(2)}) %collective-permute-start.32) | collective-permute-done | bytes 544 | tf_op jit(solution)/shard_map/ppermute | solution.py:22
  122.9 2.2 %multiply_subtract_fusion = (f32[256,1024]{1,0:T(8,128)}, f32[256,1024]{1,0:T(8,128)}, f32[256,1024]{1,0:T(8,128)}) fusion(f32[256,1024]{1,0:T(8,128)S(1)} %copy-done.2, f32[256,1024]{1,0:T(8,128)S(1)} %get-tuple-element.43, f32[]{:T(128)} %bitcast.4, f32[256,1024]{1,0:T(8,128)S(1)} %copy-done.3, f32[256,1024]{1,0:T(8,128)S(1)} %copy-done.4), kind=kLoop, calls=%fused_computation.2 | loop fusion | flops 4194304 | bytes 7340036 | tf_op jit(solution)/shard_map/sub | solution.py:188
  (75 shorter events, 34.8 us)
Async XLA Ops:
  6.3 17.6 %collective-permute-start = (bf16[2048,256]{1,0:T(8,128)(2,1)S(1)}, bf16[2048,256]{1,0:T(8,128)(2,1)S(1)}, u32[]{:S(2)}, u32[]{:S(2)}) collective-permute-start(bf16[2048,256]{1,0:T(8,128)(2,1)S(1)} %get-tuple-element.22), channel_id=1, source_target_pairs={{0,2},{1,3},{2,0},{3,1},{4,6},{5,7},{6,4},{7,5},{8,10},{9,11},{10,... | collective-permute-start | bytes 3145736 | tf_op jit(solution)/shard_map/ppermute | solution.py:22
  6.8 15.1 %collective-permute-start.4 = (bf16[256,1024]{1,0:T(8,128)(2,1)S(1)}, bf16[256,1024]{1,0:T(8,128)(2,1)S(1)}, u32[]{:S(2)}, u32[]{:S(2)}) collective-permute-start(bf16[256,1024]{1,0:T(8,128)(2,1)S(1)} %copy-done), channel_id=1, source_target_pairs={{0,4},{1,5},{2,6},{3,7},{4,0},{5,1},{6,2},{7,3},{8,12},{9,13},{10,... | collective-permute-start | bytes 1572872 | tf_op jit(solution)/shard_map/ppermute | solution.py:22
  9.4 20.9 %collective-permute-start.3 = (bf16[256,1024]{1,0:T(8,128)(2,1)S(1)}, bf16[256,1024]{1,0:T(8,128)(2,1)S(1)}, u32[]{:S(2)}, u32[]{:S(2)}) collective-permute-start(bf16[256,1024]{1,0:T(8,128)(2,1)S(1)} %copy-done), channel_id=1, source_target_pairs={{0,2},{1,3},{2,0},{3,1},{4,6},{5,7},{6,4},{7,5},{8,10},{9,11},{10,... | collective-permute-start | bytes 1572872 | tf_op jit(solution)/shard_map/ppermute | solution.py:22
  21.9 8.4 %collective-permute-start.5 = (bf16[256,1024]{1,0:T(8,128)(2,1)S(1)}, bf16[256,1024]{1,0:T(8,128)(2,1)S(1)}, u32[]{:S(2)}, u32[]{:S(2)}) collective-permute-start(bf16[256,1024]{1,0:T(8,128)(2,1)S(1)} %collective-permute-done.4.b2), channel_id=1, source_target_pairs={{0,2},{1,3},{2,0},{3,1},{4,6},{5,7},{6,4},{7,5},{8,10},{9,11},{10,... | collective-permute-start | bytes 1572872 | tf_op jit(solution)/shard_map/ppermute | solution.py:22
  21.9 6.3 %collective-permute-start.16 = (bf16[256,256]{1,0:T(8,128)(2,1)S(1)}, bf16[256,256]{1,0:T(8,128)(2,1)S(1)}, u32[]{:S(2)}, u32[]{:S(2)}) collective-permute-start(bf16[256,256]{1,0:T(8,128)(2,1)S(1)} %get-tuple-element.33), channel_id=1, source_target_pairs={{0,4},{1,5},{2,6},{3,7},{4,0},{5,1},{6,2},{7,3},{8,12},{9,13},{10,... | collective-permute-start | bytes 393224 | tf_op jit(solution)/shard_map/ppermute | solution.py:22
  23.6 6.6 %collective-permute-start.17 = (bf16[256,256]{1,0:T(8,128)(2,1)S(1)}, bf16[256,256]{1,0:T(8,128)(2,1)S(1)}, u32[]{:S(2)}, u32[]{:S(2)}) collective-permute-start(bf16[256,256]{1,0:T(8,128)(2,1)S(1)} %get-tuple-element.34), channel_id=1, source_target_pairs={{0,6},{1,7},{2,4},{3,5},{4,2},{5,3},{6,0},{7,1},{8,14},{9,15},{10,... | collective-permute-start | bytes 393224 | tf_op jit(solution)/shard_map/ppermute | solution.py:22
  31.0 23.9 %collective-permute-start.18 = (bf16[256,1024]{1,0:T(8,128)(2,1)S(1)}, bf16[256,1024]{1,0:T(8,128)(2,1)S(1)}, u32[]{:S(2)}, u32[]{:S(2)}) collective-permute-start(bf16[256,1024]{1,0:T(8,128)(2,1)S(1)} %shard_map.82), channel_id=1, source_target_pairs={{0,1},{1,0},{2,3},{3,2},{4,5},{5,4},{6,7},{7,6},{8,9},{9,8},{10,11... | collective-permute-start | bytes 1572872 | tf_op jit(solution)/shard_map/ppermute | solution.py:22
  32.8 6.2 %collective-permute-start.23 = (bf16[256,256]{1,0:T(8,128)(2,1)S(1)}, bf16[256,256]{1,0:T(8,128)(2,1)S(1)}, u32[]{:S(2)}, u32[]{:S(2)}) collective-permute-start(bf16[256,256]{1,0:T(8,128)(2,1)S(1)} %get-tuple-element.37), channel_id=1, source_target_pairs={{0,4},{1,5},{2,6},{3,7},{4,0},{5,1},{6,2},{7,3},{8,12},{9,13},{10,... | collective-permute-start | bytes 393224 | tf_op jit(solution)/shard_map/ppermute | solution.py:22
  34.3 6.7 %collective-permute-start.24 = (bf16[256,256]{1,0:T(8,128)(2,1)S(1)}, bf16[256,256]{1,0:T(8,128)(2,1)S(1)}, u32[]{:S(2)}, u32[]{:S(2)}) collective-permute-start(bf16[256,256]{1,0:T(8,128)(2,1)S(1)} %get-tuple-element.38), channel_id=1, source_target_pairs={{0,6},{1,7},{2,4},{3,5},{4,2},{5,3},{6,0},{7,1},{8,14},{9,15},{10,... | collective-permute-start | bytes 393224 | tf_op jit(solution)/shard_map/ppermute | solution.py:22
  34.3 10.3 %collective-permute-start.11 = (bf16[256,256]{1,0:T(8,128)(2,1)S(1)}, bf16[256,256]{1,0:T(8,128)(2,1)S(1)}, u32[]{:S(2)}, u32[]{:S(2)}) collective-permute-start(bf16[256,256]{1,0:T(8,128)(2,1)S(1)} %get-tuple-element.29), channel_id=1, source_target_pairs={{0,4},{1,5},{2,6},{3,7},{4,0},{5,1},{6,2},{7,3},{8,12},{9,13},{10,... | collective-permute-start | bytes 393224 | tf_op jit(solution)/shard_map/ppermute | solution.py:22
  35.6 11.0 %collective-permute-start.12 = (bf16[256,256]{1,0:T(8,128)(2,1)S(1)}, bf16[256,256]{1,0:T(8,128)(2,1)S(1)}, u32[]{:S(2)}, u32[]{:S(2)}) collective-permute-start(bf16[256,256]{1,0:T(8,128)(2,1)S(1)} %get-tuple-element.30), channel_id=1, source_target_pairs={{0,6},{1,7},{2,4},{3,5},{4,2},{5,3},{6,0},{7,1},{8,14},{9,15},{10,... | collective-permute-start | bytes 393224 | tf_op jit(solution)/shard_map/ppermute | solution.py:22
  39.0 11.2 %collective-permute-start.14 = (bf16[256,256]{1,0:T(8,128)(2,1)S(1)}, bf16[256,256]{1,0:T(8,128)(2,1)S(1)}, u32[]{:S(2)}, u32[]{:S(2)}) collective-permute-start(bf16[256,256]{1,0:T(8,128)(2,1)S(1)} %get-tuple-element.31), channel_id=1, source_target_pairs={{0,4},{1,5},{2,6},{3,7},{4,0},{5,1},{6,2},{7,3},{8,12},{9,13},{10,... | collective-permute-start | bytes 393224 | tf_op jit(solution)/shard_map/ppermute | solution.py:22
  41.0 11.2 %collective-permute-start.15 = (bf16[256,256]{1,0:T(8,128)(2,1)S(1)}, bf16[256,256]{1,0:T(8,128)(2,1)S(1)}, u32[]{:S(2)}, u32[]{:S(2)}) collective-permute-start(bf16[256,256]{1,0:T(8,128)(2,1)S(1)} %get-tuple-element.32), channel_id=1, source_target_pairs={{0,6},{1,7},{2,4},{3,5},{4,2},{5,3},{6,0},{7,1},{8,14},{9,15},{10,... | collective-permute-start | bytes 393224 | tf_op jit(solution)/shard_map/ppermute | solution.py:22
  44.6 11.2 %collective-permute-start.6 = (bf16[256,256]{1,0:T(8,128)(2,1)S(1)}, bf16[256,256]{1,0:T(8,128)(2,1)S(1)}, u32[]{:S(2)}, u32[]{:S(2)}) collective-permute-start(bf16[256,256]{1,0:T(8,128)(2,1)S(1)} %get-tuple-element.25), channel_id=1, source_target_pairs={{0,4},{1,5},{2,6},{3,7},{4,0},{5,1},{6,2},{7,3},{8,12},{9,13},{10,... | collective-permute-start | bytes 393224 | tf_op jit(solution)/shard_map/ppermute | solution.py:22
  46.6 11.2 %collective-permute-start.7 = (bf16[256,256]{1,0:T(8,128)(2,1)S(1)}, bf16[256,256]{1,0:T(8,128)(2,1)S(1)}, u32[]{:S(2)}, u32[]{:S(2)}) collective-permute-start(bf16[256,256]{1,0:T(8,128)(2,1)S(1)} %get-tuple-element.26), channel_id=1, source_target_pairs={{0,6},{1,7},{2,4},{3,5},{4,2},{5,3},{6,0},{7,1},{8,14},{9,15},{10,... | collective-permute-start | bytes 393224 | tf_op jit(solution)/shard_map/ppermute | solution.py:22
  50.3 11.2 %collective-permute-start.21 = (bf16[256,256]{1,0:T(8,128)(2,1)S(1)}, bf16[256,256]{1,0:T(8,128)(2,1)S(1)}, u32[]{:S(2)}, u32[]{:S(2)}) collective-permute-start(bf16[256,256]{1,0:T(8,128)(2,1)S(1)} %get-tuple-element.35), channel_id=1, source_target_pairs={{0,4},{1,5},{2,6},{3,7},{4,0},{5,1},{6,2},{7,3},{8,12},{9,13},{10,... | collective-permute-start | bytes 393224 | tf_op jit(solution)/shard_map/ppermute | solution.py:22
  52.3 10.9 %collective-permute-start.22 = (bf16[256,256]{1,0:T(8,128)(2,1)S(1)}, bf16[256,256]{1,0:T(8,128)(2,1)S(1)}, u32[]{:S(2)}, u32[]{:S(2)}) collective-permute-start(bf16[256,256]{1,0:T(8,128)(2,1)S(1)} %get-tuple-element.36), channel_id=1, source_target_pairs={{0,6},{1,7},{2,4},{3,5},{4,2},{5,3},{6,0},{7,1},{8,14},{9,15},{10,... | collective-permute-start | bytes 393224 | tf_op jit(solution)/shard_map/ppermute | solution.py:22
  54.9 14.9 %collective-permute-start.25 = (bf16[256,1024]{1,0:T(8,128)(2,1)S(1)}, bf16[256,1024]{1,0:T(8,128)(2,1)S(1)}, u32[]{:S(2)}, u32[]{:S(2)}) collective-permute-start(bf16[256,1024]{1,0:T(8,128)(2,1)S(1)} %shard_map.84), channel_id=1, source_target_pairs={{0,1},{1,0},{2,3},{3,2},{4,5},{5,4},{6,7},{7,6},{8,9},{9,8},{10,11... | collective-permute-start | bytes 1572872 | tf_op jit(solution)/shard_map/ppermute | solution.py:22
  55.9 25.2 %collective-permute-start.13 = (bf16[256,1024]{1,0:T(8,128)(2,1)S(1)}, bf16[256,1024]{1,0:T(8,128)(2,1)S(1)}, u32[]{:S(2)}, u32[]{:S(2)}) collective-permute-start(bf16[256,1024]{1,0:T(8,128)(2,1)S(1)} %shard_map.80), channel_id=1, source_target_pairs={{0,1},{1,0},{2,3},{3,2},{4,5},{5,4},{6,7},{7,6},{8,9},{9,8},{10,11... | collective-permute-start | bytes 1572872 | tf_op jit(solution)/shard_map/ppermute | solution.py:22
  57.9 23.2 %collective-permute-start.19 = (bf16[256,1024]{1,0:T(8,128)(2,1)S(1)}, bf16[256,1024]{1,0:T(8,128)(2,1)S(1)}, u32[]{:S(2)}, u32[]{:S(2)}) collective-permute-start(bf16[256,1024]{1,0:T(8,128)(2,1)S(1)} %add_convert_fusion.2), channel_id=1, source_target_pairs={{0,8},{1,9},{2,10},{3,11},{4,12},{5,13},{6,14},{7,15},{8,0},{9,1},... | collective-permute-start | bytes 1572872 | tf_op jit(solution)/shard_map/ppermute | solution.py:22
  66.8 24.1 %collective-permute-start.8 = (bf16[256,1024]{1,0:T(8,128)(2,1)S(1)}, bf16[256,1024]{1,0:T(8,128)(2,1)S(1)}, u32[]{:S(2)}, u32[]{:S(2)}) collective-permute-start(bf16[256,1024]{1,0:T(8,128)(2,1)S(1)} %shard_map.78), channel_id=1, source_target_pairs={{0,1},{1,0},{2,3},{3,2},{4,5},{5,4},{6,7},{7,6},{8,9},{9,8},{10,11... | collective-permute-start | bytes 1572872 | tf_op jit(solution)/shard_map/ppermute | solution.py:22
  70.0 20.9 %collective-permute-start.26 = (bf16[256,1024]{1,0:T(8,128)(2,1)S(1)}, bf16[256,1024]{1,0:T(8,128)(2,1)S(1)}, u32[]{:S(2)}, u32[]{:S(2)}) collective-permute-start(bf16[256,1024]{1,0:T(8,128)(2,1)S(1)} %add_convert_fusion), channel_id=1, source_target_pairs={{0,8},{1,9},{2,10},{3,11},{4,12},{5,13},{6,14},{7,15},{8,0},{9,1},... | collective-permute-start | bytes 1572872 | tf_op jit(solution)/shard_map/ppermute | solution.py:22
  81.4 21.6 %collective-permute-start.20 = (bf16[256,1024]{1,0:T(8,128)(2,1)S(1)}, bf16[256,1024]{1,0:T(8,128)(2,1)S(1)}, u32[]{:S(2)}, u32[]{:S(2)}) collective-permute-start(bf16[256,1024]{1,0:T(8,128)(2,1)S(1)} %add_convert_fusion.1), channel_id=1, source_target_pairs={{0,16},{1,17},{2,18},{3,19},{4,20},{5,21},{6,22},{7,23},{8,24},{9,... | collective-permute-start | bytes 1572872 | tf_op jit(solution)/shard_map/ppermute | solution.py:22
  84.0 6.1 %collective-permute-start.1 = (bf16[256,256]{1,0:T(8,128)(2,1)S(1)}, bf16[256,256]{1,0:T(8,128)(2,1)S(1)}, u32[]{:S(2)}, u32[]{:S(2)}) collective-permute-start(bf16[256,256]{1,0:T(8,128)(2,1)S(1)} %get-tuple-element.23), channel_id=1, source_target_pairs={{0,4},{1,5},{2,6},{3,7},{4,0},{5,1},{6,2},{7,3},{8,12},{9,13},{10,... | collective-permute-start | bytes 393224 | tf_op jit(solution)/shard_map/ppermute | solution.py:22
  (15 other events, 178.2 us)

commit v2 on v0

v2 whole, which is shorter than its diff:
```python
import functools
import jax
import jax.numpy as jnp
from jax import lax
from jax.experimental import pallas as pl
from jax.experimental.pallas import tpu as pltpu
from jax.sharding import PartitionSpec as P

STEP = 10
AXES = ("replica", "shard")
F32 = jnp.float32
BF16 = jnp.bfloat16
VMEM = pl.BlockSpec(memory_space=pltpu.VMEM)
PARAMS = pltpu.CompilerParams(vmem_limit_bytes=32 * 2**20)
OUTER = ((0, 1), (3, 2))
INNER = ((1, 2), (2, 1))
PAIRS = ((0, 1), (1, 0), (2, 3), (3, 2))

STEPS = (
    "bx", "bc", "own0", "px0", "px1", "br0", "br1", "pr0", "kk0", "yy0", "px2", "pr1", "own1", "kk1", "rr0",
    "za0", "yy1", "px3", "pr2", "kk2", "rr1", "za1", "zb1", "yy2", "px4", "pr3", "kk3", "rr2", "za2", "zb2",
    "yy3", "pr4", "kk4", "rr3",
)
GATES = {"pr0": ("own0",)}
EXTRA = {"kk4": ("zb2",)}
COST = {"add3": 1120000000, "kk1": 280000000, "kk2": 840000000, "kk3": 1680000000, "kk4": 2800000000}
CUT = 2
LINE = {
    "za0": ("rr0", OUTER),
    "za1": ("rr1", OUTER),
    "zb1": ("rr1", INNER),
    "za2": ("rr2", PAIRS),
    "zb2": ("rr0", INNER),
}
ARRIVES = {0: (), 1: ("za0",), 2: ("zb1",), 3: ("za2", "zb2")}


def steps_for(chunks):
    names = ["bx", "bc", "own0", "own1", "br0", "br1"]
    for i in range(chunks + 1):
        names += [kind + str(i) for kind in ("px", "pr", "kk")]
        if i < chunks:
            names.append("yy%d" % i)
        if i > 0:
            names.append("rr%d" % (i - 1))
        if 0 < i < chunks:
            names.append("za%d" % (i - 1))
    return names


def flip(values, n_replica, n_shard, replica_bits, shard_bits):
    pairs = []
    for rep in range(n_replica):
        for sh in range(n_shard):
            there = (rep ^ replica_bits) * n_shard + (sh ^ shard_bits)
            pairs.append((rep * n_shard + sh, there))
    return lax.ppermute(values, AXES, pairs)


def along(values, n_shard, hops):
    size = 4 * n_shard
    pairs = [(here * size + low, there * size + low) for here, there in hops for low in range(size)]
    return lax.ppermute(values, AXES, pairs)


def gated(values, gates):
    return lax.optimization_barrier((tuple(values), tuple(gates)))[0]


def pack_kernel(chunks, n_shard, own, where, normed, *refs):
    n_out = 3 + chunks
    outs, (buf, turned, sems) = refs[:n_out], refs[n_out:]
    mine, core, cross = outs[0], outs[1], outs[2:]
    rest, x, c, y = where[0], where[1], where[2], where[3]
    width = n_shard * own
    order = [(step, 1, dc) for step in range(chunks) for dc in (0, 1)]
    order += [(step, 0, dc) for step in range(chunks) for dc in (1, 0)]
    copies = []
    for at, (step, dx, dc) in enumerate(order):
        k = chunks - 1 - step
        block = ((rest ^ k) * 2 + (x ^ dx)) * 2 + (c ^ dc)
        start = pl.multiple_of(block * width, width)
        copy = pltpu.make_async_copy(normed.at[:, pl.ds(start, width)], buf.at[at], sems.at[at])
        copy.start()
        copies.append(copy)
    for at, (step, dx, dc) in enumerate(order):
        copies[at].wait()
        turned[...] = buf[at].T
        for j in range(n_shard):
            rows = turned[pl.ds(pl.multiple_of((y ^ j) * own, own), own), :]
            if not dx:
                into = core if dc else mine
                at_row = step * width + ((j - 1) * own if j else width - own)
            elif j == 0:
                into = cross[step + 1]
                at_row = dc * (width if step + 1 < chunks else own)
            else:
                into = cross[step]
                head = own if step > 0 else 0
                at_row = dc * (head + width - own) + head + (j - 1) * own
            into[pl.ds(at_row, own), :] = rows


def pack(where, normed, chunks, n_shard, own):
    depth, group = normed.shape[0], n_shard * own
    shapes = [jax.ShapeDtypeStruct((chunks * group, depth), BF16)] * 2
    for piece in range(chunks + 1):
        rows = (own if piece > 0 else 0) + (group - own if piece < chunks else 0)
        shapes.append(jax.ShapeDtypeStruct((2 * rows, depth), BF16))
    return pl.pallas_call(
        functools.partial(pack_kernel, chunks, n_shard, own),
        out_shape=shapes,
        in_specs=[pl.BlockSpec(memory_space=pltpu.SMEM), pl.BlockSpec(memory_space=pl.ANY)],
        out_specs=[VMEM] * len(shapes),
        scratch_shapes=[
            pltpu.VMEM((4 * chunks, depth, group), BF16),
            pltpu.VMEM((group, depth), BF16),
            pltpu.SemaphoreType.DMA((4 * chunks,)),
        ],
        compiler_params=PARAMS,
        cost_estimate=pl.CostEstimate(flops=0, bytes_accessed=2 * normed.size * 2, transcendentals=0),
    )(where, normed)


def product_kernel(offset, core_offset, stay, leave, own_a, core_a, x_a, xc_a, b0, b1, b2, b3, b4, *refs):
    n_out = (stay > 0) + (leave > 0)
    extra, outs = refs[: len(refs) - n_out], refs[len(refs) - n_out :]
    cut = b3.shape[1]
    tile = 256
    work = []
    if leave:
        work.append((stay, leave, outs[0], ()))
    if stay:
        work.append((0, stay, outs[-1], extra))
    for first, rows, out, more in work:
        lhs = [own_a[pl.ds(offset + first, rows), :], core_a[pl.ds(core_offset + first, rows), :]]
        lhs += [r[pl.ds(first, rows), :] for r in (x_a, xc_a)]
        for col in range(0, out.shape[1], tile):
            last = b3[:, pl.ds(col, tile)] if col < cut else b4[:, pl.ds(col - cut, tile)]
            rhs = [r[:, pl.ds(col, tile)] for r in (b0, b1, b2)] + [last]
            total = None
            for a, b in zip(lhs, rhs):
                part = jnp.dot(a, b, preferred_element_type=F32)
                part = part.astype(BF16).astype(F32)
                total = part if total is None else total + part
            for ref in more:
                total = total + ref[:, pl.ds(col, tile)].astype(F32)
            out[:, pl.ds(col, tile)] = total.astype(out.dtype)


def product(offset, core_offset, stay, leave, lhs, rhs, extra, cost):
    columns = rhs[0].shape[1]
    shapes = [jax.ShapeDtypeStruct((leave, columns), BF16)] * (leave > 0)
    shapes += [jax.ShapeDtypeStruct((stay, columns), F32)] * (stay > 0)
    return pl.pallas_call(
        functools.partial(product_kernel, offset, core_offset, stay, leave),
        out_shape=shapes,
        in_specs=[VMEM] * (9 + len(extra)),
        out_specs=[VMEM] * len(shapes),
        compiler_params=PARAMS,
        cost_estimate=pl.CostEstimate(flops=cost, bytes_accessed=0, transcendentals=0),
    )(*lhs, *rhs, *extra)


def add_kernel(a, b, out):
    out[...] = a[...] + b[...].astype(F32)


def add(a, b, cost):
    return pl.pallas_call(
        add_kernel,
        out_shape=jax.ShapeDtypeStruct(a.shape, F32),
        in_specs=[VMEM] * 2,
        out_specs=VMEM,
        compiler_params=PARAMS,
        cost_estimate=pl.CostEstimate(flops=cost, bytes_accessed=0, transcendentals=0),
    )(a, b)


def finish_kernel(*refs):
    terms, grad, squares = refs[:-2], refs[-2], refs[-1]
    block = min(grad.shape[0], 32)
    acc = jnp.zeros((8, grad.shape[1]), F32)
    for row in range(0, grad.shape[0], block):
        total = terms[0][pl.ds(row, block), :]
        for term in terms[1:]:
            total = total + term[pl.ds(row, block), :].astype(F32)
        grad[pl.ds(row, block), :] = total
        total = total * total
        for first in range(0, block, 8):
            acc = acc + total[first : first + 8, :]
    acc = jnp.sum(acc, axis=0, keepdims=True)
    part = acc[:, :128]
    for col in range(128, grad.shape[1], 128):
        part = part + acc[:, col : col + 128]
    squares[...] = jnp.broadcast_to(part[None], squares.shape)


def finish(terms, devices):
    return pl.pallas_call(
        finish_kernel,
        out_shape=[jax.ShapeDtypeStruct(terms[0].shape, F32), jax.ShapeDtypeStruct((devices, 1, 128), F32)],
        in_specs=[VMEM] * len(terms),
        out_specs=[VMEM] * 2,
        compiler_params=PARAMS,
    )(*terms)


def update_kernel(limit, block, squares, grad, weight, moment, variance, new_weight, new_moment, new_variance):
    clip = jnp.minimum(jnp.float32(1.0), limit / (jnp.sqrt(jnp.sum(squares[...])) + 1e-06))
    rows = pl.ds(pl.multiple_of(pl.program_id(0) * block, block), block)
    scaled = clip * grad[rows, :]
    first = 0.9 * moment[rows, :] + 0.1 * scaled
    second = 0.95 * variance[rows, :] + 0.05 * scaled * scaled
    new_moment[...] = first
    new_variance[...] = second
    first = first / (1.0 - 0.9**STEP)
    second = second / (1.0 - 0.95**STEP)
    old = weight[rows, :]
    new_weight[...] = old - 0.01 * (first / (jnp.sqrt(second) + 1e-08) + 0.1 * old)


def update(squares, grad, weight, moment, variance):
    rows, columns = grad.shape
    block = min(rows, 64)
    limit = float(rows * columns * squares.shape[0]) ** 0.5
    return pl.pallas_call(
        functools.partial(update_kernel, limit, block),
        grid=(rows // block,),
        out_shape=[jax.ShapeDtypeStruct(grad.shape, F32)] * 3,
        in_specs=[VMEM] * 5,
        out_specs=[pl.BlockSpec((block, columns), lambda i: (i, 0))] * 3,
        compiler_params=PARAMS,
    )(squares, grad, weight, moment, variance)


def shards(normed, out_grads, weight, moment, variance):
    width = normed.shape[1]
    columns = out_grads.shape[1]
    n_replica = lax.axis_size("replica")
    n_shard = lax.axis_size("shard")
    chunks = n_replica // 4
    line = chunks == 4
    own = width // (n_replica * n_shard)
    group = n_shard * own
    half = columns // 2
    middle = CUT * group - own
    rep = lax.axis_index("replica")
    where = jnp.stack([rep // 4, (rep // 2) % 2, rep % 2, lax.axis_index("shard")]).astype(jnp.int32)
    packed = pack(where, normed, chunks, n_shard, own)
    a_own, a_core, cross = packed[0], packed[1], packed[2:]

    done, arriving, sums, terms = {}, [[] for _ in range(chunks)], {}, []

    def ready(name, values):
        gates = [v for gate in GATES.get(name, ()) for v in done[gate]] if line else []
        return gated(values, gates) if gates else tuple(values)

    def go(name, value, replica_bits, shard_bits):
        with jax.named_scope("mv_" + name):
            return [flip(ready(name, [value])[0], n_replica, n_shard, replica_bits, shard_bits)]

    for name in STEPS if line else steps_for(chunks):
        kind = name.rstrip("0123456789")
        step = int(name[len(kind) :] or 0)
        cost = COST.get(name, 0)
        if kind == "bx":
            out = go(name, out_grads, 2, 0)
        elif kind == "bc":
            out = go(name, out_grads, 1, 0)
        elif kind == "br":
            value = done["bx"][0]
            out = go(name, value[:, :half] if step == 0 else value[:, half:], 1, 0)
        elif kind == "own":
            out = go(name, a_core[:middle] if step == 0 else a_core[middle:], 1, 0)
        elif kind == "px":
            out = go(name, cross[step], 2, 0)
        elif kind == "pr":
            value = done["px%d" % step][0]
            out = go(name, value[value.shape[0] // 2 :], 1, 0)
        elif kind == "kk":
            stay = own if step > 0 else 0
            leave = group - own if step < chunks else 0
            offset = step * group - stay
            late = step >= CUT
            core_part = done["own1" if late else "own0"][0]
            lhs = ready(name, (a_own, core_part, done["px%d" % step][0], done["pr%d" % step][0]))
            rhs = [out_grads] + [done[b][0] for b in ("bc", "bx", "br0", "br1")]
            extra = [done[k][0] for k in EXTRA.get(name, ())] if line else []
            out = product(offset, offset - middle * late, stay, leave, lhs, rhs, extra, cost)
        elif kind == "yy":
            value = done["kk%d" % step][0]
            out = []
            for j in range(1, n_shard):
                out += go(name, value[(j - 1) * own : j * own], 0, j)
        elif kind == "rr":
            terms = [done["kk%d" % (step + 1)][-1]]
            if line and "add%d" % step in COST:
                terms = [add(terms[0], done["yy%d" % step][0], COST["add%d" % step])]
            else:
                terms += done["yy%d" % step]
            if line:
                taken = EXTRA.get("kk%d" % (step + 1), ())
                terms += [done[k][0] for k in ARRIVES[step] if k not in taken]
            else:
                terms += arriving[chunks - 1 - step]
            if step < chunks - 1:
                total = terms[0]
                for term in terms[1:]:
                    total = total + term.astype(F32)
                sums[step] = total
                out = [total.astype(BF16)]
        elif line:
            source, hops = LINE[name]
            value = done[source][0]
            if name == "zb2":
                value = (sums[0] + done["za1"][0].astype(F32)).astype(BF16)
            with jax.named_scope("mv_" + name):
                out = [along(ready(name, [value])[0], n_shard, hops)]
        else:
            k = chunks - 1 - step
            low = k & -k
            out = go(name, done["rr%d" % step][0], 4 * low, 0)
            arriving[k ^ low] += out
        done[name] = out

    grad, squares = finish(terms, n_replica * n_shard)
    with jax.named_scope("squares"):
        squares = lax.all_to_all(squares, AXES, 0, 0)
    return update(squares, grad, weight, moment, variance)


def solution(mesh):
    spec = P(AXES, None)
    return jax.shard_map(shards, mesh=mesh, in_specs=(spec,) * 5, out_specs=(spec,) * 3, check_vma=False)
```

time: 353 us -> 99.1 us (0.28)
  waiting for transfers between devices: 239 us -> 39.5 us
  blocking collectives: 39.3 us -> 9.11 us
  starting transfers between devices: 5.69 us -> 33.9 us
  other arithmetic: 21.9 us -> 0.96 us
  local copies, waits for them, and re-layouts: 18.9 us -> 2.39 us
  between operations: 14.8 us -> 0.9 us
  matrix products: 12.7 us -> 0 us
  Pallas kernels: 0 us -> 12 us
    reduce_scatter x1 -> x0, waiting for transfers between devices: 179 us -> none  [shards(): grad = lax.psum_scatter(summed, 'replica', scatter_dimension=0, tiled=True)]
    ppermute x0 -> x25, waiting for transfers between devices: none -> 39.5 us  [the longest x20 25.8 us: flip(): return lax.ppermute(values, AXES, pairs)]
    psum x1 -> x0, blocking collectives: 39.3 us -> none  [shards(): squares = lax.psum(jnp.sum(grad * grad), ('replica', 'shard'))]
    all_gather x1 -> x0, waiting for transfers between devices: 37.5 us -> none  [shards(): piece = lax.all_gather(out_grads, 'shard', axis=0, tiled=True)]
    ppermute x0 -> x25, starting transfers between devices: none -> 33.9 us  [the longest x20 18.8 us: flip(): return lax.ppermute(values, AXES, pairs)]
    all_to_all x1 -> x0, waiting for transfers between devices: 21.8 us -> none  [shards(): lax.all_to_all(grid, 'shard', split_axis=2, concat_axis=0, tiled=True)]
    reshape x2 -> x0, local copies, waits for them, and re-layouts: 18.9 us -> none  [shards(): grid = normed.reshape(tokens, n_replica, n_shard, own_rows)]
    reduce_sum x2 -> x0, other arithmetic: 18.5 us -> none  [the longest x1 16.4 us: shards(): summed = jnp.sum(to_wire(parts), axis=0)]
  transfers between devices with their start and end apart: 3 -> 25, of which waited for: 3 -> 12; matrix products, arithmetic and copies ran while one was open for 0% -> 1% of each run, Pallas kernels for 0% -> 9%
where the time goes in v2:
time: 99.1 us; the launch traced here: 98.8 us
  waiting for transfers between devices  39.5 us (40%)
  starting transfers between devices  33.9 us (34%)
  Pallas kernels  12 us (12%)
  blocking collectives  9.11 us (9%)
  local copies, waits for them, and re-layouts  2.39 us (2%)
    ppermute x20, waiting for transfers between devices, flip(): return lax.ppermute(values, AXES, pairs)  25.8 us
    ppermute x20, starting transfers between devices, flip(): return lax.ppermute(values, AXES, pairs)  18.8 us
    ppermute x5, starting transfers between devices, along(): return lax.ppermute(values, AXES, pairs)  15.1 us
    ppermute x5, waiting for transfers between devices, along(): return lax.ppermute(values, AXES, pairs)  13.7 us
    all_to_all x1, blocking collectives, shards(): squares = lax.all_to_all(squares, AXES, 0, 0)  9.11 us
    pallas_call x5, Pallas kernels, product(): pl.pallas_call(functools.partial(product_kernel, offset, core_offset, sta...  5.32 us
    pallas_call x1, Pallas kernels, pack(): pl.pallas_call(functools.partial(pack_kernel, chunks, n_shard, own), out_...  3.28 us
    pallas_call x1, Pallas kernels, update(): pl.pallas_call(functools.partial(update_kernel, limit, block), grid=(rows...  3.19 us
  transfers between devices with their start and end apart: 25, of which 12 were waited for; matrix products, arithmetic and copies ran while one was open for 1% of the time, Pallas kernels for 9%

profile of v2, /device:TPU:0, one launch (start us, length us, event | category | flops | bytes accessed | tf_op | source)
XLA Modules:
  0.0 98.8 jit_solution(900471486458656020)
XLA Ops:
  0.6 3.0 %collective-permute-start.4 = (bf16[256,1024]{1,0:T(8,128)(2,1)}, bf16[256,1024]{1,0:T(8,128)(2,1)S(1)}, u32[]{:S(2)}, u32[]{:S(2)}) collective-permute-start(bf16[256,1024]{1,0:T(8,128)(2,1)} %b0.9), channel_id=1, source_target_pairs={{0,4},{1,5},{2,6},{3,7},{4,0},{5,1},{6,2},{7,3},{8,12},{9,13},{10,... | collective-permute-start | bytes 1572872 | tf_op jit(solution)/shard_map/mv_bx/ppermute | solution.py:57
  3.7 2.2 %copy-done.1 = bf16[256,8192]{1,0:T(8,128)(2,1)S(1)} copy-done((bf16[256,8192]{1,0:T(8,128)(2,1)S(1)}, bf16[256,8192]{1,0:T(8,128)(2,1)}, u32[]{:S(2)}) %copy-start.1) | copy-done | bytes 4194328
  5.9 3.3 %shard_map.76 = (bf16[2048,256]{1,0:T(8,128)(2,1)S(1)}, bf16[2048,256]{1,0:T(8,128)(2,1)S(1)}, bf16[512,256]{1,0:T(8,128)(2,1)S(1)}, bf16[1024,256]{1,0:T(8,128)...) custom-call(s32[4]{0:T(128)S(1)} %pad_add_fusion.where, ...), custom_call_target="tpu_custom_call" | custom-call | bytes 8388608 | tf_op jit(solution)/shard_map/pallas_call | solution.py:110
  9.9 2.0 %collective-permute-start.8 = (bf16[1024,256]{1,0:T(8,128)(2,1)S(1)}, bf16[1024,256]{1,0:T(8,128)(2,1)S(1)}, u32[]{:S(2)}, u32[]{:S(2)}) collective-permute-start(bf16[1024,256]{1,0:T(8,128)(2,1)S(1)} %get-tuple-element.22), channel_id=1, source_target_pairs={{0,4},{1,5},{2,6},{3,7},{4,0},{5,1},{6,2},{7,3},{8,12},{9,13},{10,... | collective-permute-start | bytes 1572872 | tf_op jit(solution)/shard_map/mv_px1/ppermute | solution.py:57
  11.8 4.8 %collective-permute-done.4.b2 = bf16[256,1024]{1,0:T(8,128)(2,1)S(1)} collective-permute-done((bf16[256,1024]{1,0:T(8,128)(2,1)}, bf16[256,1024]{1,0:T(8,128)(2,1)S(1)}, u32[]{:S(2)}, u32[]{:S(2)}) %collective-permute-start.4) | collective-permute-done | bytes 524320 | tf_op jit(solution)/shard_map/mv_bx/ppermute | solution.py:57
  16.7 5.5 %collective-permute-done.10.x_a = bf16[512,256]{1,0:T(8,128)(2,1)S(1)} collective-permute-done((bf16[512,256]{1,0:T(8,128)(2,1)S(1)}, bf16[512,256]{1,0:T(8,128)(2,1)S(1)}, u32[]{:S(2)}, u32[]{:S(2)}) %collective-permute-start.10) | collective-permute-done | bytes 262176 | tf_op jit(solution)/shard_map/mv_px0/ppermute | solution.py:57
  24.7 2.2 %collective-permute-start.12 = (bf16[256,1024]{1,0:T(8,128)(2,1)S(1)}, bf16[256,1024]{1,0:T(8,128)(2,1)S(1)}, u32[]{:S(2)}, u32[]{:S(2)}) collective-permute-start(bf16[256,1024]{1,0:T(8,128)(2,1)S(1)} %shard_map.78), channel_id=1, source_target_pairs={{0,1},{1,0},{2,3},{3,2},{4,5},{5,4},{6,7},{7,6},{8,9},{9,8},{10,11... | collective-permute-start | bytes 1572872 | tf_op jit(solution)/shard_map/mv_yy0/ppermute | solution.py:57
  26.8 5.8 %collective-permute-done.8.x_a = bf16[1024,256]{1,0:T(8,128)(2,1)S(1)} collective-permute-done((bf16[1024,256]{1,0:T(8,128)(2,1)S(1)}, bf16[1024,256]{1,0:T(8,128)(2,1)S(1)}, u32[]{:S(2)}, u32[]{:S(2)}) %collective-permute-start.8) | collective-permute-done | bytes 524320 | tf_op jit(solution)/shard_map/mv_px1/ppermute | solution.py:57
  32.7 1.8 %collective-permute-start.13 = (bf16[1024,256]{1,0:T(8,128)(2,1)S(1)}, bf16[1024,256]{1,0:T(8,128)(2,1)S(1)}, u32[]{:S(2)}, u32[]{:S(2)}) collective-permute-start(bf16[1024,256]{1,0:T(8,128)(2,1)S(1)} %get-tuple-element.26), channel_id=1, source_target_pairs={{0,4},{1,5},{2,6},{3,7},{4,0},{5,1},{6,2},{7,3},{8,12},{9,13},{10,... | collective-permute-start | bytes 1572872 | tf_op jit(solution)/shard_map/mv_px2/ppermute | solution.py:57
  36.1 1.6 %collective-permute-start.15 = (bf16[256,1024]{1,0:T(8,128)(2,1)S(1)}, bf16[256,1024]{1,0:T(8,128)(2,1)S(1)}, u32[]{:S(2)}, u32[]{:S(2)}) collective-permute-start(bf16[256,1024]{1,0:T(8,128)(2,1)S(1)} %get-tuple-element.28), channel_id=1, source_target_pairs={{0,1},{1,0},{2,3},{3,2},{4,5},{5,4},{6,7},{7,6},{8,9},{9,8},{10,11... | collective-permute-start | bytes 1572872 | tf_op jit(solution)/shard_map/mv_yy1/ppermute | solution.py:57
  39.3 3.9 %collective-permute-start.16 = (bf16[256,1024]{1,0:T(8,128)(2,1)S(1)}, bf16[256,1024]{1,0:T(8,128)(2,1)S(1)}, u32[]{:S(2)}, u32[]{:S(2)}) collective-permute-start(bf16[256,1024]{1,0:T(8,128)(2,1)S(1)} %fusion), channel_id=1, source_target_pairs={{0,8},{1,9},{2,10},{3,11},{4,12},{5,13},{6,14},{7,15},{24,16},{25,... | collective-permute-start | bytes 1572872 | tf_op jit(solution)/shard_map/mv_za0/ppermute | solution.py:63
  43.3 3.8 %collective-permute-done.13.x_a = bf16[1024,256]{1,0:T(8,128)(2,1)S(1)} collective-permute-done((bf16[1024,256]{1,0:T(8,128)(2,1)S(1)}, bf16[1024,256]{1,0:T(8,128)(2,1)S(1)}, u32[]{:S(2)}, u32[]{:S(2)}) %collective-permute-start.13) | collective-permute-done | bytes 524320 | tf_op jit(solution)/shard_map/mv_px2/ppermute | solution.py:57
  47.2 1.8 %collective-permute-start.19 = (bf16[1024,256]{1,0:T(8,128)(2,1)S(1)}, bf16[1024,256]{1,0:T(8,128)(2,1)S(1)}, u32[]{:S(2)}, u32[]{:S(2)}) collective-permute-start(bf16[1024,256]{1,0:T(8,128)(2,1)S(1)} %get-tuple-element.29), channel_id=1, source_target_pairs={{0,4},{1,5},{2,6},{3,7},{4,0},{5,1},{6,2},{7,3},{8,12},{9,13},{10,... | collective-permute-start | bytes 1572872 | tf_op jit(solution)/shard_map/mv_px3/ppermute | solution.py:57
  50.4 3.4 %collective-permute-done.16 = bf16[256,1024]{1,0:T(8,128)(2,1)S(1)} collective-permute-done((bf16[256,1024]{1,0:T(8,128)(2,1)S(1)}, bf16[256,1024]{1,0:T(8,128)(2,1)S(1)}, u32[]{:S(2)}, u32[]{:S(2)}) %collective-permute-start.16) | collective-permute-done | bytes 524320 | tf_op jit(solution)/shard_map/mv_za0/ppermute | solution.py:63
  54.0 4.4 %collective-permute-start.17 = (bf16[256,1024]{1,0:T(8,128)(2,1)S(1)}, bf16[256,1024]{1,0:T(8,128)(2,1)S(1)}, u32[]{:S(2)}, u32[]{:S(2)}) collective-permute-start(bf16[256,1024]{1,0:T(8,128)(2,1)S(1)} %add_convert_fusion.2), channel_id=1, source_target_pairs={{0,8},{1,9},{2,10},{3,11},{4,12},{5,13},{6,14},{7,15},{24,16},{25,... | collective-permute-start | bytes 1572872 | tf_op jit(solution)/shard_map/mv_za1/ppermute | solution.py:63
  58.4 1.6 %collective-permute-start.22 = (bf16[256,1024]{1,0:T(8,128)(2,1)S(1)}, bf16[256,1024]{1,0:T(8,128)(2,1)S(1)}, u32[]{:S(2)}, u32[]{:S(2)}) collective-permute-start(bf16[256,1024]{1,0:T(8,128)(2,1)S(1)} %get-tuple-element.32), channel_id=1, source_target_pairs={{0,1},{1,0},{2,3},{3,2},{4,5},{5,4},{6,7},{7,6},{8,9},{9,8},{10,11... | collective-permute-start | bytes 1572872 | tf_op jit(solution)/shard_map/mv_yy2/ppermute | solution.py:57
  60.7 1.6 %collective-permute-start.1 = (bf16[512,256]{1,0:T(8,128)(2,1)S(1)}, bf16[512,256]{1,0:T(8,128)(2,1)S(1)}, u32[]{:S(2)}, u32[]{:S(2)}) collective-permute-start(bf16[512,256]{1,0:T(8,128)(2,1)S(1)} %get-tuple-element.21), channel_id=1, source_target_pairs={{0,4},{1,5},{2,6},{3,7},{4,0},{5,1},{6,2},{7,3},{8,12},{9,13},{10,... | collective-permute-start | bytes 786440 | tf_op jit(solution)/shard_map/mv_px4/ppermute | solution.py:57
  62.4 5.6 %collective-permute-done.17 = bf16[256,1024]{1,0:T(8,128)(2,1)S(1)} collective-permute-done((bf16[256,1024]{1,0:T(8,128)(2,1)S(1)}, bf16[256,1024]{1,0:T(8,128)(2,1)S(1)}, u32[]{:S(2)}, u32[]{:S(2)}) %collective-permute-start.17) | collective-permute-done | bytes 524320 | tf_op jit(solution)/shard_map/mv_za1/ppermute | solution.py:63
  70.3 1.6 %collective-permute-start.21 = (bf16[256,1024]{1,0:T(8,128)(2,1)S(1)}, bf16[256,1024]{1,0:T(8,128)(2,1)S(1)}, u32[]{:S(2)}, u32[]{:S(2)}) collective-permute-start(bf16[256,1024]{1,0:T(8,128)(2,1)S(1)} %get-tuple-element.30), channel_id=1, source_target_pairs={{0,1},{1,0},{2,3},{3,2},{4,5},{5,4},{6,7},{7,6},{8,9},{9,8},{10,11... | collective-permute-start | bytes 1572872 | tf_op jit(solution)/shard_map/mv_yy3/ppermute | solution.py:57
  72.1 5.4 %collective-permute-start.24 = (bf16[256,1024]{1,0:T(8,128)(2,1)S(1)}, bf16[256,1024]{1,0:T(8,128)(2,1)S(1)}, u32[]{:S(2)}, u32[]{:S(2)}) collective-permute-start(bf16[256,1024]{1,0:T(8,128)(2,1)S(1)} %add_convert_fusion), channel_id=1, source_target_pairs={{0,8},{1,9},{2,10},{3,11},{4,12},{5,13},{6,14},{7,15},{8,0},{9,1},... | collective-permute-start | bytes 1572872 | tf_op jit(solution)/shard_map/mv_za2/ppermute | solution.py:63
  79.7 1.9 %collective-permute-done.21.b = bf16[256,1024]{1,0:T(8,128)(2,1)S(1)} collective-permute-done((bf16[256,1024]{1,0:T(8,128)(2,1)S(1)}, bf16[256,1024]{1,0:T(8,128)(2,1)S(1)}, u32[]{:S(2)}, u32[]{:S(2)}) %collective-permute-start.21) | collective-permute-done | bytes 524320 | tf_op jit(solution)/shard_map/mv_yy3/ppermute | solution.py:57
  81.7 4.7 %collective-permute-done.24.refs_1_ = bf16[256,1024]{1,0:T(8,128)(2,1)S(1)} collective-permute-done((bf16[256,1024]{1,0:T(8,128)(2,1)S(1)}, bf16[256,1024]{1,0:T(8,128)(2,1)S(1)}, u32[]{:S(2)}, u32[]{:S(2)}) %collective-permute-start.24) | collective-permute-done | bytes 524320 | tf_op jit(solution)/shard_map/mv_za2/ppermute | solution.py:63
  86.5 9.1 %all_to_all.5.squares = f32[32,1,128]{2,1,0:T(1,128)S(1)} all-to-all(f32[32,1,128]{2,1,0:T(1,128)S(1)} %get-tuple-element.33), channel_id=1, replica_groups=mesh['replica'=16,'shard'=2] {'replica','shard'}, dimensions={0} | all-to-all | bytes 32768 | tf_op jit(solution)/shard_map/squares/all_to_all | solution.py:329
  95.6 3.2 %shard_map.84 = (f32[256,1024]{1,0:T(8,128)}, f32[256,1024]{1,0:T(8,128)}, f32[256,1024]{1,0:T(8,128)}) custom-call(f32[32,1,128]{2,1,0:T(1,128)S(1)} %all_to_all.5.squares, f32[256,1024]{1,0:T(8,128)S(1)} %get-tuple-element.34.grad, f32[256,1024]{1,0:T(8,128)S(1)} %copy-done.2, f32[256,1024]{1,0:T(8,128)S(1)} %copy-done.3, f32[256,1024]{1,0:T(8,128)S(1)} %copy-done.4), custom_call_target="tpu_custom_call" | custom-call | tf_op jit(solution)/shard_map/pallas_call | solution.py:227
  (59 shorter events, 14.0 us)
Async XLA Ops:
  0.6 16.0 %collective-permute-start.4 = (bf16[256,1024]{1,0:T(8,128)(2,1)}, bf16[256,1024]{1,0:T(8,128)(2,1)S(1)}, u32[]{:S(2)}, u32[]{:S(2)}) collective-permute-start(bf16[256,1024]{1,0:T(8,128)(2,1)} %b0.9), channel_id=1, source_target_pairs={{0,4},{1,5},{2,6},{3,7},{4,0},{5,1},{6,2},{7,3},{8,12},{9,13},{10,... | collective-permute-start | bytes 1572872 | tf_op jit(solution)/shard_map/mv_bx/ppermute | solution.py:57
  9.2 13.0 %collective-permute-start.7 = (bf16[768,256]{1,0:T(8,128)(2,1)S(1)}, bf16[768,256]{1,0:T(8,128)(2,1)S(1)}, u32[]{:S(2)}, u32[]{:S(2)}) collective-permute-start(bf16[768,256]{1,0:T(8,128)(2,1)S(1)} %slice.31), channel_id=1, source_target_pairs={{0,2},{1,3},{2,0},{3,1},{4,6},{5,7},{6,4},{7,5},{8,10},{9,11},{10,... | collective-permute-start | bytes 1179656 | tf_op jit(solution)/shard_map/mv_own0/ppermute | solution.py:57
  9.3 13.5 %collective-permute-start.3 = (bf16[256,1024]{1,0:T(8,128)(2,1)S(1)}, bf16[256,1024]{1,0:T(8,128)(2,1)S(1)}, u32[]{:S(2)}, u32[]{:S(2)}) collective-permute-start(bf16[256,1024]{1,0:T(8,128)(2,1)S(1)} %copy-done), channel_id=1, source_target_pairs={{0,2},{1,3},{2,0},{3,1},{4,6},{5,7},{6,4},{7,5},{8,10},{9,11},{10,... | collective-permute-start | bytes 1572872 | tf_op jit(solution)/shard_map/mv_bc/ppermute | solution.py:57
  9.8 12.4 %collective-permute-start.10 = (bf16[512,256]{1,0:T(8,128)(2,1)S(1)}, bf16[512,256]{1,0:T(8,128)(2,1)S(1)}, u32[]{:S(2)}, u32[]{:S(2)}) collective-permute-start(bf16[512,256]{1,0:T(8,128)(2,1)S(1)} %get-tuple-element.24), channel_id=1, source_target_pairs={{0,4},{1,5},{2,6},{3,7},{4,0},{5,1},{6,2},{7,3},{8,12},{9,13},{10,... | collective-permute-start | bytes 786440 | tf_op jit(solution)/shard_map/mv_px0/ppermute | solution.py:57
  9.9 22.8 %collective-permute-start.8 = (bf16[1024,256]{1,0:T(8,128)(2,1)S(1)}, bf16[1024,256]{1,0:T(8,128)(2,1)S(1)}, u32[]{:S(2)}, u32[]{:S(2)}) collective-permute-start(bf16[1024,256]{1,0:T(8,128)(2,1)S(1)} %get-tuple-element.22), channel_id=1, source_target_pairs={{0,4},{1,5},{2,6},{3,7},{4,0},{5,1},{6,2},{7,3},{8,12},{9,13},{10,... | collective-permute-start | bytes 1572872 | tf_op jit(solution)/shard_map/mv_px1/ppermute | solution.py:57
  16.6 7.3 %collective-permute-start.5 = (bf16[256,512]{1,0:T(8,128)(2,1)S(1)}, bf16[256,512]{1,0:T(8,128)(2,1)S(1)}, u32[]{:S(2)}, u32[]{:S(2)}) collective-permute-start(bf16[256,512]{1,0:T(8,128)(2,1)S(1)} %get-tuple-element.36), channel_id=1, source_target_pairs={{0,2},{1,3},{2,0},{3,1},{4,6},{5,7},{6,4},{7,5},{8,10},{9,11},{10,... | collective-permute-start | bytes 786440 | tf_op jit(solution)/shard_map/mv_br0/ppermute | solution.py:57
  22.2 1.7 %collective-permute-start.6 = (bf16[256,512]{1,0:T(8,128)(2,1)S(1)}, bf16[256,512]{1,0:T(8,128)(2,1)S(1)}, u32[]{:S(2)}, u32[]{:S(2)}) collective-permute-start(bf16[256,512]{1,0:T(8,128)(2,1)S(1)} %get-tuple-element.35), channel_id=1, source_target_pairs={{0,2},{1,3},{2,0},{3,1},{4,6},{5,7},{6,4},{7,5},{8,10},{9,11},{10,... | collective-permute-start | bytes 786440 | tf_op jit(solution)/shard_map/mv_br1/ppermute | solution.py:57
  22.3 1.7 %collective-permute-start.11 = (bf16[256,256]{1,0:T(8,128)(2,1)S(1)}, bf16[256,256]{1,0:T(8,128)(2,1)S(1)}, u32[]{:S(2)}, u32[]{:S(2)}) collective-permute-start(bf16[256,256]{1,0:T(8,128)(2,1)S(1)} %slice.40), channel_id=1, source_target_pairs={{0,2},{1,3},{2,0},{3,1},{4,6},{5,7},{6,4},{7,5},{8,10},{9,11},{10,... | collective-permute-start | bytes 393224 | tf_op jit(solution)/shard_map/mv_pr0/ppermute | solution.py:57
  24.7 14.5 %collective-permute-start.12 = (bf16[256,1024]{1,0:T(8,128)(2,1)S(1)}, bf16[256,1024]{1,0:T(8,128)(2,1)S(1)}, u32[]{:S(2)}, u32[]{:S(2)}) collective-permute-start(bf16[256,1024]{1,0:T(8,128)(2,1)S(1)} %shard_map.78), channel_id=1, source_target_pairs={{0,1},{1,0},{2,3},{3,2},{4,5},{5,4},{6,7},{7,6},{8,9},{9,8},{10,11... | collective-permute-start | bytes 1572872 | tf_op jit(solution)/shard_map/mv_yy0/ppermute | solution.py:57
  32.7 2.2 %collective-permute-start.9 = (bf16[512,256]{1,0:T(8,128)(2,1)S(1)}, bf16[512,256]{1,0:T(8,128)(2,1)S(1)}, u32[]{:S(2)}, u32[]{:S(2)}) collective-permute-start(bf16[512,256]{1,0:T(8,128)(2,1)S(1)} %slice.39), channel_id=1, source_target_pairs={{0,2},{1,3},{2,0},{3,1},{4,6},{5,7},{6,4},{7,5},{8,10},{9,11},{10,... | collective-permute-start | bytes 786440 | tf_op jit(solution)/shard_map/mv_pr1/ppermute | solution.py:57
  32.7 14.3 %collective-permute-start.13 = (bf16[1024,256]{1,0:T(8,128)(2,1)S(1)}, bf16[1024,256]{1,0:T(8,128)(2,1)S(1)}, u32[]{:S(2)}, u32[]{:S(2)}) collective-permute-start(bf16[1024,256]{1,0:T(8,128)(2,1)S(1)} %get-tuple-element.26), channel_id=1, source_target_pairs={{0,4},{1,5},{2,6},{3,7},{4,0},{5,1},{6,2},{7,3},{8,12},{9,13},{10,... | collective-permute-start | bytes 1572872 | tf_op jit(solution)/shard_map/mv_px2/ppermute | solution.py:57
  34.6 14.4 %collective-permute-start = (bf16[1280,256]{1,0:T(8,128)(2,1)S(1)}, bf16[1280,256]{1,0:T(8,128)(2,1)S(1)}, u32[]{:S(2)}, u32[]{:S(2)}) collective-permute-start(bf16[1280,256]{1,0:T(8,128)(2,1)S(1)} %slice.27), channel_id=1, source_target_pairs={{0,2},{1,3},{2,0},{3,1},{4,6},{5,7},{6,4},{7,5},{8,10},{9,11},{10,... | collective-permute-start | bytes 1966088 | tf_op jit(solution)/shard_map/mv_own1/ppermute | solution.py:57
  36.1 14.3 %collective-permute-start.15 = (bf16[256,1024]{1,0:T(8,128)(2,1)S(1)}, bf16[256,1024]{1,0:T(8,128)(2,1)S(1)}, u32[]{:S(2)}, u32[]{:S(2)}) collective-permute-start(bf16[256,1024]{1,0:T(8,128)(2,1)S(1)} %get-tuple-element.28), channel_id=1, source_target_pairs={{0,1},{1,0},{2,3},{3,2},{4,5},{5,4},{6,7},{7,6},{8,9},{9,8},{10,11... | collective-permute-start | bytes 1572872 | tf_op jit(solution)/shard_map/mv_yy1/ppermute | solution.py:57
  39.3 14.4 %collective-permute-start.16 = (bf16[256,1024]{1,0:T(8,128)(2,1)S(1)}, bf16[256,1024]{1,0:T(8,128)(2,1)S(1)}, u32[]{:S(2)}, u32[]{:S(2)}) collective-permute-start(bf16[256,1024]{1,0:T(8,128)(2,1)S(1)} %fusion), channel_id=1, source_target_pairs={{0,8},{1,9},{2,10},{3,11},{4,12},{5,13},{6,14},{7,15},{24,16},{25,... | collective-permute-start | bytes 1572872 | tf_op jit(solution)/shard_map/mv_za0/ppermute | solution.py:63
  47.1 1.9 %collective-permute-start.14 = (bf16[512,256]{1,0:T(8,128)(2,1)S(1)}, bf16[512,256]{1,0:T(8,128)(2,1)S(1)}, u32[]{:S(2)}, u32[]{:S(2)}) collective-permute-start(bf16[512,256]{1,0:T(8,128)(2,1)S(1)} %slice.41), channel_id=1, source_target_pairs={{0,2},{1,3},{2,0},{3,1},{4,6},{5,7},{6,4},{7,5},{8,10},{9,11},{10,... | collective-permute-start | bytes 786440 | tf_op jit(solution)/shard_map/mv_pr2/ppermute | solution.py:57
  47.2 15.1 %collective-permute-start.19 = (bf16[1024,256]{1,0:T(8,128)(2,1)S(1)}, bf16[1024,256]{1,0:T(8,128)(2,1)S(1)}, u32[]{:S(2)}, u32[]{:S(2)}) collective-permute-start(bf16[1024,256]{1,0:T(8,128)(2,1)S(1)} %get-tuple-element.29), channel_id=1, source_target_pairs={{0,4},{1,5},{2,6},{3,7},{4,0},{5,1},{6,2},{7,3},{8,12},{9,13},{10,... | collective-permute-start | bytes 1572872 | tf_op jit(solution)/shard_map/mv_px3/ppermute | solution.py:57
  54.0 14.0 %collective-permute-start.17 = (bf16[256,1024]{1,0:T(8,128)(2,1)S(1)}, bf16[256,1024]{1,0:T(8,128)(2,1)S(1)}, u32[]{:S(2)}, u32[]{:S(2)}) collective-permute-start(bf16[256,1024]{1,0:T(8,128)(2,1)S(1)} %add_convert_fusion.2), channel_id=1, source_target_pairs={{0,8},{1,9},{2,10},{3,11},{4,12},{5,13},{6,14},{7,15},{24,16},{25,... | collective-permute-start | bytes 1572872 | tf_op jit(solution)/shard_map/mv_za1/ppermute | solution.py:63
  58.4 13.4 %collective-permute-start.22 = (bf16[256,1024]{1,0:T(8,128)(2,1)S(1)}, bf16[256,1024]{1,0:T(8,128)(2,1)S(1)}, u32[]{:S(2)}, u32[]{:S(2)}) collective-permute-start(bf16[256,1024]{1,0:T(8,128)(2,1)S(1)} %get-tuple-element.32), channel_id=1, source_target_pairs={{0,1},{1,0},{2,3},{3,2},{4,5},{5,4},{6,7},{7,6},{8,9},{9,8},{10,11... | collective-permute-start | bytes 1572872 | tf_op jit(solution)/shard_map/mv_yy2/ppermute | solution.py:57
  60.0 11.8 %collective-permute-start.23 = (bf16[256,1024]{1,0:T(8,128)(2,1)S(1)}, bf16[256,1024]{1,0:T(8,128)(2,1)S(1)}, u32[]{:S(2)}, u32[]{:S(2)}) collective-permute-start(bf16[256,1024]{1,0:T(8,128)(2,1)S(1)} %add_convert_fusion.2), channel_id=1, source_target_pairs={{8,16},{9,17},{10,18},{11,19},{12,20},{13,21},{14,22},{15,23},{16,... | collective-permute-start | bytes 1572872 | tf_op jit(solution)/shard_map/mv_zb1/ppermute | solution.py:63
  60.7 16.8 %collective-permute-start.1 = (bf16[512,256]{1,0:T(8,128)(2,1)S(1)}, bf16[512,256]{1,0:T(8,128)(2,1)S(1)}, u32[]{:S(2)}, u32[]{:S(2)}) collective-permute-start(bf16[512,256]{1,0:T(8,128)(2,1)S(1)} %get-tuple-element.21), channel_id=1, source_target_pairs={{0,4},{1,5},{2,6},{3,7},{4,0},{5,1},{6,2},{7,3},{8,12},{9,13},{10,... | collective-permute-start | bytes 786440 | tf_op jit(solution)/shard_map/mv_px4/ppermute | solution.py:57
  62.3 6.7 %collective-permute-start.20 = (bf16[512,256]{1,0:T(8,128)(2,1)S(1)}, bf16[512,256]{1,0:T(8,128)(2,1)S(1)}, u32[]{:S(2)}, u32[]{:S(2)}) collective-permute-start(bf16[512,256]{1,0:T(8,128)(2,1)S(1)} %slice.42), channel_id=1, source_target_pairs={{0,2},{1,3},{2,0},{3,1},{4,6},{5,7},{6,4},{7,5},{8,10},{9,11},{10,... | collective-permute-start | bytes 786440 | tf_op jit(solution)/shard_map/mv_pr3/ppermute | solution.py:57
  68.3 10.6 %collective-permute-start.18 = (bf16[256,1024]{1,0:T(8,128)(2,1)S(1)}, bf16[256,1024]{1,0:T(8,128)(2,1)S(1)}, u32[]{:S(2)}, u32[]{:S(2)}) collective-permute-start(bf16[256,1024]{1,0:T(8,128)(2,1)S(1)} %add_convert_fusion.1), channel_id=1, source_target_pairs={{8,16},{9,17},{10,18},{11,19},{12,20},{13,21},{14,22},{15,23},{16,... | collective-permute-start | bytes 1572872 | tf_op jit(solution)/shard_map/mv_zb2/ppermute | solution.py:63
  70.3 11.3 %collective-permute-start.21 = (bf16[256,1024]{1,0:T(8,128)(2,1)S(1)}, bf16[256,1024]{1,0:T(8,128)(2,1)S(1)}, u32[]{:S(2)}, u32[]{:S(2)}) collective-permute-start(bf16[256,1024]{1,0:T(8,128)(2,1)S(1)} %get-tuple-element.30), channel_id=1, source_target_pairs={{0,1},{1,0},{2,3},{3,2},{4,5},{5,4},{6,7},{7,6},{8,9},{9,8},{10,11... | collective-permute-start | bytes 1572872 | tf_op jit(solution)/shard_map/mv_yy3/ppermute | solution.py:57
  72.1 14.2 %collective-permute-start.24 = (bf16[256,1024]{1,0:T(8,128)(2,1)S(1)}, bf16[256,1024]{1,0:T(8,128)(2,1)S(1)}, u32[]{:S(2)}, u32[]{:S(2)}) collective-permute-start(bf16[256,1024]{1,0:T(8,128)(2,1)S(1)} %add_convert_fusion), channel_id=1, source_target_pairs={{0,8},{1,9},{2,10},{3,11},{4,12},{5,13},{6,14},{7,15},{8,0},{9,1},... | collective-permute-start | bytes 1572872 | tf_op jit(solution)/shard_map/mv_za2/ppermute | solution.py:63
  (6 other events, 60.2 us)

commit v3 on v2

--- a/solution.py
+++ b/solution.py
@@ -21,10 +21,11 @@
     "za0", "yy1", "px3", "pr2", "kk2", "rr1", "za1", "zb1", "yy2", "px4", "pr3", "kk3", "rr2", "za2", "zb2",
     "yy3", "pr4", "kk4", "rr3",
 )
-GATES = {"pr0": ("own0",)}
-EXTRA = {"kk4": ("zb2",)}
-COST = {"add3": 1120000000, "kk1": 280000000, "kk2": 840000000, "kk3": 1680000000, "kk4": 2800000000}
+GATES = {"px1": ("own0",)}
+EXTRA = {}
+COST = {"add2": 560000000, "add3": 1680000000, "fin": 224000000, "kk4": 1959999999}
 CUT = 2
+SPARE = 16
 LINE = {
     "za0": ("rr0", OUTER),
     "za1": ("rr1", OUTER),
@@ -162,19 +163,27 @@
     )(*lhs, *rhs, *extra)
 
 
-def add_kernel(a, b, out):
-    out[...] = a[...] + b[...].astype(F32)
-
-
-def add(a, b, cost):
-    return pl.pallas_call(
-        add_kernel,
-        out_shape=jax.ShapeDtypeStruct(a.shape, F32),
-        in_specs=[VMEM] * 2,
+def combine_kernel(*refs):
+    terms, out = refs[:-1], refs[-1]
+    rows, columns = terms[0].shape
+    total = terms[0][...]
+    for term in terms[1:]:
+        total = total + term[pl.ds(0, rows), :].astype(F32)
+    out[pl.ds(0, rows), :] = total.astype(out.dtype)
+    if out.shape[0] > rows:
+        out[pl.ds(rows, out.shape[0] - rows), :] = jnp.zeros((out.shape[0] - rows, columns), out.dtype)
+
+
+def combine(terms, dtype, cost, spare=0):
+    rows, columns = terms[0].shape
+    return pl.pallas_call(
+        combine_kernel,
+        out_shape=jax.ShapeDtypeStruct((rows + spare, columns), dtype),
+        in_specs=[VMEM] * len(terms),
         out_specs=VMEM,
         compiler_params=PARAMS,
         cost_estimate=pl.CostEstimate(flops=cost, bytes_accessed=0, transcendentals=0),
-    )(a, b)
+    )(*terms)
 
 
 def finish_kernel(*refs):
@@ -203,26 +212,30 @@
         in_specs=[VMEM] * len(terms),
         out_specs=[VMEM] * 2,
         compiler_params=PARAMS,
+        cost_estimate=pl.CostEstimate(flops=0, bytes_accessed=0, transcendentals=0),
     )(*terms)
 
 
-def update_kernel(limit, block, squares, grad, weight, moment, variance, new_weight, new_moment, new_variance):
-    clip = jnp.minimum(jnp.float32(1.0), limit / (jnp.sqrt(jnp.sum(squares[...])) + 1e-06))
+def update_kernel(limit, block, squares, grad, weight, moment, variance, new_weight, new_moment, new_variance, clip):
+    @pl.when(pl.program_id(0) == 0)
+    def _():
+        clip[0] = jnp.minimum(jnp.float32(1.0), limit / (jnp.sqrt(jnp.sum(squares[...])) + 1e-06))
+
     rows = pl.ds(pl.multiple_of(pl.program_id(0) * block, block), block)
-    scaled = clip * grad[rows, :]
+    scaled = clip[0] * grad[rows, :]
     first = 0.9 * moment[rows, :] + 0.1 * scaled
     second = 0.95 * variance[rows, :] + 0.05 * scaled * scaled
     new_moment[...] = first
     new_variance[...] = second
-    first = first / (1.0 - 0.9**STEP)
-    second = second / (1.0 - 0.95**STEP)
+    first = first * (1.0 / (1.0 - 0.9**STEP))
+    second = second * (1.0 / (1.0 - 0.95**STEP))
     old = weight[rows, :]
     new_weight[...] = old - 0.01 * (first / (jnp.sqrt(second) + 1e-08) + 0.1 * old)
 
 
 def update(squares, grad, weight, moment, variance):
     rows, columns = grad.shape
-    block = min(rows, 64)
+    block = min(rows, 128)
     limit = float(rows * columns * squares.shape[0]) ** 0.5
     return pl.pallas_call(
         functools.partial(update_kernel, limit, block),
@@ -230,6 +243,7 @@
         out_shape=[jax.ShapeDtypeStruct(grad.shape, F32)] * 3,
         in_specs=[VMEM] * 5,
         out_specs=[pl.BlockSpec((block, columns), lambda i: (i, 0))] * 3,
+        scratch_shapes=[pltpu.SMEM((1,), F32)],
         compiler_params=PARAMS,
     )(squares, grad, weight, moment, variance)
 
@@ -296,25 +310,26 @@
         elif kind == "rr":
             terms = [done["kk%d" % (step + 1)][-1]]
             if line and "add%d" % step in COST:
-                terms = [add(terms[0], done["yy%d" % step][0], COST["add%d" % step])]
+                terms = [combine([terms[0], done["yy%d" % step][0]], F32, COST["add%d" % step])]
             else:
                 terms += done["yy%d" % step]
+            sums[step] = list(terms)
             if line:
                 taken = EXTRA.get("kk%d" % (step + 1), ())
                 terms += [done[k][0] for k in ARRIVES[step] if k not in taken]
             else:
                 terms += arriving[chunks - 1 - step]
+            if line and step == chunks - 1 and "fin" in COST:
+                terms = [combine(terms[:2], F32, COST["fin"])] + terms[2:]
             if step < chunks - 1:
-                total = terms[0]
-                for term in terms[1:]:
-                    total = total + term.astype(F32)
-                sums[step] = total
-                out = [total.astype(BF16)]
+                out = [combine(terms, BF16, cost)]
         elif line:
             source, hops = LINE[name]
             value = done[source][0]
+            if name == "za1":
+                value = combine(sums[1], BF16, cost, SPARE)
             if name == "zb2":
-                value = (sums[0] + done["za1"][0].astype(F32)).astype(BF16)
+                value = combine(sums[0] + done["za1"], BF16, cost)
             with jax.named_scope("mv_" + name):
                 out = [along(ready(name, [value])[0], n_shard, hops)]
         else:

time: 99.1 us -> 96.4 us (0.973)
  waiting for transfers between devices: 39.5 us -> 33.2 us
  blocking collectives: 9.11 us -> 13.8 us
    ppermute x5, waiting for transfers between devices: 13.7 us -> 6.42 us  [along(): return lax.ppermute(values, AXES, pairs)]
    all_to_all x1, blocking collectives: 9.11 us -> 13.8 us  [shards(): squares = lax.all_to_all(squares, AXES, 0, 0)]
  transfers between devices with their start and end apart: 25 -> 25, of which waited for: 12 -> 13; matrix products, arithmetic and copies ran while one was open for 1% -> 0% of each run, Pallas kernels for 9% -> 10%
where the time goes in v3:
time: 96.4 us; the launch traced here: 96.2 us
  starting transfers between devices  33.9 us (35%)
  waiting for transfers between devices  33.2 us (34%)
  blocking collectives  13.8 us (14%)
  Pallas kernels  11.9 us (12%)
  local copies, waits for them, and re-layouts  2.39 us (2%)
    ppermute x20, waiting for transfers between devices, flip(): return lax.ppermute(values, AXES, pairs)  26.8 us
    ppermute x20, starting transfers between devices, flip(): return lax.ppermute(values, AXES, pairs)  18 us
    ppermute x5, starting transfers between devices, along(): return lax.ppermute(values, AXES, pairs)  16 us
    all_to_all x1, blocking collectives, shards(): squares = lax.all_to_all(squares, AXES, 0, 0)  13.8 us
    ppermute x5, waiting for transfers between devices, along(): return lax.ppermute(values, AXES, pairs)  6.42 us
    pallas_call x5, Pallas kernels, product(): pl.pallas_call(functools.partial(product_kernel, offset, core_offset, sta...  5.34 us
    pallas_call x1, Pallas kernels, pack(): pl.pallas_call(functools.partial(pack_kernel, chunks, n_shard, own), out_...  3.28 us
    unnamed x10, local copies, waits for them, and re-layouts  2.21 us
  transfers between devices with their start and end apart: 25, of which 13 were waited for; matrix products, arithmetic and copies ran while one was open for 0% of the time, Pallas kernels for 10%

profile of v3, /device:TPU:0, one launch (start us, length us, event | category | flops | bytes accessed | tf_op | source)
XLA Modules:
  0.0 96.2 jit_solution(480724944304840986)
XLA Ops:
  0.6 3.0 %collective-permute-start.4 = (bf16[256,1024]{1,0:T(8,128)(2,1)}, bf16[256,1024]{1,0:T(8,128)(2,1)S(1)}, u32[]{:S(2)}, u32[]{:S(2)}) collective-permute-start(bf16[256,1024]{1,0:T(8,128)(2,1)} %b0.9), channel_id=1, source_target_pairs={{0,4},{1,5},{2,6},{3,7},{4,0},{5,1},{6,2},{7,3},{8,12},{9,13},{10,... | collective-permute-start | bytes 1572872 | tf_op jit(solution)/shard_map/mv_bx/ppermute | solution.py:58
  3.7 2.2 %copy-done.1 = bf16[256,8192]{1,0:T(8,128)(2,1)S(1)} copy-done((bf16[256,8192]{1,0:T(8,128)(2,1)S(1)}, bf16[256,8192]{1,0:T(8,128)(2,1)}, u32[]{:S(2)}) %copy-start.1) | copy-done | bytes 4194328
  5.9 3.3 %shard_map.76 = (bf16[2048,256]{1,0:T(8,128)(2,1)S(1)}, bf16[2048,256]{1,0:T(8,128)(2,1)S(1)}, bf16[512,256]{1,0:T(8,128)(2,1)S(1)}, bf16[1024,256]{1,0:T(8,128)...) custom-call(s32[4]{0:T(128)S(1)} %pad_add_fusion.where, ...), custom_call_target="tpu_custom_call" | custom-call | bytes 8388608 | tf_op jit(solution)/shard_map/pallas_call | solution.py:111
  11.8 4.8 %collective-permute-done.4.b2 = bf16[256,1024]{1,0:T(8,128)(2,1)S(1)} collective-permute-done((bf16[256,1024]{1,0:T(8,128)(2,1)}, bf16[256,1024]{1,0:T(8,128)(2,1)S(1)}, u32[]{:S(2)}, u32[]{:S(2)}) %collective-permute-start.4) | collective-permute-done | bytes 524320 | tf_op jit(solution)/shard_map/mv_bx/ppermute | solution.py:58
  17.2 5.0 %collective-permute-done.17.x_a = bf16[512,256]{1,0:T(8,128)(2,1)S(1)} collective-permute-done((bf16[512,256]{1,0:T(8,128)(2,1)S(1)}, bf16[512,256]{1,0:T(8,128)(2,1)S(1)}, u32[]{:S(2)}, u32[]{:S(2)}) %collective-permute-start.17) | collective-permute-done | bytes 262176 | tf_op jit(solution)/shard_map/mv_px0/ppermute | solution.py:58
  22.3 1.3 %collective-permute-done.18.xc_a = bf16[256,256]{1,0:T(8,128)(2,1)S(1)} collective-permute-done((bf16[256,256]{1,0:T(8,128)(2,1)S(1)}, bf16[256,256]{1,0:T(8,128)(2,1)S(1)}, u32[]{:S(2)}, u32[]{:S(2)}) %collective-permute-start.18) | collective-permute-done | bytes 131104 | tf_op jit(solution)/shard_map/mv_pr0/ppermute | solution.py:58
  24.4 2.1 %collective-permute-start.19 = (bf16[256,1024]{1,0:T(8,128)(2,1)S(1)}, bf16[256,1024]{1,0:T(8,128)(2,1)S(1)}, u32[]{:S(2)}, u32[]{:S(2)}) collective-permute-start(bf16[256,1024]{1,0:T(8,128)(2,1)S(1)} %shard_map.83), channel_id=1, source_target_pairs={{0,1},{1,0},{2,3},{3,2},{4,5},{5,4},{6,7},{7,6},{8,9},{9,8},{10,11... | collective-permute-start | bytes 1572872 | tf_op jit(solution)/shard_map/mv_yy0/ppermute | solution.py:58
  26.6 1.5 %collective-permute-start.10 = (bf16[1024,256]{1,0:T(8,128)(2,1)S(1)}, bf16[1024,256]{1,0:T(8,128)(2,1)S(1)}, u32[]{:S(2)}, u32[]{:S(2)}) collective-permute-start(bf16[1024,256]{1,0:T(8,128)(2,1)S(1)} %get-tuple-element.25), channel_id=1, source_target_pairs={{0,4},{1,5},{2,6},{3,7},{4,0},{5,1},{6,2},{7,3},{8,12},{9,13},{10,... | collective-permute-start | bytes 1572872 | tf_op jit(solution)/shard_map/mv_px2/ppermute | solution.py:58
  28.1 5.4 %collective-permute-done.14.x_a = bf16[1024,256]{1,0:T(8,128)(2,1)S(1)} collective-permute-done((bf16[1024,256]{1,0:T(8,128)(2,1)S(1)}, bf16[1024,256]{1,0:T(8,128)(2,1)S(1)}, u32[]{:S(2)}, u32[]{:S(2)}) %collective-permute-start.14) | collective-permute-done | bytes 524320 | tf_op jit(solution)/shard_map/mv_px1/ppermute | solution.py:58
  36.4 2.2 %collective-permute-start.16 = (bf16[256,1024]{1,0:T(8,128)(2,1)S(1)}, bf16[256,1024]{1,0:T(8,128)(2,1)S(1)}, u32[]{:S(2)}, u32[]{:S(2)}) collective-permute-start(bf16[256,1024]{1,0:T(8,128)(2,1)S(1)} %get-tuple-element.30), channel_id=1, source_target_pairs={{0,1},{1,0},{2,3},{3,2},{4,5},{5,4},{6,7},{7,6},{8,9},{9,8},{10,11... | collective-permute-start | bytes 1572872 | tf_op jit(solution)/shard_map/mv_yy1/ppermute | solution.py:58
  38.9 3.7 %collective-permute-start.20 = (bf16[256,1024]{1,0:T(8,128)(2,1)S(1)}, bf16[256,1024]{1,0:T(8,128)(2,1)S(1)}, u32[]{:S(2)}, u32[]{:S(2)}) collective-permute-start(bf16[256,1024]{1,0:T(8,128)(2,1)S(1)} %shard_map.84), channel_id=1, source_target_pairs={{0,8},{1,9},{2,10},{3,11},{4,12},{5,13},{6,14},{7,15},{24,16},{25,... | collective-permute-start | bytes 1572872 | tf_op jit(solution)/shard_map/mv_za0/ppermute | solution.py:64
  42.6 1.6 %collective-permute-start.7 = (bf16[1024,256]{1,0:T(8,128)(2,1)S(1)}, bf16[1024,256]{1,0:T(8,128)(2,1)S(1)}, u32[]{:S(2)}, u32[]{:S(2)}) collective-permute-start(bf16[1024,256]{1,0:T(8,128)(2,1)S(1)} %get-tuple-element.22), channel_id=1, source_target_pairs={{0,4},{1,5},{2,6},{3,7},{4,0},{5,1},{6,2},{7,3},{8,12},{9,13},{10,... | collective-permute-start | bytes 1572872 | tf_op jit(solution)/shard_map/mv_px3/ppermute | solution.py:58
  44.3 1.5 %collective-permute-done.11.xc_a = bf16[512,256]{1,0:T(8,128)(2,1)S(1)} collective-permute-done((bf16[512,256]{1,0:T(8,128)(2,1)S(1)}, bf16[512,256]{1,0:T(8,128)(2,1)S(1)}, u32[]{:S(2)}, u32[]{:S(2)}) %collective-permute-start.11) | collective-permute-done | bytes 262176 | tf_op jit(solution)/shard_map/mv_pr2/ppermute | solution.py:58
  47.1 1.6 %collective-permute-start.12 = (bf16[256,1024]{1,0:T(8,128)(2,1)S(1)}, bf16[256,1024]{1,0:T(8,128)(2,1)S(1)}, u32[]{:S(2)}, u32[]{:S(2)}) collective-permute-start(bf16[256,1024]{1,0:T(8,128)(2,1)S(1)} %get-tuple-element.26), channel_id=1, source_target_pairs={{0,1},{1,0},{2,3},{3,2},{4,5},{5,4},{6,7},{7,6},{8,9},{9,8},{10,11... | collective-permute-start | bytes 1572872 | tf_op jit(solution)/shard_map/mv_yy2/ppermute | solution.py:58
  48.7 2.5 %collective-permute-done.16.refs_1_ = bf16[256,1024]{1,0:T(8,128)(2,1)S(1)} collective-permute-done((bf16[256,1024]{1,0:T(8,128)(2,1)S(1)}, bf16[256,1024]{1,0:T(8,128)(2,1)S(1)}, u32[]{:S(2)}, u32[]{:S(2)}) %collective-permute-start.16) | collective-permute-done | bytes 524320 | tf_op jit(solution)/shard_map/mv_yy1/ppermute | solution.py:58
  51.3 3.2 %collective-permute-start.23 = (bf16[272,1024]{1,0:T(8,128)(2,1)S(1)}, bf16[272,1024]{1,0:T(8,128)(2,1)S(1)}, u32[]{:S(2)}, u32[]{:S(2)}) collective-permute-start(bf16[272,1024]{1,0:T(8,128)(2,1)S(1)} %shard_map.88), channel_id=1, source_target_pairs={{0,8},{1,9},{2,10},{3,11},{4,12},{5,13},{6,14},{7,15},{24,16},{25,... | collective-permute-start | bytes 1671176 | tf_op jit(solution)/shard_map/mv_za1/ppermute | solution.py:64
  55.7 1.6 %collective-permute-start.1 = (bf16[512,256]{1,0:T(8,128)(2,1)S(1)}, bf16[512,256]{1,0:T(8,128)(2,1)S(1)}, u32[]{:S(2)}, u32[]{:S(2)}) collective-permute-start(bf16[512,256]{1,0:T(8,128)(2,1)S(1)} %get-tuple-element.21), channel_id=1, source_target_pairs={{0,4},{1,5},{2,6},{3,7},{4,0},{5,1},{6,2},{7,3},{8,12},{9,13},{10,... | collective-permute-start | bytes 786440 | tf_op jit(solution)/shard_map/mv_px4/ppermute | solution.py:58
  58.6 1.5 %collective-permute-start.9 = (bf16[256,1024]{1,0:T(8,128)(2,1)S(1)}, bf16[256,1024]{1,0:T(8,128)(2,1)S(1)}, u32[]{:S(2)}, u32[]{:S(2)}) collective-permute-start(bf16[256,1024]{1,0:T(8,128)(2,1)S(1)} %get-tuple-element.23), channel_id=1, source_target_pairs={{0,1},{1,0},{2,3},{3,2},{4,5},{5,4},{6,7},{7,6},{8,9},{9,8},{10,11... | collective-permute-start | bytes 1572872 | tf_op jit(solution)/shard_map/mv_yy3/ppermute | solution.py:58
  60.1 2.4 %collective-permute-done.12.refs_1_ = bf16[256,1024]{1,0:T(8,128)(2,1)S(1)} collective-permute-done((bf16[256,1024]{1,0:T(8,128)(2,1)S(1)}, bf16[256,1024]{1,0:T(8,128)(2,1)S(1)}, u32[]{:S(2)}, u32[]{:S(2)}) %collective-permute-start.12) | collective-permute-done | bytes 524320 | tf_op jit(solution)/shard_map/mv_yy2/ppermute | solution.py:58
  62.7 7.6 %collective-permute-start.22 = (bf16[256,1024]{1,0:T(8,128)(2,1)S(1)}, bf16[256,1024]{1,0:T(8,128)(2,1)S(1)}, u32[]{:S(2)}, u32[]{:S(2)}) collective-permute-start(bf16[256,1024]{1,0:T(8,128)(2,1)S(1)} %shard_map.86), channel_id=1, source_target_pairs={{0,8},{1,9},{2,10},{3,11},{4,12},{5,13},{6,14},{7,15},{8,0},{9,1},... | collective-permute-start | bytes 1572872 | tf_op jit(solution)/shard_map/mv_za2/ppermute | solution.py:64
  71.3 1.3 %collective-permute-done.2.xc_a = bf16[256,256]{1,0:T(8,128)(2,1)S(1)} collective-permute-done((bf16[256,256]{1,0:T(8,128)(2,1)S(1)}, bf16[256,256]{1,0:T(8,128)(2,1)S(1)}, u32[]{:S(2)}, u32[]{:S(2)}) %collective-permute-start.2) | collective-permute-done | bytes 131104 | tf_op jit(solution)/shard_map/mv_pr4/ppermute | solution.py:58
  73.5 6.4 %collective-permute-done.22.refs_1_ = bf16[256,1024]{1,0:T(8,128)(2,1)S(1)} collective-permute-done((bf16[256,1024]{1,0:T(8,128)(2,1)S(1)}, bf16[256,1024]{1,0:T(8,128)(2,1)S(1)}, u32[]{:S(2)}, u32[]{:S(2)}) %collective-permute-start.22) | collective-permute-done | bytes 524320 | tf_op jit(solution)/shard_map/mv_za2/ppermute | solution.py:64
  80.2 13.8 %all_to_all.5.squares = f32[32,1,128]{2,1,0:T(1,128)S(1)} all-to-all(f32[32,1,128]{2,1,0:T(1,128)S(1)} %get-tuple-element.33), channel_id=1, replica_groups=mesh['replica'=16,'shard'=2] {'replica','shard'}, dimensions={0} | all-to-all | bytes 32768 | tf_op jit(solution)/shard_map/squares/all_to_all | solution.py:344
  94.0 2.2 %shard_map.91 = (f32[256,1024]{1,0:T(8,128)}, f32[256,1024]{1,0:T(8,128)}, f32[256,1024]{1,0:T(8,128)}) custom-call(f32[32,1,128]{2,1,0:T(1,128)S(1)} %all_to_all.5.squares, f32[256,1024]{1,0:T(8,128)S(1)} %get-tuple-element.34.grad, f32[256,1024]{1,0:T(8,128)S(1)} %copy-done.2, f32[256,1024]{1,0:T(8,128)S(1)} %copy-done.3, f32[256,1024]{1,0:T(8,128)S(1)} %copy-done.4), custom_call_target="tpu_custom_call" | custom-call | tf_op jit(solution)/shard_map/pallas_call | solution.py:240
  (62 shorter events, 13.5 us)
Async XLA Ops:
  0.6 16.0 %collective-permute-start.4 = (bf16[256,1024]{1,0:T(8,128)(2,1)}, bf16[256,1024]{1,0:T(8,128)(2,1)S(1)}, u32[]{:S(2)}, u32[]{:S(2)}) collective-permute-start(bf16[256,1024]{1,0:T(8,128)(2,1)} %b0.9), channel_id=1, source_target_pairs={{0,4},{1,5},{2,6},{3,7},{4,0},{5,1},{6,2},{7,3},{8,12},{9,13},{10,... | collective-permute-start | bytes 1572872 | tf_op jit(solution)/shard_map/mv_bx/ppermute | solution.py:58
  9.2 1.8 %collective-permute-start.13 = (bf16[768,256]{1,0:T(8,128)(2,1)S(1)}, bf16[768,256]{1,0:T(8,128)(2,1)S(1)}, u32[]{:S(2)}, u32[]{:S(2)}) collective-permute-start(bf16[768,256]{1,0:T(8,128)(2,1)S(1)} %slice.33), channel_id=1, source_target_pairs={{0,2},{1,3},{2,0},{3,1},{4,6},{5,7},{6,4},{7,5},{8,10},{9,11},{10,... | collective-permute-start | bytes 1179656 | tf_op jit(solution)/shard_map/mv_own0/ppermute | solution.py:58
  9.3 14.3 %collective-permute-start.3 = (bf16[256,1024]{1,0:T(8,128)(2,1)S(1)}, bf16[256,1024]{1,0:T(8,128)(2,1)S(1)}, u32[]{:S(2)}, u32[]{:S(2)}) collective-permute-start(bf16[256,1024]{1,0:T(8,128)(2,1)S(1)} %copy-done), channel_id=1, source_target_pairs={{0,2},{1,3},{2,0},{3,1},{4,6},{5,7},{6,4},{7,5},{8,10},{9,11},{10,... | collective-permute-start | bytes 1572872 | tf_op jit(solution)/shard_map/mv_bc/ppermute | solution.py:58
  9.8 12.4 %collective-permute-start.17 = (bf16[512,256]{1,0:T(8,128)(2,1)S(1)}, bf16[512,256]{1,0:T(8,128)(2,1)S(1)}, u32[]{:S(2)}, u32[]{:S(2)}) collective-permute-start(bf16[512,256]{1,0:T(8,128)(2,1)S(1)} %get-tuple-element.32), channel_id=1, source_target_pairs={{0,4},{1,5},{2,6},{3,7},{4,0},{5,1},{6,2},{7,3},{8,12},{9,13},{10,... | collective-permute-start | bytes 786440 | tf_op jit(solution)/shard_map/mv_px0/ppermute | solution.py:58
  11.0 22.4 %collective-permute-start.14 = (bf16[1024,256]{1,0:T(8,128)(2,1)S(1)}, bf16[1024,256]{1,0:T(8,128)(2,1)S(1)}, u32[]{:S(2)}, u32[]{:S(2)}) collective-permute-start(bf16[1024,256]{1,0:T(8,128)(2,1)S(1)} %get-tuple-element.29), channel_id=1, source_target_pairs={{0,4},{1,5},{2,6},{3,7},{4,0},{5,1},{6,2},{7,3},{8,12},{9,13},{10,... | collective-permute-start | bytes 1572872 | tf_op jit(solution)/shard_map/mv_px1/ppermute | solution.py:58
  16.6 7.0 %collective-permute-start.5 = (bf16[256,512]{1,0:T(8,128)(2,1)S(1)}, bf16[256,512]{1,0:T(8,128)(2,1)S(1)}, u32[]{:S(2)}, u32[]{:S(2)}) collective-permute-start(bf16[256,512]{1,0:T(8,128)(2,1)S(1)} %get-tuple-element.36), channel_id=1, source_target_pairs={{0,2},{1,3},{2,0},{3,1},{4,6},{5,7},{6,4},{7,5},{8,10},{9,11},{10,... | collective-permute-start | bytes 786440 | tf_op jit(solution)/shard_map/mv_br0/ppermute | solution.py:58
  16.7 6.9 %collective-permute-start.6 = (bf16[256,512]{1,0:T(8,128)(2,1)S(1)}, bf16[256,512]{1,0:T(8,128)(2,1)S(1)}, u32[]{:S(2)}, u32[]{:S(2)}) collective-permute-start(bf16[256,512]{1,0:T(8,128)(2,1)S(1)} %get-tuple-element.35), channel_id=1, source_target_pairs={{0,2},{1,3},{2,0},{3,1},{4,6},{5,7},{6,4},{7,5},{8,10},{9,11},{10,... | collective-permute-start | bytes 786440 | tf_op jit(solution)/shard_map/mv_br1/ppermute | solution.py:58
  24.4 14.4 %collective-permute-start.19 = (bf16[256,1024]{1,0:T(8,128)(2,1)S(1)}, bf16[256,1024]{1,0:T(8,128)(2,1)S(1)}, u32[]{:S(2)}, u32[]{:S(2)}) collective-permute-start(bf16[256,1024]{1,0:T(8,128)(2,1)S(1)} %shard_map.83), channel_id=1, source_target_pairs={{0,1},{1,0},{2,3},{3,2},{4,5},{5,4},{6,7},{7,6},{8,9},{9,8},{10,11... | collective-permute-start | bytes 1572872 | tf_op jit(solution)/shard_map/mv_yy0/ppermute | solution.py:58
  26.6 17.6 %collective-permute-start.10 = (bf16[1024,256]{1,0:T(8,128)(2,1)S(1)}, bf16[1024,256]{1,0:T(8,128)(2,1)S(1)}, u32[]{:S(2)}, u32[]{:S(2)}) collective-permute-start(bf16[1024,256]{1,0:T(8,128)(2,1)S(1)} %get-tuple-element.25), channel_id=1, source_target_pairs={{0,4},{1,5},{2,6},{3,7},{4,0},{5,1},{6,2},{7,3},{8,12},{9,13},{10,... | collective-permute-start | bytes 1572872 | tf_op jit(solution)/shard_map/mv_px2/ppermute | solution.py:58
  33.5 1.6 %collective-permute-start.15 = (bf16[512,256]{1,0:T(8,128)(2,1)S(1)}, bf16[512,256]{1,0:T(8,128)(2,1)S(1)}, u32[]{:S(2)}, u32[]{:S(2)}) collective-permute-start(bf16[512,256]{1,0:T(8,128)(2,1)S(1)} %slice.41), channel_id=1, source_target_pairs={{0,2},{1,3},{2,0},{3,1},{4,6},{5,7},{6,4},{7,5},{8,10},{9,11},{10,... | collective-permute-start | bytes 786440 | tf_op jit(solution)/shard_map/mv_pr1/ppermute | solution.py:58
  33.6 10.7 %collective-permute-start = (bf16[1280,256]{1,0:T(8,128)(2,1)S(1)}, bf16[1280,256]{1,0:T(8,128)(2,1)S(1)}, u32[]{:S(2)}, u32[]{:S(2)}) collective-permute-start(bf16[1280,256]{1,0:T(8,128)(2,1)S(1)} %slice.27), channel_id=1, source_target_pairs={{0,2},{1,3},{2,0},{3,1},{4,6},{5,7},{6,4},{7,5},{8,10},{9,11},{10,... | collective-permute-start | bytes 1966088 | tf_op jit(solution)/shard_map/mv_own1/ppermute | solution.py:58
  36.4 14.9 %collective-permute-start.16 = (bf16[256,1024]{1,0:T(8,128)(2,1)S(1)}, bf16[256,1024]{1,0:T(8,128)(2,1)S(1)}, u32[]{:S(2)}, u32[]{:S(2)}) collective-permute-start(bf16[256,1024]{1,0:T(8,128)(2,1)S(1)} %get-tuple-element.30), channel_id=1, source_target_pairs={{0,1},{1,0},{2,3},{3,2},{4,5},{5,4},{6,7},{7,6},{8,9},{9,8},{10,11... | collective-permute-start | bytes 1572872 | tf_op jit(solution)/shard_map/mv_yy1/ppermute | solution.py:58
  38.9 15.7 %collective-permute-start.20 = (bf16[256,1024]{1,0:T(8,128)(2,1)S(1)}, bf16[256,1024]{1,0:T(8,128)(2,1)S(1)}, u32[]{:S(2)}, u32[]{:S(2)}) collective-permute-start(bf16[256,1024]{1,0:T(8,128)(2,1)S(1)} %shard_map.84), channel_id=1, source_target_pairs={{0,8},{1,9},{2,10},{3,11},{4,12},{5,13},{6,14},{7,15},{24,16},{25,... | collective-permute-start | bytes 1572872 | tf_op jit(solution)/shard_map/mv_za0/ppermute | solution.py:64
  42.6 13.0 %collective-permute-start.7 = (bf16[1024,256]{1,0:T(8,128)(2,1)S(1)}, bf16[1024,256]{1,0:T(8,128)(2,1)S(1)}, u32[]{:S(2)}, u32[]{:S(2)}) collective-permute-start(bf16[1024,256]{1,0:T(8,128)(2,1)S(1)} %get-tuple-element.22), channel_id=1, source_target_pairs={{0,4},{1,5},{2,6},{3,7},{4,0},{5,1},{6,2},{7,3},{8,12},{9,13},{10,... | collective-permute-start | bytes 1572872 | tf_op jit(solution)/shard_map/mv_px3/ppermute | solution.py:58
  44.2 1.6 %collective-permute-start.11 = (bf16[512,256]{1,0:T(8,128)(2,1)S(1)}, bf16[512,256]{1,0:T(8,128)(2,1)S(1)}, u32[]{:S(2)}, u32[]{:S(2)}) collective-permute-start(bf16[512,256]{1,0:T(8,128)(2,1)S(1)} %slice.40), channel_id=1, source_target_pairs={{0,2},{1,3},{2,0},{3,1},{4,6},{5,7},{6,4},{7,5},{8,10},{9,11},{10,... | collective-permute-start | bytes 786440 | tf_op jit(solution)/shard_map/mv_pr2/ppermute | solution.py:58
  47.1 15.4 %collective-permute-start.12 = (bf16[256,1024]{1,0:T(8,128)(2,1)S(1)}, bf16[256,1024]{1,0:T(8,128)(2,1)S(1)}, u32[]{:S(2)}, u32[]{:S(2)}) collective-permute-start(bf16[256,1024]{1,0:T(8,128)(2,1)S(1)} %get-tuple-element.26), channel_id=1, source_target_pairs={{0,1},{1,0},{2,3},{3,2},{4,5},{5,4},{6,7},{7,6},{8,9},{9,8},{10,11... | collective-permute-start | bytes 1572872 | tf_op jit(solution)/shard_map/mv_yy2/ppermute | solution.py:58
  51.3 18.9 %collective-permute-start.23 = (bf16[272,1024]{1,0:T(8,128)(2,1)S(1)}, bf16[272,1024]{1,0:T(8,128)(2,1)S(1)}, u32[]{:S(2)}, u32[]{:S(2)}) collective-permute-start(bf16[272,1024]{1,0:T(8,128)(2,1)S(1)} %shard_map.88), channel_id=1, source_target_pairs={{0,8},{1,9},{2,10},{3,11},{4,12},{5,13},{6,14},{7,15},{24,16},{25,... | collective-permute-start | bytes 1671176 | tf_op jit(solution)/shard_map/mv_za1/ppermute | solution.py:64
  54.8 7.8 %collective-permute-start.21 = (bf16[256,1024]{1,0:T(8,128)(2,1)S(1)}, bf16[256,1024]{1,0:T(8,128)(2,1)S(1)}, u32[]{:S(2)}, u32[]{:S(2)}) collective-permute-start(bf16[256,1024]{1,0:T(8,128)(2,1)S(1)} %shard_map.85), channel_id=1, source_target_pairs={{8,16},{9,17},{10,18},{11,19},{12,20},{13,21},{14,22},{15,23},{16,... | collective-permute-start | bytes 1572872 | tf_op jit(solution)/shard_map/mv_zb1/ppermute | solution.py:64
  55.6 1.6 %collective-permute-start.8 = (bf16[512,256]{1,0:T(8,128)(2,1)S(1)}, bf16[512,256]{1,0:T(8,128)(2,1)S(1)}, u32[]{:S(2)}, u32[]{:S(2)}) collective-permute-start(bf16[512,256]{1,0:T(8,128)(2,1)S(1)} %slice.39), channel_id=1, source_target_pairs={{0,2},{1,3},{2,0},{3,1},{4,6},{5,7},{6,4},{7,5},{8,10},{9,11},{10,... | collective-permute-start | bytes 786440 | tf_op jit(solution)/shard_map/mv_pr3/ppermute | solution.py:58
  55.7 15.4 %collective-permute-start.1 = (bf16[512,256]{1,0:T(8,128)(2,1)S(1)}, bf16[512,256]{1,0:T(8,128)(2,1)S(1)}, u32[]{:S(2)}, u32[]{:S(2)}) collective-permute-start(bf16[512,256]{1,0:T(8,128)(2,1)S(1)} %get-tuple-element.21), channel_id=1, source_target_pairs={{0,4},{1,5},{2,6},{3,7},{4,0},{5,1},{6,2},{7,3},{8,12},{9,13},{10,... | collective-permute-start | bytes 786440 | tf_op jit(solution)/shard_map/mv_px4/ppermute | solution.py:58
  58.6 14.8 %collective-permute-start.9 = (bf16[256,1024]{1,0:T(8,128)(2,1)S(1)}, bf16[256,1024]{1,0:T(8,128)(2,1)S(1)}, u32[]{:S(2)}, u32[]{:S(2)}) collective-permute-start(bf16[256,1024]{1,0:T(8,128)(2,1)S(1)} %get-tuple-element.23), channel_id=1, source_target_pairs={{0,1},{1,0},{2,3},{3,2},{4,5},{5,4},{6,7},{7,6},{8,9},{9,8},{10,11... | collective-permute-start | bytes 1572872 | tf_op jit(solution)/shard_map/mv_yy3/ppermute | solution.py:58
  62.7 17.2 %collective-permute-start.22 = (bf16[256,1024]{1,0:T(8,128)(2,1)S(1)}, bf16[256,1024]{1,0:T(8,128)(2,1)S(1)}, u32[]{:S(2)}, u32[]{:S(2)}) collective-permute-start(bf16[256,1024]{1,0:T(8,128)(2,1)S(1)} %shard_map.86), channel_id=1, source_target_pairs={{0,8},{1,9},{2,10},{3,11},{4,12},{5,13},{6,14},{7,15},{8,0},{9,1},... | collective-permute-start | bytes 1572872 | tf_op jit(solution)/shard_map/mv_za2/ppermute | solution.py:64
  70.4 9.5 %collective-permute-start.24 = (bf16[256,1024]{1,0:T(8,128)(2,1)S(1)}, bf16[256,1024]{1,0:T(8,128)(2,1)S(1)}, u32[]{:S(2)}, u32[]{:S(2)}) collective-permute-start(bf16[256,1024]{1,0:T(8,128)(2,1)S(1)} %shard_map.89), channel_id=1, source_target_pairs={{8,16},{9,17},{10,18},{11,19},{12,20},{13,21},{14,22},{15,23},{16,... | collective-permute-start | bytes 1572872 | tf_op jit(solution)/shard_map/mv_zb2/ppermute | solution.py:64
  71.2 1.4 %collective-permute-start.2 = (bf16[256,256]{1,0:T(8,128)(2,1)S(1)}, bf16[256,256]{1,0:T(8,128)(2,1)S(1)}, u32[]{:S(2)}, u32[]{:S(2)}) collective-permute-start(bf16[256,256]{1,0:T(8,128)(2,1)S(1)} %slice.36), channel_id=1, source_target_pairs={{0,2},{1,3},{2,0},{3,1},{4,6},{5,7},{6,4},{7,5},{8,10},{9,11},{10,... | collective-permute-start | bytes 393224 | tf_op jit(solution)/shard_map/mv_pr4/ppermute | solution.py:58
  (6 other events, 74.3 us)

commit v4 on v3

--- a/solution.py
+++ b/solution.py
@@ -23,9 +23,9 @@
 )
 GATES = {"px1": ("own0",)}
 EXTRA = {}
-COST = {"add2": 560000000, "add3": 1680000000, "fin": 224000000, "kk4": 1959999999}
+COST = {"add2": 560000000, "add3": 1120000000, "kk4": 1959999999}
 CUT = 2
-SPARE = 16
+SPARE = 0
 LINE = {
     "za0": ("rr0", OUTER),
     "za1": ("rr1", OUTER),

time: 96.4 us -> 95.4 us (0.990)
  waiting for transfers between devices: 33.2 us -> 37.2 us
  blocking collectives: 13.8 us -> 11 us
  starting transfers between devices: 33.9 us -> 31.7 us
    ppermute x5, waiting for transfers between devices: 6.42 us -> 10.5 us  [along(): return lax.ppermute(values, AXES, pairs)]
    all_to_all x1, blocking collectives: 13.8 us -> 11 us  [shards(): squares = lax.all_to_all(squares, AXES, 0, 0)]
    ppermute x5, starting transfers between devices: 16 us -> 13.7 us  [along(): return lax.ppermute(values, AXES, pairs)]
  transfers between devices with their start and end apart: 25 -> 25, of which waited for: 13 -> 14; matrix products, arithmetic and copies ran while one was open for 0% -> 0% of each run, Pallas kernels for 10% -> 10%
where the time goes in v4:
time: 95.4 us; the launch traced here: 95.2 us
  waiting for transfers between devices  37.2 us (39%)
  starting transfers between devices  31.7 us (33%)
  Pallas kernels  11.9 us (12%)
  blocking collectives  11 us (12%)
  local copies, waits for them, and re-layouts  2.39 us (3%)
    ppermute x20, waiting for transfers between devices, flip(): return lax.ppermute(values, AXES, pairs)  26.7 us
    ppermute x20, starting transfers between devices, flip(): return lax.ppermute(values, AXES, pairs)  18 us
    ppermute x5, starting transfers between devices, along(): return lax.ppermute(values, AXES, pairs)  13.7 us
    all_to_all x1, blocking collectives, shards(): squares = lax.all_to_all(squares, AXES, 0, 0)  11 us
    ppermute x5, waiting for transfers between devices, along(): return lax.ppermute(values, AXES, pairs)  10.5 us
    pallas_call x5, Pallas kernels, product(): pl.pallas_call(functools.partial(product_kernel, offset, core_offset, sta...  5.34 us
    pallas_call x1, Pallas kernels, pack(): pl.pallas_call(functools.partial(pack_kernel, chunks, n_shard, own), out_...  3.28 us
    unnamed x10, local copies, waits for them, and re-layouts  2.21 us
  transfers between devices with their start and end apart: 25, of which 14 were waited for; matrix products, arithmetic and copies ran while one was open for 0% of the time, Pallas kernels for 10%

profile of v4, /device:TPU:0, one launch (start us, length us, event | category | flops | bytes accessed | tf_op | source)
XLA Modules:
  0.0 95.2 jit_solution(4297446745897626206)
XLA Ops:
  0.6 3.0 %collective-permute-start.4 = (bf16[256,1024]{1,0:T(8,128)(2,1)}, bf16[256,1024]{1,0:T(8,128)(2,1)S(1)}, u32[]{:S(2)}, u32[]{:S(2)}) collective-permute-start(bf16[256,1024]{1,0:T(8,128)(2,1)} %b0.9), channel_id=1, source_target_pairs={{0,4},{1,5},{2,6},{3,7},{4,0},{5,1},{6,2},{7,3},{8,12},{9,13},{10,... | collective-permute-start | bytes 1572872 | tf_op jit(solution)/shard_map/mv_bx/ppermute | solution.py:58
  3.7 2.2 %copy-done.1 = bf16[256,8192]{1,0:T(8,128)(2,1)S(1)} copy-done((bf16[256,8192]{1,0:T(8,128)(2,1)S(1)}, bf16[256,8192]{1,0:T(8,128)(2,1)}, u32[]{:S(2)}) %copy-start.1) | copy-done | bytes 4194328
  5.9 3.3 %shard_map.76 = (bf16[2048,256]{1,0:T(8,128)(2,1)S(1)}, bf16[2048,256]{1,0:T(8,128)(2,1)S(1)}, bf16[512,256]{1,0:T(8,128)(2,1)S(1)}, bf16[1024,256]{1,0:T(8,128)...) custom-call(s32[4]{0:T(128)S(1)} %pad_add_fusion.where, ...), custom_call_target="tpu_custom_call" | custom-call | bytes 8388608 | tf_op jit(solution)/shard_map/pallas_call | solution.py:111
  11.8 4.8 %collective-permute-done.4.b2 = bf16[256,1024]{1,0:T(8,128)(2,1)S(1)} collective-permute-done((bf16[256,1024]{1,0:T(8,128)(2,1)}, bf16[256,1024]{1,0:T(8,128)(2,1)S(1)}, u32[]{:S(2)}, u32[]{:S(2)}) %collective-permute-start.4) | collective-permute-done | bytes 524320 | tf_op jit(solution)/shard_map/mv_bx/ppermute | solution.py:58
  17.2 5.0 %collective-permute-done.17.x_a = bf16[512,256]{1,0:T(8,128)(2,1)S(1)} collective-permute-done((bf16[512,256]{1,0:T(8,128)(2,1)S(1)}, bf16[512,256]{1,0:T(8,128)(2,1)S(1)}, u32[]{:S(2)}, u32[]{:S(2)}) %collective-permute-start.17) | collective-permute-done | bytes 262176 | tf_op jit(solution)/shard_map/mv_px0/ppermute | solution.py:58
  22.3 1.3 %collective-permute-done.18.xc_a = bf16[256,256]{1,0:T(8,128)(2,1)S(1)} collective-permute-done((bf16[256,256]{1,0:T(8,128)(2,1)S(1)}, bf16[256,256]{1,0:T(8,128)(2,1)S(1)}, u32[]{:S(2)}, u32[]{:S(2)}) %collective-permute-start.18) | collective-permute-done | bytes 131104 | tf_op jit(solution)/shard_map/mv_pr0/ppermute | solution.py:58
  24.4 2.1 %collective-permute-start.19 = (bf16[256,1024]{1,0:T(8,128)(2,1)S(1)}, bf16[256,1024]{1,0:T(8,128)(2,1)S(1)}, u32[]{:S(2)}, u32[]{:S(2)}) collective-permute-start(bf16[256,1024]{1,0:T(8,128)(2,1)S(1)} %shard_map.83), channel_id=1, source_target_pairs={{0,1},{1,0},{2,3},{3,2},{4,5},{5,4},{6,7},{7,6},{8,9},{9,8},{10,11... | collective-permute-start | bytes 1572872 | tf_op jit(solution)/shard_map/mv_yy0/ppermute | solution.py:58
  26.6 1.5 %collective-permute-start.10 = (bf16[1024,256]{1,0:T(8,128)(2,1)S(1)}, bf16[1024,256]{1,0:T(8,128)(2,1)S(1)}, u32[]{:S(2)}, u32[]{:S(2)}) collective-permute-start(bf16[1024,256]{1,0:T(8,128)(2,1)S(1)} %get-tuple-element.25), channel_id=1, source_target_pairs={{0,4},{1,5},{2,6},{3,7},{4,0},{5,1},{6,2},{7,3},{8,12},{9,13},{10,... | collective-permute-start | bytes 1572872 | tf_op jit(solution)/shard_map/mv_px2/ppermute | solution.py:58
  28.1 5.4 %collective-permute-done.14.x_a = bf16[1024,256]{1,0:T(8,128)(2,1)S(1)} collective-permute-done((bf16[1024,256]{1,0:T(8,128)(2,1)S(1)}, bf16[1024,256]{1,0:T(8,128)(2,1)S(1)}, u32[]{:S(2)}, u32[]{:S(2)}) %collective-permute-start.14) | collective-permute-done | bytes 524320 | tf_op jit(solution)/shard_map/mv_px1/ppermute | solution.py:58
  36.4 2.2 %collective-permute-start.16 = (bf16[256,1024]{1,0:T(8,128)(2,1)S(1)}, bf16[256,1024]{1,0:T(8,128)(2,1)S(1)}, u32[]{:S(2)}, u32[]{:S(2)}) collective-permute-start(bf16[256,1024]{1,0:T(8,128)(2,1)S(1)} %get-tuple-element.30), channel_id=1, source_target_pairs={{0,1},{1,0},{2,3},{3,2},{4,5},{5,4},{6,7},{7,6},{8,9},{9,8},{10,11... | collective-permute-start | bytes 1572872 | tf_op jit(solution)/shard_map/mv_yy1/ppermute | solution.py:58
  38.9 3.7 %collective-permute-start.20 = (bf16[256,1024]{1,0:T(8,128)(2,1)S(1)}, bf16[256,1024]{1,0:T(8,128)(2,1)S(1)}, u32[]{:S(2)}, u32[]{:S(2)}) collective-permute-start(bf16[256,1024]{1,0:T(8,128)(2,1)S(1)} %shard_map.84), channel_id=1, source_target_pairs={{0,8},{1,9},{2,10},{3,11},{4,12},{5,13},{6,14},{7,15},{24,16},{25,... | collective-permute-start | bytes 1572872 | tf_op jit(solution)/shard_map/mv_za0/ppermute | solution.py:64
  42.7 1.6 %collective-permute-start.7 = (bf16[1024,256]{1,0:T(8,128)(2,1)S(1)}, bf16[1024,256]{1,0:T(8,128)(2,1)S(1)}, u32[]{:S(2)}, u32[]{:S(2)}) collective-permute-start(bf16[1024,256]{1,0:T(8,128)(2,1)S(1)} %get-tuple-element.22), channel_id=1, source_target_pairs={{0,4},{1,5},{2,6},{3,7},{4,0},{5,1},{6,2},{7,3},{8,12},{9,13},{10,... | collective-permute-start | bytes 1572872 | tf_op jit(solution)/shard_map/mv_px3/ppermute | solution.py:58
  44.3 1.5 %collective-permute-done.11.xc_a = bf16[512,256]{1,0:T(8,128)(2,1)S(1)} collective-permute-done((bf16[512,256]{1,0:T(8,128)(2,1)S(1)}, bf16[512,256]{1,0:T(8,128)(2,1)S(1)}, u32[]{:S(2)}, u32[]{:S(2)}) %collective-permute-start.11) | collective-permute-done | bytes 262176 | tf_op jit(solution)/shard_map/mv_pr2/ppermute | solution.py:58
  47.2 1.6 %collective-permute-start.12 = (bf16[256,1024]{1,0:T(8,128)(2,1)S(1)}, bf16[256,1024]{1,0:T(8,128)(2,1)S(1)}, u32[]{:S(2)}, u32[]{:S(2)}) collective-permute-start(bf16[256,1024]{1,0:T(8,128)(2,1)S(1)} %get-tuple-element.26), channel_id=1, source_target_pairs={{0,1},{1,0},{2,3},{3,2},{4,5},{5,4},{6,7},{7,6},{8,9},{9,8},{10,11... | collective-permute-start | bytes 1572872 | tf_op jit(solution)/shard_map/mv_yy2/ppermute | solution.py:58
  48.7 2.5 %collective-permute-done.16.refs_1_ = bf16[256,1024]{1,0:T(8,128)(2,1)S(1)} collective-permute-done((bf16[256,1024]{1,0:T(8,128)(2,1)S(1)}, bf16[256,1024]{1,0:T(8,128)(2,1)S(1)}, u32[]{:S(2)}, u32[]{:S(2)}) %collective-permute-start.16) | collective-permute-done | bytes 524320 | tf_op jit(solution)/shard_map/mv_yy1/ppermute | solution.py:58
  51.3 3.2 %collective-permute-start.23 = (bf16[256,1024]{1,0:T(8,128)(2,1)S(1)}, bf16[256,1024]{1,0:T(8,128)(2,1)S(1)}, u32[]{:S(2)}, u32[]{:S(2)}) collective-permute-start(bf16[256,1024]{1,0:T(8,128)(2,1)S(1)} %shard_map.87), channel_id=1, source_target_pairs={{0,8},{1,9},{2,10},{3,11},{4,12},{5,13},{6,14},{7,15},{24,16},{25,... | collective-permute-start | bytes 1572872 | tf_op jit(solution)/shard_map/mv_za1/ppermute | solution.py:64
  55.8 1.6 %collective-permute-start.1 = (bf16[512,256]{1,0:T(8,128)(2,1)S(1)}, bf16[512,256]{1,0:T(8,128)(2,1)S(1)}, u32[]{:S(2)}, u32[]{:S(2)}) collective-permute-start(bf16[512,256]{1,0:T(8,128)(2,1)S(1)} %get-tuple-element.21), channel_id=1, source_target_pairs={{0,4},{1,5},{2,6},{3,7},{4,0},{5,1},{6,2},{7,3},{8,12},{9,13},{10,... | collective-permute-start | bytes 786440 | tf_op jit(solution)/shard_map/mv_px4/ppermute | solution.py:58
  58.6 1.5 %collective-permute-start.9 = (bf16[256,1024]{1,0:T(8,128)(2,1)S(1)}, bf16[256,1024]{1,0:T(8,128)(2,1)S(1)}, u32[]{:S(2)}, u32[]{:S(2)}) collective-permute-start(bf16[256,1024]{1,0:T(8,128)(2,1)S(1)} %get-tuple-element.23), channel_id=1, source_target_pairs={{0,1},{1,0},{2,3},{3,2},{4,5},{5,4},{6,7},{7,6},{8,9},{9,8},{10,11... | collective-permute-start | bytes 1572872 | tf_op jit(solution)/shard_map/mv_yy3/ppermute | solution.py:58
  60.2 2.3 %collective-permute-done.12.refs_1_ = bf16[256,1024]{1,0:T(8,128)(2,1)S(1)} collective-permute-done((bf16[256,1024]{1,0:T(8,128)(2,1)S(1)}, bf16[256,1024]{1,0:T(8,128)(2,1)S(1)}, u32[]{:S(2)}, u32[]{:S(2)}) %collective-permute-start.12) | collective-permute-done | bytes 524320 | tf_op jit(solution)/shard_map/mv_yy2/ppermute | solution.py:58
  62.6 2.6 %collective-permute-done.23.refs_2_ = bf16[256,1024]{1,0:T(8,128)(2,1)S(1)} collective-permute-done((bf16[256,1024]{1,0:T(8,128)(2,1)S(1)}, bf16[256,1024]{1,0:T(8,128)(2,1)S(1)}, u32[]{:S(2)}, u32[]{:S(2)}) %collective-permute-start.23) | collective-permute-done | bytes 524320 | tf_op jit(solution)/shard_map/mv_za1/ppermute | solution.py:64
  66.2 5.3 %collective-permute-start.22 = (bf16[256,1024]{1,0:T(8,128)(2,1)S(1)}, bf16[256,1024]{1,0:T(8,128)(2,1)S(1)}, u32[]{:S(2)}, u32[]{:S(2)}) collective-permute-start(bf16[256,1024]{1,0:T(8,128)(2,1)S(1)} %shard_map.86), channel_id=1, source_target_pairs={{0,8},{1,9},{2,10},{3,11},{4,12},{5,13},{6,14},{7,15},{8,0},{9,1},... | collective-permute-start | bytes 1572872 | tf_op jit(solution)/shard_map/mv_za2/ppermute | solution.py:64
  73.8 7.9 %collective-permute-done.22.refs_1_ = bf16[256,1024]{1,0:T(8,128)(2,1)S(1)} collective-permute-done((bf16[256,1024]{1,0:T(8,128)(2,1)S(1)}, bf16[256,1024]{1,0:T(8,128)(2,1)S(1)}, u32[]{:S(2)}, u32[]{:S(2)}) %collective-permute-start.22) | collective-permute-done | bytes 524320 | tf_op jit(solution)/shard_map/mv_za2/ppermute | solution.py:64
  81.9 11.0 %all_to_all.5.squares = f32[32,1,128]{2,1,0:T(1,128)S(1)} all-to-all(f32[32,1,128]{2,1,0:T(1,128)S(1)} %get-tuple-element.33), channel_id=1, replica_groups=mesh['replica'=16,'shard'=2] {'replica','shard'}, dimensions={0} | all-to-all | bytes 32768 | tf_op jit(solution)/shard_map/squares/all_to_all | solution.py:344
  92.9 2.2 %shard_map.90 = (f32[256,1024]{1,0:T(8,128)}, f32[256,1024]{1,0:T(8,128)}, f32[256,1024]{1,0:T(8,128)}) custom-call(f32[32,1,128]{2,1,0:T(1,128)S(1)} %all_to_all.5.squares, f32[256,1024]{1,0:T(8,128)S(1)} %get-tuple-element.34.grad, f32[256,1024]{1,0:T(8,128)S(1)} %copy-done.2, f32[256,1024]{1,0:T(8,128)S(1)} %copy-done.3, f32[256,1024]{1,0:T(8,128)S(1)} %copy-done.4), custom_call_target="tpu_custom_call" | custom-call | tf_op jit(solution)/shard_map/pallas_call | solution.py:240
  (61 shorter events, 14.9 us)
Async XLA Ops:
  0.6 16.0 %collective-permute-start.4 = (bf16[256,1024]{1,0:T(8,128)(2,1)}, bf16[256,1024]{1,0:T(8,128)(2,1)S(1)}, u32[]{:S(2)}, u32[]{:S(2)}) collective-permute-start(bf16[256,1024]{1,0:T(8,128)(2,1)} %b0.9), channel_id=1, source_target_pairs={{0,4},{1,5},{2,6},{3,7},{4,0},{5,1},{6,2},{7,3},{8,12},{9,13},{10,... | collective-permute-start | bytes 1572872 | tf_op jit(solution)/shard_map/mv_bx/ppermute | solution.py:58
  9.2 1.8 %collective-permute-start.13 = (bf16[768,256]{1,0:T(8,128)(2,1)S(1)}, bf16[768,256]{1,0:T(8,128)(2,1)S(1)}, u32[]{:S(2)}, u32[]{:S(2)}) collective-permute-start(bf16[768,256]{1,0:T(8,128)(2,1)S(1)} %slice.33), channel_id=1, source_target_pairs={{0,2},{1,3},{2,0},{3,1},{4,6},{5,7},{6,4},{7,5},{8,10},{9,11},{10,... | collective-permute-start | bytes 1179656 | tf_op jit(solution)/shard_map/mv_own0/ppermute | solution.py:58
  9.3 14.3 %collective-permute-start.3 = (bf16[256,1024]{1,0:T(8,128)(2,1)S(1)}, bf16[256,1024]{1,0:T(8,128)(2,1)S(1)}, u32[]{:S(2)}, u32[]{:S(2)}) collective-permute-start(bf16[256,1024]{1,0:T(8,128)(2,1)S(1)} %copy-done), channel_id=1, source_target_pairs={{0,2},{1,3},{2,0},{3,1},{4,6},{5,7},{6,4},{7,5},{8,10},{9,11},{10,... | collective-permute-start | bytes 1572872 | tf_op jit(solution)/shard_map/mv_bc/ppermute | solution.py:58
  9.8 12.4 %collective-permute-start.17 = (bf16[512,256]{1,0:T(8,128)(2,1)S(1)}, bf16[512,256]{1,0:T(8,128)(2,1)S(1)}, u32[]{:S(2)}, u32[]{:S(2)}) collective-permute-start(bf16[512,256]{1,0:T(8,128)(2,1)S(1)} %get-tuple-element.32), channel_id=1, source_target_pairs={{0,4},{1,5},{2,6},{3,7},{4,0},{5,1},{6,2},{7,3},{8,12},{9,13},{10,... | collective-permute-start | bytes 786440 | tf_op jit(solution)/shard_map/mv_px0/ppermute | solution.py:58
  11.0 22.4 %collective-permute-start.14 = (bf16[1024,256]{1,0:T(8,128)(2,1)S(1)}, bf16[1024,256]{1,0:T(8,128)(2,1)S(1)}, u32[]{:S(2)}, u32[]{:S(2)}) collective-permute-start(bf16[1024,256]{1,0:T(8,128)(2,1)S(1)} %get-tuple-element.29), channel_id=1, source_target_pairs={{0,4},{1,5},{2,6},{3,7},{4,0},{5,1},{6,2},{7,3},{8,12},{9,13},{10,... | collective-permute-start | bytes 1572872 | tf_op jit(solution)/shard_map/mv_px1/ppermute | solution.py:58
  16.6 7.0 %collective-permute-start.5 = (bf16[256,512]{1,0:T(8,128)(2,1)S(1)}, bf16[256,512]{1,0:T(8,128)(2,1)S(1)}, u32[]{:S(2)}, u32[]{:S(2)}) collective-permute-start(bf16[256,512]{1,0:T(8,128)(2,1)S(1)} %get-tuple-element.36), channel_id=1, source_target_pairs={{0,2},{1,3},{2,0},{3,1},{4,6},{5,7},{6,4},{7,5},{8,10},{9,11},{10,... | collective-permute-start | bytes 786440 | tf_op jit(solution)/shard_map/mv_br0/ppermute | solution.py:58
  16.7 6.9 %collective-permute-start.6 = (bf16[256,512]{1,0:T(8,128)(2,1)S(1)}, bf16[256,512]{1,0:T(8,128)(2,1)S(1)}, u32[]{:S(2)}, u32[]{:S(2)}) collective-permute-start(bf16[256,512]{1,0:T(8,128)(2,1)S(1)} %get-tuple-element.35), channel_id=1, source_target_pairs={{0,2},{1,3},{2,0},{3,1},{4,6},{5,7},{6,4},{7,5},{8,10},{9,11},{10,... | collective-permute-start | bytes 786440 | tf_op jit(solution)/shard_map/mv_br1/ppermute | solution.py:58
  22.2 1.4 %collective-permute-start.18 = (bf16[256,256]{1,0:T(8,128)(2,1)S(1)}, bf16[256,256]{1,0:T(8,128)(2,1)S(1)}, u32[]{:S(2)}, u32[]{:S(2)}) collective-permute-start(bf16[256,256]{1,0:T(8,128)(2,1)S(1)} %slice.42), channel_id=1, source_target_pairs={{0,2},{1,3},{2,0},{3,1},{4,6},{5,7},{6,4},{7,5},{8,10},{9,11},{10,... | collective-permute-start | bytes 393224 | tf_op jit(solution)/shard_map/mv_pr0/ppermute | solution.py:58
  24.4 14.4 %collective-permute-start.19 = (bf16[256,1024]{1,0:T(8,128)(2,1)S(1)}, bf16[256,1024]{1,0:T(8,128)(2,1)S(1)}, u32[]{:S(2)}, u32[]{:S(2)}) collective-permute-start(bf16[256,1024]{1,0:T(8,128)(2,1)S(1)} %shard_map.83), channel_id=1, source_target_pairs={{0,1},{1,0},{2,3},{3,2},{4,5},{5,4},{6,7},{7,6},{8,9},{9,8},{10,11... | collective-permute-start | bytes 1572872 | tf_op jit(solution)/shard_map/mv_yy0/ppermute | solution.py:58
  26.6 17.7 %collective-permute-start.10 = (bf16[1024,256]{1,0:T(8,128)(2,1)S(1)}, bf16[1024,256]{1,0:T(8,128)(2,1)S(1)}, u32[]{:S(2)}, u32[]{:S(2)}) collective-permute-start(bf16[1024,256]{1,0:T(8,128)(2,1)S(1)} %get-tuple-element.25), channel_id=1, source_target_pairs={{0,4},{1,5},{2,6},{3,7},{4,0},{5,1},{6,2},{7,3},{8,12},{9,13},{10,... | collective-permute-start | bytes 1572872 | tf_op jit(solution)/shard_map/mv_px2/ppermute | solution.py:58
  33.5 1.6 %collective-permute-start.15 = (bf16[512,256]{1,0:T(8,128)(2,1)S(1)}, bf16[512,256]{1,0:T(8,128)(2,1)S(1)}, u32[]{:S(2)}, u32[]{:S(2)}) collective-permute-start(bf16[512,256]{1,0:T(8,128)(2,1)S(1)} %slice.41), channel_id=1, source_target_pairs={{0,2},{1,3},{2,0},{3,1},{4,6},{5,7},{6,4},{7,5},{8,10},{9,11},{10,... | collective-permute-start | bytes 786440 | tf_op jit(solution)/shard_map/mv_pr1/ppermute | solution.py:58
  33.6 10.7 %collective-permute-start = (bf16[1280,256]{1,0:T(8,128)(2,1)S(1)}, bf16[1280,256]{1,0:T(8,128)(2,1)S(1)}, u32[]{:S(2)}, u32[]{:S(2)}) collective-permute-start(bf16[1280,256]{1,0:T(8,128)(2,1)S(1)} %slice.27), channel_id=1, source_target_pairs={{0,2},{1,3},{2,0},{3,1},{4,6},{5,7},{6,4},{7,5},{8,10},{9,11},{10,... | collective-permute-start | bytes 1966088 | tf_op jit(solution)/shard_map/mv_own1/ppermute | solution.py:58
  36.4 14.9 %collective-permute-start.16 = (bf16[256,1024]{1,0:T(8,128)(2,1)S(1)}, bf16[256,1024]{1,0:T(8,128)(2,1)S(1)}, u32[]{:S(2)}, u32[]{:S(2)}) collective-permute-start(bf16[256,1024]{1,0:T(8,128)(2,1)S(1)} %get-tuple-element.30), channel_id=1, source_target_pairs={{0,1},{1,0},{2,3},{3,2},{4,5},{5,4},{6,7},{7,6},{8,9},{9,8},{10,11... | collective-permute-start | bytes 1572872 | tf_op jit(solution)/shard_map/mv_yy1/ppermute | solution.py:58
  38.9 15.7 %collective-permute-start.20 = (bf16[256,1024]{1,0:T(8,128)(2,1)S(1)}, bf16[256,1024]{1,0:T(8,128)(2,1)S(1)}, u32[]{:S(2)}, u32[]{:S(2)}) collective-permute-start(bf16[256,1024]{1,0:T(8,128)(2,1)S(1)} %shard_map.84), channel_id=1, source_target_pairs={{0,8},{1,9},{2,10},{3,11},{4,12},{5,13},{6,14},{7,15},{24,16},{25,... | collective-permute-start | bytes 1572872 | tf_op jit(solution)/shard_map/mv_za0/ppermute | solution.py:64
  42.7 13.0 %collective-permute-start.7 = (bf16[1024,256]{1,0:T(8,128)(2,1)S(1)}, bf16[1024,256]{1,0:T(8,128)(2,1)S(1)}, u32[]{:S(2)}, u32[]{:S(2)}) collective-permute-start(bf16[1024,256]{1,0:T(8,128)(2,1)S(1)} %get-tuple-element.22), channel_id=1, source_target_pairs={{0,4},{1,5},{2,6},{3,7},{4,0},{5,1},{6,2},{7,3},{8,12},{9,13},{10,... | collective-permute-start | bytes 1572872 | tf_op jit(solution)/shard_map/mv_px3/ppermute | solution.py:58
  44.3 1.6 %collective-permute-start.11 = (bf16[512,256]{1,0:T(8,128)(2,1)S(1)}, bf16[512,256]{1,0:T(8,128)(2,1)S(1)}, u32[]{:S(2)}, u32[]{:S(2)}) collective-permute-start(bf16[512,256]{1,0:T(8,128)(2,1)S(1)} %slice.40), channel_id=1, source_target_pairs={{0,2},{1,3},{2,0},{3,1},{4,6},{5,7},{6,4},{7,5},{8,10},{9,11},{10,... | collective-permute-start | bytes 786440 | tf_op jit(solution)/shard_map/mv_pr2/ppermute | solution.py:58
  47.2 15.3 %collective-permute-start.12 = (bf16[256,1024]{1,0:T(8,128)(2,1)S(1)}, bf16[256,1024]{1,0:T(8,128)(2,1)S(1)}, u32[]{:S(2)}, u32[]{:S(2)}) collective-permute-start(bf16[256,1024]{1,0:T(8,128)(2,1)S(1)} %get-tuple-element.26), channel_id=1, source_target_pairs={{0,1},{1,0},{2,3},{3,2},{4,5},{5,4},{6,7},{7,6},{8,9},{9,8},{10,11... | collective-permute-start | bytes 1572872 | tf_op jit(solution)/shard_map/mv_yy2/ppermute | solution.py:58
  51.3 13.9 %collective-permute-start.23 = (bf16[256,1024]{1,0:T(8,128)(2,1)S(1)}, bf16[256,1024]{1,0:T(8,128)(2,1)S(1)}, u32[]{:S(2)}, u32[]{:S(2)}) collective-permute-start(bf16[256,1024]{1,0:T(8,128)(2,1)S(1)} %shard_map.87), channel_id=1, source_target_pairs={{0,8},{1,9},{2,10},{3,11},{4,12},{5,13},{6,14},{7,15},{24,16},{25,... | collective-permute-start | bytes 1572872 | tf_op jit(solution)/shard_map/mv_za1/ppermute | solution.py:64
  54.8 11.3 %collective-permute-start.21 = (bf16[256,1024]{1,0:T(8,128)(2,1)S(1)}, bf16[256,1024]{1,0:T(8,128)(2,1)S(1)}, u32[]{:S(2)}, u32[]{:S(2)}) collective-permute-start(bf16[256,1024]{1,0:T(8,128)(2,1)S(1)} %shard_map.85), channel_id=1, source_target_pairs={{8,16},{9,17},{10,18},{11,19},{12,20},{13,21},{14,22},{15,23},{16,... | collective-permute-start | bytes 1572872 | tf_op jit(solution)/shard_map/mv_zb1/ppermute | solution.py:64
  55.7 1.6 %collective-permute-start.8 = (bf16[512,256]{1,0:T(8,128)(2,1)S(1)}, bf16[512,256]{1,0:T(8,128)(2,1)S(1)}, u32[]{:S(2)}, u32[]{:S(2)}) collective-permute-start(bf16[512,256]{1,0:T(8,128)(2,1)S(1)} %slice.39), channel_id=1, source_target_pairs={{0,2},{1,3},{2,0},{3,1},{4,6},{5,7},{6,4},{7,5},{8,10},{9,11},{10,... | collective-permute-start | bytes 786440 | tf_op jit(solution)/shard_map/mv_pr3/ppermute | solution.py:58
  55.8 15.7 %collective-permute-start.1 = (bf16[512,256]{1,0:T(8,128)(2,1)S(1)}, bf16[512,256]{1,0:T(8,128)(2,1)S(1)}, u32[]{:S(2)}, u32[]{:S(2)}) collective-permute-start(bf16[512,256]{1,0:T(8,128)(2,1)S(1)} %get-tuple-element.21), channel_id=1, source_target_pairs={{0,4},{1,5},{2,6},{3,7},{4,0},{5,1},{6,2},{7,3},{8,12},{9,13},{10,... | collective-permute-start | bytes 786440 | tf_op jit(solution)/shard_map/mv_px4/ppermute | solution.py:58
  58.6 15.1 %collective-permute-start.9 = (bf16[256,1024]{1,0:T(8,128)(2,1)S(1)}, bf16[256,1024]{1,0:T(8,128)(2,1)S(1)}, u32[]{:S(2)}, u32[]{:S(2)}) collective-permute-start(bf16[256,1024]{1,0:T(8,128)(2,1)S(1)} %get-tuple-element.23), channel_id=1, source_target_pairs={{0,1},{1,0},{2,3},{3,2},{4,5},{5,4},{6,7},{7,6},{8,9},{9,8},{10,11... | collective-permute-start | bytes 1572872 | tf_op jit(solution)/shard_map/mv_yy3/ppermute | solution.py:58
  65.4 8.5 %collective-permute-start.24 = (bf16[256,1024]{1,0:T(8,128)(2,1)S(1)}, bf16[256,1024]{1,0:T(8,128)(2,1)S(1)}, u32[]{:S(2)}, u32[]{:S(2)}) collective-permute-start(bf16[256,1024]{1,0:T(8,128)(2,1)S(1)} %shard_map.88), channel_id=1, source_target_pairs={{8,16},{9,17},{10,18},{11,19},{12,20},{13,21},{14,22},{15,23},{16,... | collective-permute-start | bytes 1572872 | tf_op jit(solution)/shard_map/mv_zb2/ppermute | solution.py:64
  66.2 15.5 %collective-permute-start.22 = (bf16[256,1024]{1,0:T(8,128)(2,1)S(1)}, bf16[256,1024]{1,0:T(8,128)(2,1)S(1)}, u32[]{:S(2)}, u32[]{:S(2)}) collective-permute-start(bf16[256,1024]{1,0:T(8,128)(2,1)S(1)} %shard_map.86), channel_id=1, source_target_pairs={{0,8},{1,9},{2,10},{3,11},{4,12},{5,13},{6,14},{7,15},{8,0},{9,1},... | collective-permute-start | bytes 1572872 | tf_op jit(solution)/shard_map/mv_za2/ppermute | solution.py:64
  (6 other events, 70.0 us)

commit v5 on v4

--- a/solution.py
+++ b/solution.py
@@ -127,7 +127,7 @@
     n_out = (stay > 0) + (leave > 0)
     extra, outs = refs[: len(refs) - n_out], refs[len(refs) - n_out :]
     cut = b3.shape[1]
-    tile = 256
+    tile = 512
     work = []
     if leave:
         work.append((stay, leave, outs[0], ()))

time: 95.4 us -> 95.4 us (level)
  no operation moved by 1% of the time
where the time goes in v5:
time: 95.4 us; the launch traced here: 95.2 us
  waiting for transfers between devices  37.2 us (39%)
  starting transfers between devices  31.6 us (33%)
  Pallas kernels  12 us (13%)
  blocking collectives  11 us (12%)
  local copies, waits for them, and re-layouts  2.39 us (3%)
    ppermute x20, waiting for transfers between devices, flip(): return lax.ppermute(values, AXES, pairs)  26.7 us
    ppermute x20, starting transfers between devices, flip(): return lax.ppermute(values, AXES, pairs)  17.9 us
    ppermute x5, starting transfers between devices, along(): return lax.ppermute(values, AXES, pairs)  13.7 us
    all_to_all x1, blocking collectives, shards(): squares = lax.all_to_all(squares, AXES, 0, 0)  11 us
    ppermute x5, waiting for transfers between devices, along(): return lax.ppermute(values, AXES, pairs)  10.5 us
    pallas_call x5, Pallas kernels, product(): pl.pallas_call(functools.partial(product_kernel, offset, core_offset, sta...  5.41 us
    pallas_call x1, Pallas kernels, pack(): pl.pallas_call(functools.partial(pack_kernel, chunks, n_shard, own), out_...  3.28 us
    unnamed x10, local copies, waits for them, and re-layouts  2.21 us
  transfers between devices with their start and end apart: 25, of which 14 were waited for; matrix products, arithmetic and copies ran while one was open for 0% of the time, Pallas kernels for 10%

profile of v5, /device:TPU:0, one launch (start us, length us, event | category | flops | bytes accessed | tf_op | source)
XLA Modules:
  0.0 95.2 jit_solution(5432148471928416848)
XLA Ops:
  0.6 3.0 %collective-permute-start.4 = (bf16[256,1024]{1,0:T(8,128)(2,1)}, bf16[256,1024]{1,0:T(8,128)(2,1)S(1)}, u32[]{:S(2)}, u32[]{:S(2)}) collective-permute-start(bf16[256,1024]{1,0:T(8,128)(2,1)} %b0.9), channel_id=1, source_target_pairs={{0,4},{1,5},{2,6},{3,7},{4,0},{5,1},{6,2},{7,3},{8,12},{9,13},{10,... | collective-permute-start | bytes 1572872 | tf_op jit(solution)/shard_map/mv_bx/ppermute | solution.py:58
  3.7 2.2 %copy-done.1 = bf16[256,8192]{1,0:T(8,128)(2,1)S(1)} copy-done((bf16[256,8192]{1,0:T(8,128)(2,1)S(1)}, bf16[256,8192]{1,0:T(8,128)(2,1)}, u32[]{:S(2)}) %copy-start.1) | copy-done | bytes 4194328
  5.9 3.3 %shard_map.76 = (bf16[2048,256]{1,0:T(8,128)(2,1)S(1)}, bf16[2048,256]{1,0:T(8,128)(2,1)S(1)}, bf16[512,256]{1,0:T(8,128)(2,1)S(1)}, bf16[1024,256]{1,0:T(8,128)...) custom-call(s32[4]{0:T(128)S(1)} %pad_add_fusion.where, ...), custom_call_target="tpu_custom_call" | custom-call | bytes 8388608 | tf_op jit(solution)/shard_map/pallas_call | solution.py:111
  11.8 4.8 %collective-permute-done.4.b2 = bf16[256,1024]{1,0:T(8,128)(2,1)S(1)} collective-permute-done((bf16[256,1024]{1,0:T(8,128)(2,1)}, bf16[256,1024]{1,0:T(8,128)(2,1)S(1)}, u32[]{:S(2)}, u32[]{:S(2)}) %collective-permute-start.4) | collective-permute-done | bytes 524320 | tf_op jit(solution)/shard_map/mv_bx/ppermute | solution.py:58
  17.2 5.0 %collective-permute-done.17.x_a = bf16[512,256]{1,0:T(8,128)(2,1)S(1)} collective-permute-done((bf16[512,256]{1,0:T(8,128)(2,1)S(1)}, bf16[512,256]{1,0:T(8,128)(2,1)S(1)}, u32[]{:S(2)}, u32[]{:S(2)}) %collective-permute-start.17) | collective-permute-done | bytes 262176 | tf_op jit(solution)/shard_map/mv_px0/ppermute | solution.py:58
  22.3 1.3 %collective-permute-done.18.xc_a = bf16[256,256]{1,0:T(8,128)(2,1)S(1)} collective-permute-done((bf16[256,256]{1,0:T(8,128)(2,1)S(1)}, bf16[256,256]{1,0:T(8,128)(2,1)S(1)}, u32[]{:S(2)}, u32[]{:S(2)}) %collective-permute-start.18) | collective-permute-done | bytes 131104 | tf_op jit(solution)/shard_map/mv_pr0/ppermute | solution.py:58
  24.4 2.2 %collective-permute-start.19 = (bf16[256,1024]{1,0:T(8,128)(2,1)S(1)}, bf16[256,1024]{1,0:T(8,128)(2,1)S(1)}, u32[]{:S(2)}, u32[]{:S(2)}) collective-permute-start(bf16[256,1024]{1,0:T(8,128)(2,1)S(1)} %shard_map.83), channel_id=1, source_target_pairs={{0,1},{1,0},{2,3},{3,2},{4,5},{5,4},{6,7},{7,6},{8,9},{9,8},{10,11... | collective-permute-start | bytes 1572872 | tf_op jit(solution)/shard_map/mv_yy0/ppermute | solution.py:58
  26.6 1.5 %collective-permute-start.10 = (bf16[1024,256]{1,0:T(8,128)(2,1)S(1)}, bf16[1024,256]{1,0:T(8,128)(2,1)S(1)}, u32[]{:S(2)}, u32[]{:S(2)}) collective-permute-start(bf16[1024,256]{1,0:T(8,128)(2,1)S(1)} %get-tuple-element.25), channel_id=1, source_target_pairs={{0,4},{1,5},{2,6},{3,7},{4,0},{5,1},{6,2},{7,3},{8,12},{9,13},{10,... | collective-permute-start | bytes 1572872 | tf_op jit(solution)/shard_map/mv_px2/ppermute | solution.py:58
  28.1 5.4 %collective-permute-done.14.x_a = bf16[1024,256]{1,0:T(8,128)(2,1)S(1)} collective-permute-done((bf16[1024,256]{1,0:T(8,128)(2,1)S(1)}, bf16[1024,256]{1,0:T(8,128)(2,1)S(1)}, u32[]{:S(2)}, u32[]{:S(2)}) %collective-permute-start.14) | collective-permute-done | bytes 524320 | tf_op jit(solution)/shard_map/mv_px1/ppermute | solution.py:58
  36.4 2.2 %collective-permute-start.16 = (bf16[256,1024]{1,0:T(8,128)(2,1)S(1)}, bf16[256,1024]{1,0:T(8,128)(2,1)S(1)}, u32[]{:S(2)}, u32[]{:S(2)}) collective-permute-start(bf16[256,1024]{1,0:T(8,128)(2,1)S(1)} %get-tuple-element.30), channel_id=1, source_target_pairs={{0,1},{1,0},{2,3},{3,2},{4,5},{5,4},{6,7},{7,6},{8,9},{9,8},{10,11... | collective-permute-start | bytes 1572872 | tf_op jit(solution)/shard_map/mv_yy1/ppermute | solution.py:58
  38.9 3.7 %collective-permute-start.20 = (bf16[256,1024]{1,0:T(8,128)(2,1)S(1)}, bf16[256,1024]{1,0:T(8,128)(2,1)S(1)}, u32[]{:S(2)}, u32[]{:S(2)}) collective-permute-start(bf16[256,1024]{1,0:T(8,128)(2,1)S(1)} %shard_map.84), channel_id=1, source_target_pairs={{0,8},{1,9},{2,10},{3,11},{4,12},{5,13},{6,14},{7,15},{24,16},{25,... | collective-permute-start | bytes 1572872 | tf_op jit(solution)/shard_map/mv_za0/ppermute | solution.py:64
  42.7 1.6 %collective-permute-start.7 = (bf16[1024,256]{1,0:T(8,128)(2,1)S(1)}, bf16[1024,256]{1,0:T(8,128)(2,1)S(1)}, u32[]{:S(2)}, u32[]{:S(2)}) collective-permute-start(bf16[1024,256]{1,0:T(8,128)(2,1)S(1)} %get-tuple-element.22), channel_id=1, source_target_pairs={{0,4},{1,5},{2,6},{3,7},{4,0},{5,1},{6,2},{7,3},{8,12},{9,13},{10,... | collective-permute-start | bytes 1572872 | tf_op jit(solution)/shard_map/mv_px3/ppermute | solution.py:58
  44.4 1.5 %collective-permute-done.11.xc_a = bf16[512,256]{1,0:T(8,128)(2,1)S(1)} collective-permute-done((bf16[512,256]{1,0:T(8,128)(2,1)S(1)}, bf16[512,256]{1,0:T(8,128)(2,1)S(1)}, u32[]{:S(2)}, u32[]{:S(2)}) %collective-permute-start.11) | collective-permute-done | bytes 262176 | tf_op jit(solution)/shard_map/mv_pr2/ppermute | solution.py:58
  47.2 1.6 %collective-permute-start.12 = (bf16[256,1024]{1,0:T(8,128)(2,1)S(1)}, bf16[256,1024]{1,0:T(8,128)(2,1)S(1)}, u32[]{:S(2)}, u32[]{:S(2)}) collective-permute-start(bf16[256,1024]{1,0:T(8,128)(2,1)S(1)} %get-tuple-element.26), channel_id=1, source_target_pairs={{0,1},{1,0},{2,3},{3,2},{4,5},{5,4},{6,7},{7,6},{8,9},{9,8},{10,11... | collective-permute-start | bytes 1572872 | tf_op jit(solution)/shard_map/mv_yy2/ppermute | solution.py:58
  48.8 2.5 %collective-permute-done.16.refs_1_ = bf16[256,1024]{1,0:T(8,128)(2,1)S(1)} collective-permute-done((bf16[256,1024]{1,0:T(8,128)(2,1)S(1)}, bf16[256,1024]{1,0:T(8,128)(2,1)S(1)}, u32[]{:S(2)}, u32[]{:S(2)}) %collective-permute-start.16) | collective-permute-done | bytes 524320 | tf_op jit(solution)/shard_map/mv_yy1/ppermute | solution.py:58
  51.4 3.2 %collective-permute-start.23 = (bf16[256,1024]{1,0:T(8,128)(2,1)S(1)}, bf16[256,1024]{1,0:T(8,128)(2,1)S(1)}, u32[]{:S(2)}, u32[]{:S(2)}) collective-permute-start(bf16[256,1024]{1,0:T(8,128)(2,1)S(1)} %shard_map.87), channel_id=1, source_target_pairs={{0,8},{1,9},{2,10},{3,11},{4,12},{5,13},{6,14},{7,15},{24,16},{25,... | collective-permute-start | bytes 1572872 | tf_op jit(solution)/shard_map/mv_za1/ppermute | solution.py:64
  55.8 1.6 %collective-permute-start.1 = (bf16[512,256]{1,0:T(8,128)(2,1)S(1)}, bf16[512,256]{1,0:T(8,128)(2,1)S(1)}, u32[]{:S(2)}, u32[]{:S(2)}) collective-permute-start(bf16[512,256]{1,0:T(8,128)(2,1)S(1)} %get-tuple-element.21), channel_id=1, source_target_pairs={{0,4},{1,5},{2,6},{3,7},{4,0},{5,1},{6,2},{7,3},{8,12},{9,13},{10,... | collective-permute-start | bytes 786440 | tf_op jit(solution)/shard_map/mv_px4/ppermute | solution.py:58
  58.7 1.5 %collective-permute-start.9 = (bf16[256,1024]{1,0:T(8,128)(2,1)S(1)}, bf16[256,1024]{1,0:T(8,128)(2,1)S(1)}, u32[]{:S(2)}, u32[]{:S(2)}) collective-permute-start(bf16[256,1024]{1,0:T(8,128)(2,1)S(1)} %get-tuple-element.23), channel_id=1, source_target_pairs={{0,1},{1,0},{2,3},{3,2},{4,5},{5,4},{6,7},{7,6},{8,9},{9,8},{10,11... | collective-permute-start | bytes 1572872 | tf_op jit(solution)/shard_map/mv_yy3/ppermute | solution.py:58
  60.2 2.3 %collective-permute-done.12.refs_1_ = bf16[256,1024]{1,0:T(8,128)(2,1)S(1)} collective-permute-done((bf16[256,1024]{1,0:T(8,128)(2,1)S(1)}, bf16[256,1024]{1,0:T(8,128)(2,1)S(1)}, u32[]{:S(2)}, u32[]{:S(2)}) %collective-permute-start.12) | collective-permute-done | bytes 524320 | tf_op jit(solution)/shard_map/mv_yy2/ppermute | solution.py:58
  62.6 2.6 %collective-permute-done.23.refs_2_ = bf16[256,1024]{1,0:T(8,128)(2,1)S(1)} collective-permute-done((bf16[256,1024]{1,0:T(8,128)(2,1)S(1)}, bf16[256,1024]{1,0:T(8,128)(2,1)S(1)}, u32[]{:S(2)}, u32[]{:S(2)}) %collective-permute-start.23) | collective-permute-done | bytes 524320 | tf_op jit(solution)/shard_map/mv_za1/ppermute | solution.py:64
  66.2 5.3 %collective-permute-start.22 = (bf16[256,1024]{1,0:T(8,128)(2,1)S(1)}, bf16[256,1024]{1,0:T(8,128)(2,1)S(1)}, u32[]{:S(2)}, u32[]{:S(2)}) collective-permute-start(bf16[256,1024]{1,0:T(8,128)(2,1)S(1)} %shard_map.86), channel_id=1, source_target_pairs={{0,8},{1,9},{2,10},{3,11},{4,12},{5,13},{6,14},{7,15},{8,0},{9,1},... | collective-permute-start | bytes 1572872 | tf_op jit(solution)/shard_map/mv_za2/ppermute | solution.py:64
  73.9 7.9 %collective-permute-done.22.refs_1_ = bf16[256,1024]{1,0:T(8,128)(2,1)S(1)} collective-permute-done((bf16[256,1024]{1,0:T(8,128)(2,1)S(1)}, bf16[256,1024]{1,0:T(8,128)(2,1)S(1)}, u32[]{:S(2)}, u32[]{:S(2)}) %collective-permute-start.22) | collective-permute-done | bytes 524320 | tf_op jit(solution)/shard_map/mv_za2/ppermute | solution.py:64
  82.0 11.0 %all_to_all.5.squares = f32[32,1,128]{2,1,0:T(1,128)S(1)} all-to-all(f32[32,1,128]{2,1,0:T(1,128)S(1)} %get-tuple-element.33), channel_id=1, replica_groups=mesh['replica'=16,'shard'=2] {'replica','shard'}, dimensions={0} | all-to-all | bytes 32768 | tf_op jit(solution)/shard_map/squares/all_to_all | solution.py:344
  93.0 2.2 %shard_map.90 = (f32[256,1024]{1,0:T(8,128)}, f32[256,1024]{1,0:T(8,128)}, f32[256,1024]{1,0:T(8,128)}) custom-call(f32[32,1,128]{2,1,0:T(1,128)S(1)} %all_to_all.5.squares, f32[256,1024]{1,0:T(8,128)S(1)} %get-tuple-element.34.grad, f32[256,1024]{1,0:T(8,128)S(1)} %copy-done.2, f32[256,1024]{1,0:T(8,128)S(1)} %copy-done.3, f32[256,1024]{1,0:T(8,128)S(1)} %copy-done.4), custom_call_target="tpu_custom_call" | custom-call | tf_op jit(solution)/shard_map/pallas_call | solution.py:240
  (61 shorter events, 14.9 us)
Async XLA Ops:
  0.6 16.0 %collective-permute-start.4 = (bf16[256,1024]{1,0:T(8,128)(2,1)}, bf16[256,1024]{1,0:T(8,128)(2,1)S(1)}, u32[]{:S(2)}, u32[]{:S(2)}) collective-permute-start(bf16[256,1024]{1,0:T(8,128)(2,1)} %b0.9), channel_id=1, source_target_pairs={{0,4},{1,5},{2,6},{3,7},{4,0},{5,1},{6,2},{7,3},{8,12},{9,13},{10,... | collective-permute-start | bytes 1572872 | tf_op jit(solution)/shard_map/mv_bx/ppermute | solution.py:58
  9.2 1.8 %collective-permute-start.13 = (bf16[768,256]{1,0:T(8,128)(2,1)S(1)}, bf16[768,256]{1,0:T(8,128)(2,1)S(1)}, u32[]{:S(2)}, u32[]{:S(2)}) collective-permute-start(bf16[768,256]{1,0:T(8,128)(2,1)S(1)} %slice.33), channel_id=1, source_target_pairs={{0,2},{1,3},{2,0},{3,1},{4,6},{5,7},{6,4},{7,5},{8,10},{9,11},{10,... | collective-permute-start | bytes 1179656 | tf_op jit(solution)/shard_map/mv_own0/ppermute | solution.py:58
  9.3 14.3 %collective-permute-start.3 = (bf16[256,1024]{1,0:T(8,128)(2,1)S(1)}, bf16[256,1024]{1,0:T(8,128)(2,1)S(1)}, u32[]{:S(2)}, u32[]{:S(2)}) collective-permute-start(bf16[256,1024]{1,0:T(8,128)(2,1)S(1)} %copy-done), channel_id=1, source_target_pairs={{0,2},{1,3},{2,0},{3,1},{4,6},{5,7},{6,4},{7,5},{8,10},{9,11},{10,... | collective-permute-start | bytes 1572872 | tf_op jit(solution)/shard_map/mv_bc/ppermute | solution.py:58
  9.8 12.4 %collective-permute-start.17 = (bf16[512,256]{1,0:T(8,128)(2,1)S(1)}, bf16[512,256]{1,0:T(8,128)(2,1)S(1)}, u32[]{:S(2)}, u32[]{:S(2)}) collective-permute-start(bf16[512,256]{1,0:T(8,128)(2,1)S(1)} %get-tuple-element.32), channel_id=1, source_target_pairs={{0,4},{1,5},{2,6},{3,7},{4,0},{5,1},{6,2},{7,3},{8,12},{9,13},{10,... | collective-permute-start | bytes 786440 | tf_op jit(solution)/shard_map/mv_px0/ppermute | solution.py:58
  11.0 22.4 %collective-permute-start.14 = (bf16[1024,256]{1,0:T(8,128)(2,1)S(1)}, bf16[1024,256]{1,0:T(8,128)(2,1)S(1)}, u32[]{:S(2)}, u32[]{:S(2)}) collective-permute-start(bf16[1024,256]{1,0:T(8,128)(2,1)S(1)} %get-tuple-element.29), channel_id=1, source_target_pairs={{0,4},{1,5},{2,6},{3,7},{4,0},{5,1},{6,2},{7,3},{8,12},{9,13},{10,... | collective-permute-start | bytes 1572872 | tf_op jit(solution)/shard_map/mv_px1/ppermute | solution.py:58
  16.6 7.0 %collective-permute-start.5 = (bf16[256,512]{1,0:T(8,128)(2,1)S(1)}, bf16[256,512]{1,0:T(8,128)(2,1)S(1)}, u32[]{:S(2)}, u32[]{:S(2)}) collective-permute-start(bf16[256,512]{1,0:T(8,128)(2,1)S(1)} %get-tuple-element.36), channel_id=1, source_target_pairs={{0,2},{1,3},{2,0},{3,1},{4,6},{5,7},{6,4},{7,5},{8,10},{9,11},{10,... | collective-permute-start | bytes 786440 | tf_op jit(solution)/shard_map/mv_br0/ppermute | solution.py:58
  16.7 6.9 %collective-permute-start.6 = (bf16[256,512]{1,0:T(8,128)(2,1)S(1)}, bf16[256,512]{1,0:T(8,128)(2,1)S(1)}, u32[]{:S(2)}, u32[]{:S(2)}) collective-permute-start(bf16[256,512]{1,0:T(8,128)(2,1)S(1)} %get-tuple-element.35), channel_id=1, source_target_pairs={{0,2},{1,3},{2,0},{3,1},{4,6},{5,7},{6,4},{7,5},{8,10},{9,11},{10,... | collective-permute-start | bytes 786440 | tf_op jit(solution)/shard_map/mv_br1/ppermute | solution.py:58
  22.2 1.4 %collective-permute-start.18 = (bf16[256,256]{1,0:T(8,128)(2,1)S(1)}, bf16[256,256]{1,0:T(8,128)(2,1)S(1)}, u32[]{:S(2)}, u32[]{:S(2)}) collective-permute-start(bf16[256,256]{1,0:T(8,128)(2,1)S(1)} %slice.42), channel_id=1, source_target_pairs={{0,2},{1,3},{2,0},{3,1},{4,6},{5,7},{6,4},{7,5},{8,10},{9,11},{10,... | collective-permute-start | bytes 393224 | tf_op jit(solution)/shard_map/mv_pr0/ppermute | solution.py:58
  24.4 14.4 %collective-permute-start.19 = (bf16[256,1024]{1,0:T(8,128)(2,1)S(1)}, bf16[256,1024]{1,0:T(8,128)(2,1)S(1)}, u32[]{:S(2)}, u32[]{:S(2)}) collective-permute-start(bf16[256,1024]{1,0:T(8,128)(2,1)S(1)} %shard_map.83), channel_id=1, source_target_pairs={{0,1},{1,0},{2,3},{3,2},{4,5},{5,4},{6,7},{7,6},{8,9},{9,8},{10,11... | collective-permute-start | bytes 1572872 | tf_op jit(solution)/shard_map/mv_yy0/ppermute | solution.py:58
  26.6 17.7 %collective-permute-start.10 = (bf16[1024,256]{1,0:T(8,128)(2,1)S(1)}, bf16[1024,256]{1,0:T(8,128)(2,1)S(1)}, u32[]{:S(2)}, u32[]{:S(2)}) collective-permute-start(bf16[1024,256]{1,0:T(8,128)(2,1)S(1)} %get-tuple-element.25), channel_id=1, source_target_pairs={{0,4},{1,5},{2,6},{3,7},{4,0},{5,1},{6,2},{7,3},{8,12},{9,13},{10,... | collective-permute-start | bytes 1572872 | tf_op jit(solution)/shard_map/mv_px2/ppermute | solution.py:58
  33.5 1.6 %collective-permute-start.15 = (bf16[512,256]{1,0:T(8,128)(2,1)S(1)}, bf16[512,256]{1,0:T(8,128)(2,1)S(1)}, u32[]{:S(2)}, u32[]{:S(2)}) collective-permute-start(bf16[512,256]{1,0:T(8,128)(2,1)S(1)} %slice.41), channel_id=1, source_target_pairs={{0,2},{1,3},{2,0},{3,1},{4,6},{5,7},{6,4},{7,5},{8,10},{9,11},{10,... | collective-permute-start | bytes 786440 | tf_op jit(solution)/shard_map/mv_pr1/ppermute | solution.py:58
  33.6 10.7 %collective-permute-start = (bf16[1280,256]{1,0:T(8,128)(2,1)S(1)}, bf16[1280,256]{1,0:T(8,128)(2,1)S(1)}, u32[]{:S(2)}, u32[]{:S(2)}) collective-permute-start(bf16[1280,256]{1,0:T(8,128)(2,1)S(1)} %slice.27), channel_id=1, source_target_pairs={{0,2},{1,3},{2,0},{3,1},{4,6},{5,7},{6,4},{7,5},{8,10},{9,11},{10,... | collective-permute-start | bytes 1966088 | tf_op jit(solution)/shard_map/mv_own1/ppermute | solution.py:58
  36.4 14.9 %collective-permute-start.16 = (bf16[256,1024]{1,0:T(8,128)(2,1)S(1)}, bf16[256,1024]{1,0:T(8,128)(2,1)S(1)}, u32[]{:S(2)}, u32[]{:S(2)}) collective-permute-start(bf16[256,1024]{1,0:T(8,128)(2,1)S(1)} %get-tuple-element.30), channel_id=1, source_target_pairs={{0,1},{1,0},{2,3},{3,2},{4,5},{5,4},{6,7},{7,6},{8,9},{9,8},{10,11... | collective-permute-start | bytes 1572872 | tf_op jit(solution)/shard_map/mv_yy1/ppermute | solution.py:58
  38.9 15.7 %collective-permute-start.20 = (bf16[256,1024]{1,0:T(8,128)(2,1)S(1)}, bf16[256,1024]{1,0:T(8,128)(2,1)S(1)}, u32[]{:S(2)}, u32[]{:S(2)}) collective-permute-start(bf16[256,1024]{1,0:T(8,128)(2,1)S(1)} %shard_map.84), channel_id=1, source_target_pairs={{0,8},{1,9},{2,10},{3,11},{4,12},{5,13},{6,14},{7,15},{24,16},{25,... | collective-permute-start | bytes 1572872 | tf_op jit(solution)/shard_map/mv_za0/ppermute | solution.py:64
  42.7 13.0 %collective-permute-start.7 = (bf16[1024,256]{1,0:T(8,128)(2,1)S(1)}, bf16[1024,256]{1,0:T(8,128)(2,1)S(1)}, u32[]{:S(2)}, u32[]{:S(2)}) collective-permute-start(bf16[1024,256]{1,0:T(8,128)(2,1)S(1)} %get-tuple-element.22), channel_id=1, source_target_pairs={{0,4},{1,5},{2,6},{3,7},{4,0},{5,1},{6,2},{7,3},{8,12},{9,13},{10,... | collective-permute-start | bytes 1572872 | tf_op jit(solution)/shard_map/mv_px3/ppermute | solution.py:58
  44.3 1.6 %collective-permute-start.11 = (bf16[512,256]{1,0:T(8,128)(2,1)S(1)}, bf16[512,256]{1,0:T(8,128)(2,1)S(1)}, u32[]{:S(2)}, u32[]{:S(2)}) collective-permute-start(bf16[512,256]{1,0:T(8,128)(2,1)S(1)} %slice.40), channel_id=1, source_target_pairs={{0,2},{1,3},{2,0},{3,1},{4,6},{5,7},{6,4},{7,5},{8,10},{9,11},{10,... | collective-permute-start | bytes 786440 | tf_op jit(solution)/shard_map/mv_pr2/ppermute | solution.py:58
  47.2 15.3 %collective-permute-start.12 = (bf16[256,1024]{1,0:T(8,128)(2,1)S(1)}, bf16[256,1024]{1,0:T(8,128)(2,1)S(1)}, u32[]{:S(2)}, u32[]{:S(2)}) collective-permute-start(bf16[256,1024]{1,0:T(8,128)(2,1)S(1)} %get-tuple-element.26), channel_id=1, source_target_pairs={{0,1},{1,0},{2,3},{3,2},{4,5},{5,4},{6,7},{7,6},{8,9},{9,8},{10,11... | collective-permute-start | bytes 1572872 | tf_op jit(solution)/shard_map/mv_yy2/ppermute | solution.py:58
  51.4 13.9 %collective-permute-start.23 = (bf16[256,1024]{1,0:T(8,128)(2,1)S(1)}, bf16[256,1024]{1,0:T(8,128)(2,1)S(1)}, u32[]{:S(2)}, u32[]{:S(2)}) collective-permute-start(bf16[256,1024]{1,0:T(8,128)(2,1)S(1)} %shard_map.87), channel_id=1, source_target_pairs={{0,8},{1,9},{2,10},{3,11},{4,12},{5,13},{6,14},{7,15},{24,16},{25,... | collective-permute-start | bytes 1572872 | tf_op jit(solution)/shard_map/mv_za1/ppermute | solution.py:64
  54.8 11.3 %collective-permute-start.21 = (bf16[256,1024]{1,0:T(8,128)(2,1)S(1)}, bf16[256,1024]{1,0:T(8,128)(2,1)S(1)}, u32[]{:S(2)}, u32[]{:S(2)}) collective-permute-start(bf16[256,1024]{1,0:T(8,128)(2,1)S(1)} %shard_map.85), channel_id=1, source_target_pairs={{8,16},{9,17},{10,18},{11,19},{12,20},{13,21},{14,22},{15,23},{16,... | collective-permute-start | bytes 1572872 | tf_op jit(solution)/shard_map/mv_zb1/ppermute | solution.py:64
  55.7 1.6 %collective-permute-start.8 = (bf16[512,256]{1,0:T(8,128)(2,1)S(1)}, bf16[512,256]{1,0:T(8,128)(2,1)S(1)}, u32[]{:S(2)}, u32[]{:S(2)}) collective-permute-start(bf16[512,256]{1,0:T(8,128)(2,1)S(1)} %slice.39), channel_id=1, source_target_pairs={{0,2},{1,3},{2,0},{3,1},{4,6},{5,7},{6,4},{7,5},{8,10},{9,11},{10,... | collective-permute-start | bytes 786440 | tf_op jit(solution)/shard_map/mv_pr3/ppermute | solution.py:58
  55.8 15.7 %collective-permute-start.1 = (bf16[512,256]{1,0:T(8,128)(2,1)S(1)}, bf16[512,256]{1,0:T(8,128)(2,1)S(1)}, u32[]{:S(2)}, u32[]{:S(2)}) collective-permute-start(bf16[512,256]{1,0:T(8,128)(2,1)S(1)} %get-tuple-element.21), channel_id=1, source_target_pairs={{0,4},{1,5},{2,6},{3,7},{4,0},{5,1},{6,2},{7,3},{8,12},{9,13},{10,... | collective-permute-start | bytes 786440 | tf_op jit(solution)/shard_map/mv_px4/ppermute | solution.py:58
  58.7 15.1 %collective-permute-start.9 = (bf16[256,1024]{1,0:T(8,128)(2,1)S(1)}, bf16[256,1024]{1,0:T(8,128)(2,1)S(1)}, u32[]{:S(2)}, u32[]{:S(2)}) collective-permute-start(bf16[256,1024]{1,0:T(8,128)(2,1)S(1)} %get-tuple-element.23), channel_id=1, source_target_pairs={{0,1},{1,0},{2,3},{3,2},{4,5},{5,4},{6,7},{7,6},{8,9},{9,8},{10,11... | collective-permute-start | bytes 1572872 | tf_op jit(solution)/shard_map/mv_yy3/ppermute | solution.py:58
  65.4 8.5 %collective-permute-start.24 = (bf16[256,1024]{1,0:T(8,128)(2,1)S(1)}, bf16[256,1024]{1,0:T(8,128)(2,1)S(1)}, u32[]{:S(2)}, u32[]{:S(2)}) collective-permute-start(bf16[256,1024]{1,0:T(8,128)(2,1)S(1)} %shard_map.88), channel_id=1, source_target_pairs={{8,16},{9,17},{10,18},{11,19},{12,20},{13,21},{14,22},{15,23},{16,... | collective-permute-start | bytes 1572872 | tf_op jit(solution)/shard_map/mv_zb2/ppermute | solution.py:64
  66.2 15.5 %collective-permute-start.22 = (bf16[256,1024]{1,0:T(8,128)(2,1)S(1)}, bf16[256,1024]{1,0:T(8,128)(2,1)S(1)}, u32[]{:S(2)}, u32[]{:S(2)}) collective-permute-start(bf16[256,1024]{1,0:T(8,128)(2,1)S(1)} %shard_map.86), channel_id=1, source_target_pairs={{0,8},{1,9},{2,10},{3,11},{4,12},{5,13},{6,14},{7,15},{8,0},{9,1},... | collective-permute-start | bytes 1572872 | tf_op jit(solution)/shard_map/mv_za2/ppermute | solution.py:64
  (6 other events, 70.0 us)
